TPU v7x, 32 devices: a whole 2x2x4 slice. The times are simulated.
32 devices in a mesh: fsdp: 8 (over y, x, core), seq: 4 (over z).
Axes of the slice: x: 2, y: 2, z: 4, core: 2. Of those that a mesh axis runs over, the one named last changes fastest.
Arguments:
- block_input: bfloat16 [8, 2048, 2560], P('fsdp', 'seq'), may hold values from -6 to 6
- cont_lengths: int32 [8, 4], P('fsdp'), may hold values from 1 to 384, 1024 in all within a row
- attn_gain: bfloat16 [2560], P('fsdp'), may hold values from 0.099609375 to 1.8984375
- q_down: bfloat16 [2560, 768], P('fsdp'), may hold values from -0.125 to 0.125
- q_gain: bfloat16 [768], P('fsdp'), may hold values from 0.099609375 to 1.8984375
- q_up: bfloat16 [768, 3840], P('fsdp'), may hold values from -0.21875 to 0.21875
- kv_down: bfloat16 [2560, 288], P('fsdp'), may hold values from -0.125 to 0.125
- kv_gain: bfloat16 [256], P('fsdp'), may hold values from 0.099609375 to 1.8984375
- kv_up: bfloat16 [256, 5120], P('fsdp'), may hold values from -0.375 to 0.375
- out_proj: bfloat16 [2560, 2560], P('fsdp'), may hold values from -12 to 12
- mlp_gain: bfloat16 [2560], P('fsdp'), may hold values from 0.099609375 to 1.8984375
- gate_up: bfloat16 [2560, 12800], P('fsdp'), may hold values from -0.125 to 0.125
- down_proj: bfloat16 [6400, 2560], P('fsdp'), may hold values from -0.625 to 0.625
- out_cotangent: bfloat16 [8, 2048, 2560], P('fsdp', 'seq'), may hold values from -6 to 6
Outputs:
- output: bfloat16 [8, 2048, 2560], P('fsdp', 'seq')
- grad_input: float32 [8, 2048, 2560], P('fsdp', 'seq')
- attn_gain_grad: float32 [2560], P('fsdp')
- q_down_grad: float32 [2560, 768], P('fsdp')
- q_gain_grad: float32 [768], P('fsdp')
- q_up_grad: float32 [768, 3840], P('fsdp')
- kv_down_grad: float32 [2560, 288], P('fsdp')
- kv_gain_grad: float32 [256], P('fsdp')
- kv_up_grad: float32 [256, 5120], P('fsdp')
- out_proj_grad: float32 [2560, 2560], P('fsdp')
- mlp_gain_grad: float32 [2560], P('fsdp')
- gate_up_grad: float32 [2560, 12800], P('fsdp')
- down_proj_grad: float32 [6400, 2560], P('fsdp')
Inputs may be any that keep to these rules, and one draw needn't show every extreme that they name: `cont_lengths`: each group's 4 continuation lengths sum to 1024, each up to 384; in every group the longest has exactly 384 tokens.
All inputs are finite; a program needn't handle non-finite values.
Results may differ from a plain program's by a relative error of at most 0.02.
Values may be sent and summed in bfloat16 or wider, within the bound.
No kernel may reach another device: no remote copies, remote signals or barrier semaphores. Data moves between devices by JAX's collectives and lax.ppermute only.
A program may use at most 512 MiB of HBM per device.

v0:
```python
import math

import jax
import jax.numpy as jnp
from jax import lax
from jax.sharding import PartitionSpec as P

D = 2560
HEADS = 40
NOPE = 64
ROPE = 32
VDIM = 64
KVRANK = 256
FF = 6400
PROMPT = 1024
GROUP = 2048


variance_eps = 1e-05
depth_scale = 1.4 / math.sqrt(62.0)
masked_score = -1e30


def rms_forward(values, gain_vector):
    inverse = lax.rsqrt(jnp.mean(values * values, axis=-1, keepdims=True) + variance_eps)
    return (values * inverse * gain_vector, inverse)


def rms_backward(values, inverse, gain_vector, upstream):
    scaled = upstream * gain_vector
    inner_mean = jnp.mean(scaled * values, axis=-1, keepdims=True)
    grad_values = inverse * scaled - values * inverse * inverse * inverse * inner_mean
    grad_gain = jnp.sum(upstream * values * inverse, axis=0)
    return (grad_values, grad_gain)


def rotate(values, cosine_table, sine_table):
    half_width = values.shape[-1] // 2
    first_half = values[..., :half_width]
    second = values[..., half_width:]
    return jnp.concatenate(
        [
            first_half * cosine_table - second * sine_table,
            second * cosine_table + first_half * sine_table,
        ],
        axis=-1,
    )


def layout(lengths, group_len, prompt_len):
    token_index = jnp.arange(group_len, dtype=jnp.int32)
    cont_ends = prompt_len + jnp.cumsum(lengths)
    starts = cont_ends - lengths
    started = (token_index[:, None] >= starts[None, :]).astype(jnp.int32)
    segment = jnp.sum(started, axis=1)
    own_start = jnp.max(started * starts[None, :], axis=1)
    position = jnp.where(segment > 0, prompt_len + token_index - own_start, token_index)
    return (segment, position)


def rope_tables(position, rope_width):
    steps_half = jnp.arange(rope_width // 2, dtype=jnp.float32)
    frequency = jnp.exp(steps_half * (-2.0 * math.log(10000.0) / rope_width))
    angles = position.astype(jnp.float32)[:, None] * frequency[None, :]
    return (jnp.cos(angles), jnp.sin(angles))


def masked_scores(q_block, key_rows, seg_block, idx_block, segment, token_index, score_scale):
    raw_scores = (
        jnp.einsum("qhd,khd->hqk", q_block, key_rows, preferred_element_type=jnp.float32)
        * score_scale
    )
    allowed = (token_index[None, :] <= idx_block[:, None]) & (
        (segment[None, :] == seg_block[:, None]) | (segment[None, :] == 0)
    )
    return jnp.where(allowed[None], raw_scores, masked_score)


def attend_group(queries, key_rows, value_rows, segment, score_scale):
    group_len = key_rows.shape[0]
    heads_here = key_rows.shape[1]
    block_rows = min(512, group_len)
    block_count = group_len // block_rows
    token_index = jnp.arange(group_len, dtype=jnp.int32)

    def one_block(inputs):
        q_block, seg_block, idx_block = inputs
        block_scores = masked_scores(
            q_block, key_rows, seg_block, idx_block, segment, token_index, score_scale
        )
        row_max = jnp.max(block_scores, axis=-1, keepdims=True)
        unscaled = jnp.exp(block_scores - row_max)
        row_total = jnp.sum(unscaled, axis=-1, keepdims=True)
        probs_low = (unscaled / row_total).astype(jnp.bfloat16)
        block_out = jnp.einsum(
            "hqk,khd->qhd", probs_low, value_rows, preferred_element_type=jnp.float32
        ).astype(jnp.bfloat16)
        return (block_out, (row_max + jnp.log(row_total))[..., 0])

    attended, log_total = lax.map(
        one_block,
        (
            queries.reshape(block_count, block_rows, heads_here, queries.shape[-1]),
            segment.reshape(block_count, block_rows),
            token_index.reshape(block_count, block_rows),
        ),
    )
    return (attended.reshape(group_len, heads_here, value_rows.shape[-1]), log_total)


def attend_back(queries, key_rows, value_rows, grad_attended, log_total, segment, score_scale):
    group_len = key_rows.shape[0]
    heads_here = key_rows.shape[1]
    block_rows = min(512, group_len)
    block_count = group_len // block_rows
    token_index = jnp.arange(group_len, dtype=jnp.int32)

    def one_block(carried, inputs):
        key_sum, value_sum = carried
        q_block, grad_block, total_block, seg_block, idx_block = inputs
        block_scores = masked_scores(
            q_block, key_rows, seg_block, idx_block, segment, token_index, score_scale
        )
        attn_probs = jnp.exp(block_scores - total_block[..., None])
        probs_low = attn_probs.astype(jnp.bfloat16)
        grad_probs = jnp.einsum(
            "qhd,khd->hqk", grad_block, value_rows, preferred_element_type=jnp.float32
        )
        inner_sum = jnp.sum(attn_probs * grad_probs, axis=-1, keepdims=True)
        grad_scores = (attn_probs * (grad_probs - inner_sum)).astype(jnp.bfloat16)
        grad_query = (
            jnp.einsum("hqk,khd->qhd", grad_scores, key_rows, preferred_element_type=jnp.float32)
            * score_scale
        ).astype(jnp.bfloat16)
        key_sum = (
            key_sum
            + jnp.einsum("hqk,qhd->khd", grad_scores, q_block, preferred_element_type=jnp.float32)
            * score_scale
        )
        value_sum = value_sum + jnp.einsum(
            "hqk,qhd->khd", probs_low, grad_block, preferred_element_type=jnp.float32
        )
        return ((key_sum, value_sum), grad_query)

    start_sums = (jnp.zeros(key_rows.shape, jnp.float32), jnp.zeros(value_rows.shape, jnp.float32))
    sums_end, grad_queries = lax.scan(
        one_block,
        start_sums,
        (
            queries.reshape(block_count, block_rows, heads_here, queries.shape[-1]),
            grad_attended.reshape(block_count, block_rows, heads_here, grad_attended.shape[-1]),
            log_total,
            segment.reshape(block_count, block_rows),
            token_index.reshape(block_count, block_rows),
        ),
    )
    return (
        grad_queries.reshape(queries.shape),
        sums_end[0].astype(jnp.bfloat16),
        sums_end[1].astype(jnp.bfloat16),
    )


def contract_rows(left, right):
    return lax.dot_general(
        left, right, (((0,), (0,)), ((), ())), preferred_element_type=jnp.float32
    )


def contract_cols(left, right):
    return lax.dot_general(
        left, right, (((1,), (1,)), ((), ())), preferred_element_type=jnp.float32
    )


def body(
    block_input,
    cont_lengths,
    attn_gain,
    q_down,
    q_gain,
    q_up,
    kv_down,
    kv_gain,
    kv_up,
    out_proj,
    mlp_gain,
    gate_up,
    down_proj,
    out_cotangent,
):
    groups_here = block_input.shape[0]
    local_len = block_input.shape[1]
    token_offset = lax.axis_index("seq") * local_len
    qk_width = NOPE + ROPE
    score_scale = qk_width ** (-0.5)
    segment, position = jax.vmap(lambda lengths: layout(lengths, GROUP, PROMPT))(cont_lengths)
    own_position = lax.dynamic_slice_in_dim(position, token_offset, local_len, 1)
    cosine_table, sine_table = rope_tables(own_position.reshape(-1), ROPE)
    row_count = groups_here * local_len
    attn_full = (
        lax.all_gather(attn_gain, "fsdp", axis=0, tiled=True),
        lax.all_gather(q_down, "fsdp", axis=0, tiled=True),
        lax.all_gather(q_gain, "fsdp", axis=0, tiled=True),
        lax.all_gather(q_up, "fsdp", axis=0, tiled=True),
        lax.all_gather(kv_down, "fsdp", axis=0, tiled=True),
        lax.all_gather(kv_gain, "fsdp", axis=0, tiled=True),
        lax.all_gather(kv_up, "fsdp", axis=0, tiled=True),
        lax.all_gather(out_proj, "fsdp", axis=0, tiled=True),
    )
    token_rows = block_input.reshape(row_count, D).astype(jnp.float32)
    normed_float, attn_inverse = rms_forward(token_rows, attn_full[0].astype(jnp.float32))
    normed = normed_float.astype(jnp.bfloat16)
    q_latent = jnp.dot(normed, attn_full[1], preferred_element_type=jnp.float32)
    q_lat_float, q_inverse = rms_forward(q_latent, attn_full[2].astype(jnp.float32))
    q_lat_normed = q_lat_float.astype(jnp.bfloat16)
    q_full = jnp.dot(q_lat_normed, attn_full[3], preferred_element_type=jnp.float32).reshape(
        row_count, HEADS, qk_width
    )
    queries = jnp.concatenate(
        [
            q_full[..., :NOPE],
            rotate(q_full[..., NOPE:], cosine_table[:, None], sine_table[:, None]),
        ],
        axis=-1,
    ).astype(jnp.bfloat16)
    kv_latent = jnp.dot(normed, attn_full[4], preferred_element_type=jnp.float32)
    kv_float, kv_inverse = rms_forward(kv_latent[:, :KVRANK], attn_full[5].astype(jnp.float32))
    kv_normed = kv_float.astype(jnp.bfloat16)
    key_rope = rotate(kv_latent[:, KVRANK:], cosine_table, sine_table).astype(jnp.bfloat16)

    def shaped(tensor):
        return tensor.reshape(groups_here, local_len, HEADS, tensor.shape[-1])

    kv_full = jnp.dot(kv_normed, attn_full[6], preferred_element_type=jnp.float32).reshape(
        row_count, HEADS, NOPE + VDIM
    )
    key_rows = jnp.concatenate(
        [
            kv_full[..., :NOPE].astype(jnp.bfloat16),
            jnp.broadcast_to(key_rope[:, None, :], (row_count, HEADS, ROPE)),
        ],
        axis=-1,
    )
    value_rows = kv_full[..., NOPE:].astype(jnp.bfloat16)
    head_queries, head_keys, head_values = (
        lax.all_to_all(shaped(queries), "seq", split_axis=2, concat_axis=1, tiled=True),
        lax.all_to_all(shaped(key_rows), "seq", split_axis=2, concat_axis=1, tiled=True),
        lax.all_to_all(shaped(value_rows), "seq", split_axis=2, concat_axis=1, tiled=True),
    )

    def group_attend(group_items):
        return attend_group(
            group_items[0], group_items[1], group_items[2], group_items[3], score_scale
        )

    attended_heads, log_total = lax.map(
        group_attend, (head_queries, head_keys, head_values, segment)
    )
    attended_tokens = lax.all_to_all(attended_heads, "seq", split_axis=1, concat_axis=2, tiled=True)
    attended_rows = attended_tokens.reshape(row_count, HEADS * VDIM)
    attn_branch = jnp.dot(attended_rows, attn_full[7], preferred_element_type=jnp.float32)
    middle = token_rows + depth_scale * attn_branch
    mlp_full = (
        lax.all_gather(mlp_gain, "fsdp", axis=0, tiled=True),
        lax.all_gather(gate_up, "fsdp", axis=0, tiled=True),
        lax.all_gather(down_proj, "fsdp", axis=0, tiled=True),
    )
    mlp_float, mlp_inverse = rms_forward(middle, mlp_full[0].astype(jnp.float32))
    mlp_normed = mlp_float.astype(jnp.bfloat16)
    gate_up_out = jnp.dot(mlp_normed, mlp_full[1], preferred_element_type=jnp.float32)
    gate_part = gate_up_out[:, :FF]
    up_part = gate_up_out[:, FF:]
    gate_sigmoid = jax.nn.sigmoid(gate_part)
    silu_gate = gate_part * gate_sigmoid
    activated = (silu_gate * up_part).astype(jnp.bfloat16)
    mlp_branch = jnp.dot(activated, mlp_full[2], preferred_element_type=jnp.float32)
    output = (middle + depth_scale * mlp_branch).astype(jnp.bfloat16).reshape(block_input.shape)
    mlp_back = (
        lax.all_gather(mlp_gain, "fsdp", axis=0, tiled=True),
        lax.all_gather(gate_up, "fsdp", axis=0, tiled=True),
        lax.all_gather(down_proj, "fsdp", axis=0, tiled=True),
    )
    attn_back = (
        lax.all_gather(attn_gain, "fsdp", axis=0, tiled=True),
        lax.all_gather(q_down, "fsdp", axis=0, tiled=True),
        lax.all_gather(q_gain, "fsdp", axis=0, tiled=True),
        lax.all_gather(q_up, "fsdp", axis=0, tiled=True),
        lax.all_gather(kv_down, "fsdp", axis=0, tiled=True),
        lax.all_gather(kv_gain, "fsdp", axis=0, tiled=True),
        lax.all_gather(kv_up, "fsdp", axis=0, tiled=True),
        lax.all_gather(out_proj, "fsdp", axis=0, tiled=True),
    )
    cotangent = out_cotangent.reshape(row_count, D).astype(jnp.float32)
    grad_mlp = (depth_scale * cotangent).astype(jnp.bfloat16)
    grad_act = contract_cols(grad_mlp, mlp_back[2])
    grad_gate = grad_act * up_part * gate_sigmoid * (1.0 + gate_part * (1.0 - gate_sigmoid))
    grad_up = grad_act * silu_gate
    grad_gate_up = jnp.concatenate([grad_gate, grad_up], axis=1).astype(jnp.bfloat16)
    grad_mlp_normed = contract_cols(grad_gate_up, mlp_back[1])
    grad_mid_norm, mlp_gain_part = rms_backward(
        middle, mlp_inverse, mlp_back[0].astype(jnp.float32), grad_mlp_normed
    )
    grad_middle = cotangent + grad_mid_norm
    grad_attn = (depth_scale * grad_middle).astype(jnp.bfloat16)
    out_proj_part = contract_rows(attended_rows, grad_attn)
    grad_attended = contract_cols(grad_attn, attn_back[7]).astype(jnp.bfloat16)
    grad_heads = lax.all_to_all(
        grad_attended.reshape(groups_here, local_len, HEADS, VDIM),
        "seq",
        split_axis=2,
        concat_axis=1,
        tiled=True,
    )

    def group_back(group_items):
        return attend_back(
            group_items[0],
            group_items[1],
            group_items[2],
            group_items[3],
            group_items[4],
            group_items[5],
            score_scale,
        )

    grad_q_heads, grad_k_heads, grad_v_heads = lax.map(
        group_back, (head_queries, head_keys, head_values, grad_heads, log_total, segment)
    )
    grad_queries, grad_keys, grad_values = (
        lax.all_to_all(grad_q_heads, "seq", split_axis=1, concat_axis=2, tiled=True),
        lax.all_to_all(grad_k_heads, "seq", split_axis=1, concat_axis=2, tiled=True),
        lax.all_to_all(grad_v_heads, "seq", split_axis=1, concat_axis=2, tiled=True),
    )
    grad_queries = grad_queries.reshape(row_count, HEADS, qk_width).astype(jnp.float32)
    grad_keys = grad_keys.reshape(row_count, HEADS, qk_width)
    grad_values = grad_values.reshape(row_count, HEADS, VDIM)
    grad_q_full = jnp.concatenate(
        [
            grad_queries[..., :NOPE],
            rotate(grad_queries[..., NOPE:], cosine_table[:, None], -sine_table[:, None]),
        ],
        axis=-1,
    )
    grad_q_full = grad_q_full.astype(jnp.bfloat16).reshape(row_count, HEADS * qk_width)
    q_up_part = contract_rows(q_lat_normed, grad_q_full)
    grad_q_lat_normed = contract_cols(grad_q_full, attn_back[3])
    grad_q_float, q_gain_part = rms_backward(
        q_latent, q_inverse, attn_back[2].astype(jnp.float32), grad_q_lat_normed
    )
    grad_q_latent = grad_q_float.astype(jnp.bfloat16)
    grad_kv_full = jnp.concatenate([grad_keys[..., :NOPE], grad_values], axis=-1).reshape(
        row_count, HEADS * (NOPE + VDIM)
    )
    kv_up_part = contract_rows(kv_normed, grad_kv_full)
    grad_kv_normed = contract_cols(grad_kv_full, attn_back[6])
    grad_kv_first, kv_gain_part = rms_backward(
        kv_latent[:, :KVRANK], kv_inverse, attn_back[5].astype(jnp.float32), grad_kv_normed
    )
    grad_rope = jnp.sum(grad_keys[..., NOPE:].astype(jnp.float32), axis=1)
    grad_rope_back = rotate(grad_rope, cosine_table, -sine_table)
    grad_kv_latent = jnp.concatenate([grad_kv_first, grad_rope_back], axis=1).astype(jnp.bfloat16)
    q_down_part = contract_rows(normed, grad_q_latent)
    kv_down_part = contract_rows(normed, grad_kv_latent)
    grad_normed = contract_cols(grad_q_latent, attn_back[1]) + contract_cols(
        grad_kv_latent, attn_back[4]
    )
    grad_in_norm, attn_gain_part = rms_backward(
        token_rows, attn_inverse, attn_back[0].astype(jnp.float32), grad_normed
    )
    grad_input = (grad_middle + grad_in_norm).reshape(block_input.shape)
    down_grad = lax.psum_scatter(
        contract_rows(activated, grad_mlp).astype(jnp.bfloat16),
        "fsdp",
        scatter_dimension=0,
        tiled=True,
    )
    gate_up_grad = lax.psum_scatter(
        contract_rows(mlp_normed, grad_gate_up).astype(jnp.bfloat16),
        "fsdp",
        scatter_dimension=0,
        tiled=True,
    )
    shares = (
        lax.psum_scatter(
            attn_gain_part.astype(jnp.bfloat16), "fsdp", scatter_dimension=0, tiled=True
        ).astype(jnp.float32),
        lax.psum_scatter(
            q_down_part.astype(jnp.bfloat16), "fsdp", scatter_dimension=0, tiled=True
        ).astype(jnp.float32),
        lax.psum_scatter(
            q_gain_part.astype(jnp.bfloat16), "fsdp", scatter_dimension=0, tiled=True
        ).astype(jnp.float32),
        lax.psum_scatter(
            q_up_part.astype(jnp.bfloat16), "fsdp", scatter_dimension=0, tiled=True
        ).astype(jnp.float32),
        lax.psum_scatter(
            kv_down_part.astype(jnp.bfloat16), "fsdp", scatter_dimension=0, tiled=True
        ).astype(jnp.float32),
        lax.psum_scatter(
            kv_gain_part.astype(jnp.bfloat16), "fsdp", scatter_dimension=0, tiled=True
        ).astype(jnp.float32),
        lax.psum_scatter(
            kv_up_part.astype(jnp.bfloat16), "fsdp", scatter_dimension=0, tiled=True
        ).astype(jnp.float32),
        lax.psum_scatter(
            out_proj_part.astype(jnp.bfloat16), "fsdp", scatter_dimension=0, tiled=True
        ).astype(jnp.float32),
        lax.psum_scatter(
            mlp_gain_part.astype(jnp.bfloat16), "fsdp", scatter_dimension=0, tiled=True
        ).astype(jnp.float32),
    )
    totals = (
        lax.psum(shares[0].astype(jnp.bfloat16), "seq").astype(jnp.float32),
        lax.psum(shares[1].astype(jnp.bfloat16), "seq").astype(jnp.float32),
        lax.psum(shares[2].astype(jnp.bfloat16), "seq").astype(jnp.float32),
        lax.psum(shares[3].astype(jnp.bfloat16), "seq").astype(jnp.float32),
        lax.psum(shares[4].astype(jnp.bfloat16), "seq").astype(jnp.float32),
        lax.psum(shares[5].astype(jnp.bfloat16), "seq").astype(jnp.float32),
        lax.psum(shares[6].astype(jnp.bfloat16), "seq").astype(jnp.float32),
        lax.psum(shares[7].astype(jnp.bfloat16), "seq").astype(jnp.float32),
        lax.psum(shares[8].astype(jnp.bfloat16), "seq").astype(jnp.float32),
        lax.psum(gate_up_grad, "seq").astype(jnp.float32),
        lax.psum(down_grad, "seq").astype(jnp.float32),
    )
    return (
        output,
        grad_input,
        totals[0],
        totals[1],
        totals[2],
        totals[3],
        totals[4],
        totals[5],
        totals[6],
        totals[7],
        totals[8],
        totals[9],
        totals[10],
    )


def solution(mesh):
    placed = (
        P("fsdp", "seq", None),
        P("fsdp", None),
        P("fsdp"),
        P("fsdp", None),
        P("fsdp"),
        P("fsdp", None),
        P("fsdp", None),
        P("fsdp"),
        P("fsdp", None),
        P("fsdp", None),
        P("fsdp"),
        P("fsdp", None),
        P("fsdp", None),
        P("fsdp", "seq", None),
    )
    return jax.shard_map(
        body,
        mesh=mesh,
        in_specs=placed,
        out_specs=(
            P("fsdp", "seq", None),
            P("fsdp", "seq", None),
            P("fsdp"),
            P("fsdp", None),
            P("fsdp"),
            P("fsdp", None),
            P("fsdp", None),
            P("fsdp"),
            P("fsdp", None),
            P("fsdp", None),
            P("fsdp"),
            P("fsdp", None),
            P("fsdp", None),
        ),
        check_vma=False,
    )
```

profile of v0, /device:TPU:0, one launch (start us, length us, event | category | flops | bytes accessed | tf_op | source)
XLA Modules:
  0.0 3177.4 jit_solution(1631463414289713429)
XLA Ops:
  100.5 55.0 %all-to-all-done.2 = bf16[1,512,40,64]{1,3,0,2:T(8,128)(2,1)} async-done(((bf16[1,512,40,64]{1,3,0,2:T(8,128)(2,1)}), bf16[1,512,40,64]{1,3,0,2:T(8,128)(2,1)}, u32[]{:S(2)}, u32[]{:S(2)}) %all-to-all-start.2) | async-done | bytes 2621472 | tf_op jit(solution)/shard_map/all_to_all | solution.py:249
  175.4 72.6 %all-to-all-done.1 = bf16[1,512,40,96]{1,3,0,2:T(8,128)(2,1)} async-done(((bf16[1,512,40,96]{1,3,0,2:T(8,128)(2,1)}), bf16[1,512,40,96]{1,3,0,2:T(8,128)(2,1)}, u32[]{:S(2)}, u32[]{:S(2)}) %all-to-all-start.1) | async-done | bytes 3932192 | tf_op jit(solution)/shard_map/all_to_all | solution.py:248
  277.2 62.7 %all-to-all-done = bf16[1,512,40,96]{1,3,0,2:T(8,128)(2,1)} async-done(((bf16[1,512,40,96]{1,3,0,2:T(8,128)(2,1)}), bf16[1,512,40,96]{1,3,0,2:T(8,128)(2,1)}, u32[]{:S(2)}, u32[]{:S(2)}) %all-to-all-start) | async-done | bytes 3932192 | tf_op jit(solution)/shard_map/all_to_all | solution.py:247
  360.4 237.8 %while.48 = (s32[]{:T(128)}, bf16[4,512,10,64]{1,3,2,0:T(8,128)(2,1)}, f32[4,10,512]{2,1,0:T(8,128)}, s32[4,512]{1,0:T(4,128)S(1)}, s32[2048]{0:T(1024)S(1)}, /*...) while((s32[]{:T(128)}, ...), condition=%wide.region_9.10_spmd.clone, body=%wide.region_6.9_spmd.clone.sunk | while | flops 3485791232 | bytes 148910240 | solution.py:100
  620.4 58.9 %all-to-all-done.3 = bf16[4,2,163840]{2,1,0:T(2,128)(2,1)S(1)} async-done(((bf16[4,2,163840]{2,1,0:T(2,128)(2,1)}), bf16[4,2,163840]{2,1,0:T(2,128)(2,1)S(1)}, u32[]{:S(2)}, u32[]{:S(2)}) %all-to-all-start.3) | async-done | bytes 2621472 | tf_op jit(solution)/shard_map/all_to_all | solution.py:260
  712.3 43.6 %fusion.90 = f32[512,12800]{1,0:T(8,128)} fusion(bf16[2560,12800]{1,0:T(8,128)(2,1)} %all-gather.17.cloned.1.call-done, f32[512,2560]{1,0:T(8,128)} %get-tuple-element.465, f32[2560]{0:T(1024)S(1)} %convert_element_type.240, f32[512]{0:T(512)S(1)} %add_rsqrt_fusion), kind=kOutput, calls=%fused_computation.178 | convolution fusion | flops 33558364160 | bytes 97005568 | tf_op jit(solution)/shard_map/dot_general | solution.py:271
  755.9 33.6 %multiply_convert_fusion.3 = (bf16[512,6400]{1,0:T(8,128)(2,1)}, bf16[512,6400]{1,0:T(8,128)(2,1)}, bf16[512,6400]{1,0:T(8,128)(2,1)}) fusion(f32[512,12800]{1,0:T(8,128)} %fusion.90, bf16[6400,2560]{1,0:T(8,128)(2,1)} %all-gather.19.cloned.1.call-done, bf16[1,512,2560]{2,1,0:T(8,128)(2,1)S(1)} %copy-done.18), kind=kOutput, calls=%fused_computation.61 | convolution fusion | flops 16830300160 | bytes 81264640 | tf_op jit(solution)/shard_map/dot_general | solution.py:171
  789.5 49.6 %multiply_reduce_fusion.1 = (bf16[2560]{0:T(1024)(128)(2,1)}, f32[512]{0:T(512)S(1)}, f32[512,2560]{1,0:T(8,128)}) fusion(f32[512,2560]{1,0:T(8,128)} %get-tuple-element.465, f32[512]{0:T(512)S(1)} %add_rsqrt_fusion, f32[2560]{0:T(1024)S(1)} %convert_element_type.240, bf16[2560,12800]{1,0:T(8,128)(2,1)} %all-gather.17.cloned.1.call-done, ...), kind=kOutput, calls=%fused_computation.93 | convolution fusion | flops 33588508672 | bytes 89148416 | tf_op jit(solution)/shard_map/dot_general | solution.py:171
  863.0 58.6 %all-to-all-done.4 = bf16[1,512,40,64]{1,3,0,2:T(8,128)(2,1)S(1)} async-done(((bf16[1,512,40,64]{1,3,0,2:T(8,128)(2,1)}), bf16[1,512,40,64]{1,3,0,2:T(8,128)(2,1)S(1)}, u32[]{:S(2)}, u32[]{:S(2)}) %all-to-all-start.4) | async-done | bytes 2621472 | tf_op jit(solution)/shard_map/all_to_all | solution.py:308
  933.0 540.8 %while.49 = (s32[]{:T(128)}, f32[2048,10,96]{0,2,1:T(8,128)}, f32[2048,10,64]{0,2,1:T(8,128)}, bf16[4,512,10,96]{1,3,2,0:T(8,128)(2,1)}, bf16[4,512,10,96]{1,3,2...) while((s32[]{:T(128)}, f32[2048,10,96]{0,2,1:T(8,128)}, ...), condition=%wide.region_14.15_spmd.clone, body=%wide.region_12.14_spmd.clone.sunk | while | flops 8895132672 | bytes 375632064 | solution.py:146
  954.5 30.1 multiply_reduce_fusion.11
  984.5 34.2 %multiply_convert_fusion.21 = bf16[10,512,2048]{2,1,0:T(8,128)(2,1)} fusion(f32[10,512,2048]{2,1,0:T(8,128)} %get-tuple-element.612, f32[10,512,2048]{2,1,0:T(8,128)} %fusion.166, f32[10,512]{1,0:T(8,128)S(1)} %get-tuple-element.613, f32[10,512]{1,0:T(8,128)S(1)} %dynamic-slice_bitcast_fusion.2, pred[512,2048]{1,0:T(8,128)(4,1)S(1)} %fusion.167), kind=kLoop, calls=%fused_computation.23.clone.1 | loop fusion | flops 62914560 | bytes 105947136 | tf_op jit(solution)/shard_map/while/body/eval_jaxpr/while/body/eval_jaxpr/convert_element_type | solution.py:130
  1116.8 34.2 %multiply_convert_fusion.21 = bf16[10,512,2048]{2,1,0:T(8,128)(2,1)} fusion(f32[10,512,2048]{2,1,0:T(8,128)} %get-tuple-element.612, f32[10,512,2048]{2,1,0:T(8,128)} %fusion.166, f32[10,512]{1,0:T(8,128)S(1)} %get-tuple-element.613, f32[10,512]{1,0:T(8,128)S(1)} %dynamic-slice_bitcast_fusion.2, pred[512,2048]{1,0:T(8,128)(4,1)S(1)} %fusion.167), kind=kLoop, calls=%fused_computation.23.clone.1 | loop fusion | flops 62914560 | bytes 105947136 | tf_op jit(solution)/shard_map/while/body/eval_jaxpr/while/body/eval_jaxpr/convert_element_type | solution.py:130
  1222.7 30.0 multiply_reduce_fusion.11
  1252.8 34.2 %multiply_convert_fusion.21 = bf16[10,512,2048]{2,1,0:T(8,128)(2,1)} fusion(f32[10,512,2048]{2,1,0:T(8,128)} %get-tuple-element.612, f32[10,512,2048]{2,1,0:T(8,128)} %fusion.166, f32[10,512]{1,0:T(8,128)S(1)} %get-tuple-element.613, f32[10,512]{1,0:T(8,128)S(1)} %dynamic-slice_bitcast_fusion.2, pred[512,2048]{1,0:T(8,128)(4,1)S(1)} %fusion.167), kind=kLoop, calls=%fused_computation.23.clone.1 | loop fusion | flops 62914560 | bytes 105947136 | tf_op jit(solution)/shard_map/while/body/eval_jaxpr/while/body/eval_jaxpr/convert_element_type | solution.py:130
  1358.7 30.0 multiply_reduce_fusion.11
  1388.7 34.2 %multiply_convert_fusion.21 = bf16[10,512,2048]{2,1,0:T(8,128)(2,1)} fusion(f32[10,512,2048]{2,1,0:T(8,128)} %get-tuple-element.612, f32[10,512,2048]{2,1,0:T(8,128)} %fusion.166, f32[10,512]{1,0:T(8,128)S(1)} %get-tuple-element.613, f32[10,512]{1,0:T(8,128)S(1)} %dynamic-slice_bitcast_fusion.2, pred[512,2048]{1,0:T(8,128)(4,1)S(1)} %fusion.167), kind=kLoop, calls=%fused_computation.23.clone.1 | loop fusion | flops 62914560 | bytes 105947136 | tf_op jit(solution)/shard_map/while/body/eval_jaxpr/while/body/eval_jaxpr/convert_element_type | solution.py:130
  1591.2 64.8 %all-to-all-done.6 = bf16[4,2,245760]{2,1,0:T(2,128)(2,1)} async-done(((bf16[4,2,245760]{2,1,0:T(2,128)(2,1)}), bf16[4,2,245760]{2,1,0:T(2,128)(2,1)}, u32[]{:S(2)}, u32[]{:S(2)}) %all-to-all-start.6) | async-done | bytes 3932192 | tf_op jit(solution)/shard_map/all_to_all | solution.py:332
  1837.3 46.9 %convolution_convert_fusion = bf16[2560,12800]{1,0:T(8,128)(2,1)} fusion(bf16[512,6400]{1,0:T(8,128)(2,1)} %get-tuple-element.437, bf16[512,6400]{1,0:T(8,128)(2,1)} %get-tuple-element.436, f32[512,2560]{1,0:T(8,128)} %get-tuple-element.465, f32[2560]{0:T(1024)S(1)} %copy-done.41, f32[512]{0:T(512)S(1)} %copy-done.52), kind=kOutput, calls=%fused_computation.56 | convolution fusion | flops 33617346560 | bytes 83898368 | tf_op jit(solution)/shard_map/dot_general | solution.py:165
  1886.3 37.0 %reduce-scatter.12.cloned.1.call-done = bf16[96,3840]{1,0:T(8,128)(2,1)} async-done(((bf16[768,3840]{1,0:T(8,128)(2,1)}), bf16[96,3840]{1,0:T(8,128)(2,1)}) %reduce-scatter.12.cloned.1.call-update) | async-done | bytes 737296 | tf_op jit(solution)/shard_map/reduce_scatter | solution.py:394
  1923.3 99.2 %reduce-scatter.16.cloned.1.call-done = bf16[320,2560]{1,0:T(8,128)(2,1)} async-done(((bf16[2560,2560]{1,0:T(8,128)(2,1)}), bf16[320,2560]{1,0:T(8,128)(2,1)}) %reduce-scatter.16.cloned.1.call-update) | async-done | bytes 1638416 | tf_op jit(solution)/shard_map/reduce_scatter | solution.py:406
  2022.5 205.5 %reduce-scatter.20.cloned.1.call-done = bf16[800,2560]{1,0:T(8,128)(2,1)} async-done(((bf16[6400,2560]{1,0:T(8,128)(2,1)}), bf16[800,2560]{1,0:T(8,128)(2,1)}) %reduce-scatter.20.cloned.1.call-update) | async-done | bytes 4096016 | tf_op jit(solution)/shard_map/reduce_scatter | solution.py:372
  2228.0 380.5 %reduce-scatter.18.cloned.1.call-done = bf16[320,12800]{1,0:T(8,128)(2,1)} async-done(((bf16[2560,12800]{1,0:T(8,128)(2,1)}), bf16[320,12800]{1,0:T(8,128)(2,1)}) %reduce-scatter.18.cloned.1.call-update) | async-done | bytes 8192016 | tf_op jit(solution)/shard_map/reduce_scatter | solution.py:378
  2692.3 451.4 %all-reduce.14.cloned.1.call-done = (bf16[320,768]{1,0:T(8,128)(2,1)}, bf16[96,3840]{1,0:T(8,128)(2,1)}, bf16[320,288]{0,1:T(8,128)(2,1)}, bf16[32,5120]{1,0:T(8...) async-done(((bf16[320,768]{1,0:T(8,128)(2,1)}, bf16[96,3840]{1,0:T(8,128)(2,1)}, bf16[320,288]{0,1:T(8,128)(2,1)}, ...) | async-done | bytes 15667216 | tf_op jit(solution)/shard_map/psum | solution.py:415
  (390 shorter events, 1210.3 us)
Async XLA Ops:
  7.2 34.0 %all-gather.21.cloned.1.call-start = ((), (), s32[]{:S(2)}) async-start(), calls=%async_computation.27 | async-start | bytes 1990656 | tf_op jit(solution)/shard_map/all_gather | solution.py:206
  7.9 63.4 %all-gather.13.cloned.1.call-start = ((), (), s32[]{:S(2)}) async-start(), calls=%async_computation.17 | async-start | bytes 2949120 | tf_op jit(solution)/shard_map/all_gather | solution.py:208
  8.7 151.9 %all-gather.9.cloned.1.call-start = ((), (), s32[]{:S(2)}) async-start(), calls=%async_computation.15 | async-start | bytes 4423680 | tf_op jit(solution)/shard_map/all_gather | solution.py:203
  9.5 156.7 %all-gather.11.cloned.1.call-start = ((), (), s32[]{:S(2)}) async-start(), calls=%async_computation.16 | async-start | bytes 6635520 | tf_op jit(solution)/shard_map/all_gather | solution.py:205
  10.0 689.4 %all-gather.15.cloned.1.call-start = ((), (), s32[]{:S(2)}) async-start(), calls=%async_computation.18 | async-start | bytes 14745600 | tf_op jit(solution)/shard_map/all_gather | solution.py:209
  10.6 701.6 %all-gather.17.cloned.1.call-start = ((), (), s32[]{:S(2)}) async-start(), calls=%async_computation.19 | async-start | bytes 73728000 | tf_op jit(solution)/shard_map/all_gather | solution.py:266
  90.6 64.9 %all-to-all-start.2 = ((bf16[1,512,40,64]{1,3,0,2:T(8,128)(2,1)}), bf16[1,512,40,64]{1,3,0,2:T(8,128)(2,1)}, u32[]{:S(2)}, u32[]{:S(2)}) async-start(bf16[1,512,40,64]{1,3,0,2:T(8,128)(2,1)} %get-tuple-element.443), calls=%async_computation.2 | async-start | bytes 5242880 | tf_op jit(solution)/shard_map/all_to_all | solution.py:249
  155.5 92.5 %all-to-all-start.1 = ((bf16[1,512,40,96]{1,3,0,2:T(8,128)(2,1)}), bf16[1,512,40,96]{1,3,0,2:T(8,128)(2,1)}, u32[]{:S(2)}, u32[]{:S(2)}) async-start(bf16[1,512,40,96]{1,3,0,2:T(8,128)(2,1)} %maximum_bitcast_fusion.1), calls=%async_computation.1 | async-start | bytes 7864320 | tf_op jit(solution)/shard_map/all_to_all | solution.py:248
  247.9 92.0 %all-to-all-start = ((bf16[1,512,40,96]{1,3,0,2:T(8,128)(2,1)}), bf16[1,512,40,96]{1,3,0,2:T(8,128)(2,1)}, u32[]{:S(2)}, u32[]{:S(2)}) async-start(bf16[1,512,40,96]{1,3,0,2:T(8,128)(2,1)} %maximum_bitcast_fusion), calls=%async_computation | async-start | bytes 7864320 | tf_op jit(solution)/shard_map/all_to_all | solution.py:247
  252.8 503.1 %all-gather.19.cloned.1.call-start = ((), (), s32[]{:S(2)}) async-start(), calls=%async_computation.20 | async-start | bytes 36864000 | tf_op jit(solution)/shard_map/all_gather | solution.py:267
  616.1 63.2 %all-to-all-start.3 = ((bf16[4,2,163840]{2,1,0:T(2,128)(2,1)}), bf16[4,2,163840]{2,1,0:T(2,128)(2,1)S(1)}, u32[]{:S(2)}, u32[]{:S(2)}) async-start(bf16[4,2,163840]{2,1,0:T(2,128)(2,1)} %reshape.697), calls=%async_computation.3 | async-start | bytes 5242880 | tf_op jit(solution)/shard_map/all_to_all | solution.py:260
  620.4 218.7 %copy-start.40 = (f32[2560]{0:T(1024)}, f32[2560]{0:T(1024)S(1)}, u32[]{:S(2)}) copy-start(f32[2560]{0:T(1024)S(1)} %convert_element_type.240) | copy-start | bytes 30724
  859.3 62.3 %all-to-all-start.4 = ((bf16[1,512,40,64]{1,3,0,2:T(8,128)(2,1)}), bf16[1,512,40,64]{1,3,0,2:T(8,128)(2,1)S(1)}, u32[]{:S(2)}, u32[]{:S(2)}) async-start(bf16[1,512,40,64]{1,3,0,2:T(8,128)(2,1)} %bitcast.240), calls=%async_computation.4 | async-start | bytes 5242880 | tf_op jit(solution)/shard_map/all_to_all | solution.py:308
  1501.6 62.5 %all-to-all-start.7 = ((bf16[4,2,163840]{2,1,0:T(2,128)(2,1)}), bf16[4,2,163840]{2,1,0:T(2,128)(2,1)S(1)}, u32[]{:S(2)}, u32[]{:S(2)}) async-start(bf16[4,2,163840]{2,1,0:T(2,128)(2,1)} %reshape.703), calls=%async_computation.7 | async-start | bytes 5242880 | tf_op jit(solution)/shard_map/all_to_all | solution.py:333
  1564.1 91.9 %all-to-all-start.6 = ((bf16[4,2,245760]{2,1,0:T(2,128)(2,1)}), bf16[4,2,245760]{2,1,0:T(2,128)(2,1)}, u32[]{:S(2)}, u32[]{:S(2)}) async-start(bf16[4,2,245760]{2,1,0:T(2,128)(2,1)} %reshape.701), calls=%async_computation.6 | async-start | bytes 7864320 | tf_op jit(solution)/shard_map/all_to_all | solution.py:332
  1656.0 91.9 %all-to-all-start.5 = ((bf16[4,2,245760]{2,1,0:T(2,128)(2,1)}), bf16[4,2,245760]{2,1,0:T(2,128)(2,1)}, u32[]{:S(2)}, u32[]{:S(2)}) async-start(bf16[4,2,245760]{2,1,0:T(2,128)(2,1)} %reshape.699), calls=%async_computation.5 | async-start | bytes 7864320 | tf_op jit(solution)/shard_map/all_to_all | solution.py:331
  1660.8 223.8 %reduce-scatter.22.cloned.1.call-start = ((), (), s32[]{:S(2)}) async-start(), calls=%async_computation.28 | async-start | bytes 2211840
  1716.0 170.3 %reduce-scatter.14.cloned.1.call-start = ((), (), s32[]{:S(2)}) async-start(), calls=%async_computation.23 | async-start | bytes 2949120 | tf_op jit(solution)/shard_map/reduce_scatter | solution.py:403
  1721.7 164.7 %reduce-scatter.10.cloned.1.call-start = ((), (), s32[]{:S(2)}) async-start(), calls=%async_computation.21 | async-start | bytes 4423680 | tf_op jit(solution)/shard_map/reduce_scatter | solution.py:388
  1787.3 136.1 %reduce-scatter.12.cloned.1.call-start = ((), (), s32[]{:S(2)}) async-start(), calls=%async_computation.22 | async-start | bytes 6635520 | tf_op jit(solution)/shard_map/reduce_scatter | solution.py:394
  1796.4 226.1 %reduce-scatter.16.cloned.1.call-start = ((), (), s32[]{:S(2)}) async-start(), calls=%async_computation.24 | async-start | bytes 14745600 | tf_op jit(solution)/shard_map/reduce_scatter | solution.py:406
  1810.8 417.2 %reduce-scatter.20.cloned.1.call-start = ((), (), s32[]{:S(2)}) async-start(), calls=%async_computation.26 | async-start | bytes 36864000 | tf_op jit(solution)/shard_map/reduce_scatter | solution.py:372
  1836.6 771.9 %reduce-scatter.18.cloned.1.call-start = ((), (), s32[]{:S(2)}) async-start(), calls=%async_computation.25 | async-start | bytes 73728000 | tf_op jit(solution)/shard_map/reduce_scatter | solution.py:378
  1884.3 1259.4 %all-reduce.14.cloned.1.call-start = ((), (), s32[]{:S(2)}) async-start(), calls=%async_computation.29 | async-start | bytes 31408128 | tf_op jit(solution)/shard_map/psum | solution.py:415
  (72 other events, 1033.8 us)
Sparse Core Ops, SparseCore 0:
  9.9 29.3 all-gather.20
  41.2 30.1 all-gather.12
  73.2 35.6 all-gather.8
  110.6 43.8 all-gather.10
  156.3 74.3 all-gather.14
  232.4 296.1 all-gather.16
  530.5 157.4 all-gather.18
  1716.1 41.5 reduce-scatter.21
  1762.0 43.6 reduce-scatter.13
  1809.5 50.0 reduce-scatter.9
  1863.6 59.6 reduce-scatter.11
  1927.3 95.1 reduce-scatter.15
  2026.3 201.6 reduce-scatter.19
  2231.6 376.8 reduce-scatter.17
  2612.3 531.3 all-reduce.13
where the time goes:
time: 3190 us; the launch traced here: 3180 us
  waiting for transfers between devices  1620 us (51%)
  matrix products  860 us (27%)
  local copies, waits for them, and re-layouts  290 us (9%)
  other arithmetic  284 us (9%)
  blocking collectives  62.1 us (2%)
  starting transfers between devices  37.2 us (1%)
    psum x1, waiting for transfers between devices, body(): lax.psum(shares[1].astype(jnp.bfloat16), 'seq').astype(jnp.float32)  451 us
    reduce_scatter x1, waiting for transfers between devices, body(): lax.psum_scatter(contract_rows(mlp_normed, grad_gate_up).astype(jnp.bfloa...  380 us
    reduce_scatter x1, waiting for transfers between devices, body(): lax.psum_scatter(contract_rows(activated, grad_mlp).astype(jnp.bfloat16),...  205 us
    dot_general x8, matrix products, masked_scores(): jnp.einsum('qhd,khd->hqk', q_block, key_rows, preferred_element_type=jnp....  152 us
    convert_element_type x4, other arithmetic, one_block(): grad_scores = (attn_probs * (grad_probs - inner_sum)).astype(jnp.bfloat16)  137 us
    dot_general x4, matrix products, one_block(): jnp.einsum('qhd,khd->hqk', grad_block, value_rows, preferred_element_type...  120 us
    unnamed x158, local copies, waits for them, and re-layouts  120 us
    dot_general x7, matrix products, contract_cols(): lax.dot_general(left, right, (((1,), (1,)), ((), ())), preferred_element_...  108 us
  transfers between devices with their start and end apart: 23, of which 14 were waited for; matrix products, arithmetic and copies ran while one was open for 22% of the time, Pallas kernels for 0%

commit v1 on v0

v1 whole, which is shorter than its diff:
```python
import functools, math
import jax
import jax.numpy as jnp
from jax import lax
from jax.experimental import pallas as pl
from jax.experimental.pallas import tpu as pltpu
from jax.sharding import PartitionSpec as P

HEADS = 40
NOPE = 64
ROPE = 32
PROMPT = 1024
LANES = 128
NEG = -1e30
SCALE = (NOPE + ROPE) ** -0.5
LOG2E = math.log2(math.e)
LN2 = math.log(2.0)


def dot(a, b, ca, cb):
    return lax.dot_general(a, b, (((ca,), (cb,)), ((), ())), preferred_element_type=jnp.float32)


def fwd_kernel(bounds, qlat, qup, kvn, kvup, krope, cos, sin_r, sin_l, start, out, q_out, lse_out, m_scr, acc_scr, *, full_rows, mask_rows):
    rows = qlat.shape[0]
    lane = lax.broadcasted_iota(jnp.int32, (1, LANES), 1)
    low_half = lane < NOPE
    raw = dot(qlat[...], qup[...], 1, 0)
    for h in range(2):
        u = raw[:, h * LANES:(h + 1) * LANES]
        turned = u * cos[...] + pltpu.roll(u, 16, 1) * sin_r[...] + pltpu.roll(u, LANES - 16, 1) * sin_l[...]
        q_out[:, h * LANES:(h + 1) * LANES] = turned.astype(jnp.bfloat16)
    m_scr[...] = jnp.full_like(m_scr, NEG)
    acc_scr[...] = jnp.zeros_like(acc_scr)

    def block(first, size, masked):
        span = pl.ds(first, size)
        kv = dot(kvn[span, :], kvup[...], 1, 0).astype(jnp.bfloat16)
        rope_rows = krope[span, :]
        if masked:
            key_index = first + lax.broadcasted_iota(jnp.int32, (size, rows), 0)
            own = bounds[3] + lax.broadcasted_iota(jnp.int32, (size, rows), 1)
            allowed = (key_index <= own) & ((key_index >= start[...]) | (key_index < PROMPT))
        for h in range(2):
            kv_h = kv[:, h * LANES:(h + 1) * LANES]
            key = jnp.where(low_half, kv_h, rope_rows)
            val = jnp.where(low_half, jnp.ones_like(kv_h), kv_h)
            s = dot(key, q_out[:, h * LANES:(h + 1) * LANES], 1, 1)
            if masked:
                s = jnp.where(allowed, s, NEG)
            m_old = m_scr[h:h + 1, :]
            m_new = jnp.maximum(m_old, jnp.max(s, axis=0, keepdims=True))
            p = jnp.exp2(s - m_new)
            m_scr[h:h + 1, :] = m_new
            acc_scr[h] = acc_scr[h] * jnp.exp2(m_old - m_new) + dot(val, p.astype(jnp.bfloat16), 0, 0)

    lax.fori_loop(0, bounds[0], lambda i, c: (block(pl.multiple_of(i * full_rows, full_rows), full_rows, False), c)[1], 0)
    lax.fori_loop(bounds[1], bounds[2], lambda i, c: (block(pl.multiple_of(i * mask_rows, mask_rows), mask_rows, True), c)[1], 0)
    parts = []
    for h in range(2):
        total = acc_scr[h, 0:1, :]
        parts.append(acc_scr[h, NOPE:, :] / total)
        lse_out[h:h + 1, :] = m_scr[h:h + 1, :] + jnp.log2(total)
    out[...] = jnp.concatenate(parts, axis=0).T.astype(jnp.bfloat16)


def attend_forward(bounds, qlat, qup, kvn, kvup, krope, cos, sin_r, sin_l, start, full_rows=512, mask_rows=256):
    rows, rank = qlat.shape
    keys = kvn.shape[0]
    whole = lambda *_: (0, 0)
    col = lambda i, b: (0, i)
    pairs = HEADS // 2
    flops = pairs * 2 * 2 * rows * 1536 * LANES * 2
    return pl.pallas_call(
        functools.partial(fwd_kernel, full_rows=full_rows, mask_rows=mask_rows),
        grid_spec=pltpu.PrefetchScalarGridSpec(
            num_scalar_prefetch=1,
            grid=(pairs,),
            in_specs=[
                pl.BlockSpec((rows, rank), whole),
                pl.BlockSpec((rank, 2 * LANES), col),
                pl.BlockSpec(kvn.shape, whole),
                pl.BlockSpec((kvn.shape[1], 2 * LANES), col),
                pl.BlockSpec(krope.shape, whole),
                pl.BlockSpec(cos.shape, whole),
                pl.BlockSpec(cos.shape, whole),
                pl.BlockSpec(cos.shape, whole),
                pl.BlockSpec((1, rows), whole),
            ],
            out_specs=[
                pl.BlockSpec((rows, LANES), col),
                pl.BlockSpec((rows, 2 * LANES), col),
                pl.BlockSpec((8, rows), lambda i, b: (i, 0)),
            ],
            scratch_shapes=[pltpu.VMEM((8, rows), jnp.float32), pltpu.VMEM((2, LANES, rows), jnp.float32)],
        ),
        out_shape=[
            jax.ShapeDtypeStruct((rows, HEADS * NOPE), jnp.bfloat16),
            jax.ShapeDtypeStruct((rows, HEADS * LANES), jnp.bfloat16),
            jax.ShapeDtypeStruct((pairs * 8, rows), jnp.float32),
        ],
        compiler_params=pltpu.CompilerParams(vmem_limit_bytes=48 << 20),
        cost_estimate=pl.CostEstimate(flops=flops, bytes_accessed=30 << 20, transcendentals=HEADS * rows * 1536),
        name="attend_forward",
    )(bounds, qlat, qup, kvn, kvup, krope, cos, sin_r, sin_l, start)


def bwd_kernel(bounds, q, kvn, kvn_t, kvup, krope, grad_out, out, lse, cos, sin_r, sin_l, start, dq_out, dkvup, dkvn, drope, go_scr, dq_scr, delta_scr, *, full_rows, mask_rows):
    rows = q.shape[0]
    lane = lax.broadcasted_iota(jnp.int32, (1, LANES), 1)
    low_half = lane < NOPE

    @pl.when(pl.program_id(0) == 0)
    def _():
        dkvn[...] = jnp.zeros_like(dkvn)
        drope[...] = jnp.zeros_like(drope)

    go = grad_out[...].astype(jnp.float32)
    prod_t = (go * out[...].astype(jnp.float32)).T
    delta_scr[0:1, :] = jnp.sum(prod_t[:NOPE], axis=0, keepdims=True)
    delta_scr[1:2, :] = jnp.sum(prod_t[NOPE:], axis=0, keepdims=True)
    zero = jnp.zeros_like(go)
    go_scr[0] = jnp.where(low_half, zero, pltpu.roll(go, NOPE, 1)).astype(jnp.bfloat16)
    go_scr[1] = jnp.where(low_half, zero, go).astype(jnp.bfloat16)
    dq_scr[...] = jnp.zeros_like(dq_scr)
    dkvup[...] = jnp.zeros_like(dkvup)

    def block(first, size, masked):
        span = pl.ds(first, size)
        kv = dot(kvn[span, :], kvup[...], 1, 0).astype(jnp.bfloat16)
        rope_rows = krope[span, :]
        if masked:
            key_index = first + lax.broadcasted_iota(jnp.int32, (size, rows), 0)
            own = bounds[3] + lax.broadcasted_iota(jnp.int32, (size, rows), 1)
            allowed = (key_index <= own) & ((key_index >= start[...]) | (key_index < PROMPT))
        pieces = []
        rope_sum = None
        for h in range(2):
            kv_h = kv[:, h * LANES:(h + 1) * LANES]
            q_h = q[:, h * LANES:(h + 1) * LANES]
            key = jnp.where(low_half, kv_h, rope_rows)
            p = jnp.exp2(dot(key, q_h, 1, 1) - lse[h:h + 1, :])
            if masked:
                p = jnp.where(allowed, p, 0.0)
            ds = (p * (dot(kv_h, go_scr[h], 1, 1) - delta_scr[h:h + 1, :])).astype(jnp.bfloat16)
            dk = dot(ds, q_h, 1, 0) * LN2
            dv = dot(p.astype(jnp.bfloat16), go_scr[h], 1, 0)
            dq_scr[h] += dot(key, ds, 0, 0)
            pieces.append(jnp.where(low_half, dk, dv).astype(jnp.bfloat16))
            rope_sum = dk if rope_sum is None else rope_sum + dk
        dkv = jnp.concatenate(pieces, axis=1)
        drope[span, :] += rope_sum
        dkvn[span, :] += dot(dkv, kvup[...], 1, 1)
        dkvup[...] += dot(kvn_t[:, span], dkv, 1, 0)

    lax.fori_loop(0, bounds[0], lambda i, c: (block(pl.multiple_of(i * full_rows, full_rows), full_rows, False), c)[1], 0)
    lax.fori_loop(bounds[1], bounds[2], lambda i, c: (block(pl.multiple_of(i * mask_rows, mask_rows), mask_rows, True), c)[1], 0)
    for h in range(2):
        u = dq_scr[h].T * SCALE
        turned = u * cos[...] - pltpu.roll(u, 16, 1) * sin_r[...] - pltpu.roll(u, LANES - 16, 1) * sin_l[...]
        dq_out[:, h * LANES:(h + 1) * LANES] = turned.astype(jnp.bfloat16)


def attend_backward(bounds, q, kvn, kvn_t, kvup, krope, grad_out, out, lse, cos, sin_r, sin_l, start, full_rows=512, mask_rows=256):
    rows = q.shape[0]
    keys, rank = kvn.shape
    whole = lambda *_: (0, 0)
    col = lambda i, b: (0, i)
    pairs = HEADS // 2
    flops = pairs * 2 * 5 * rows * 1536 * LANES * 2
    return pl.pallas_call(
        functools.partial(bwd_kernel, full_rows=full_rows, mask_rows=mask_rows),
        grid_spec=pltpu.PrefetchScalarGridSpec(
            num_scalar_prefetch=1,
            grid=(pairs,),
            in_specs=[
                pl.BlockSpec((rows, 2 * LANES), col),
                pl.BlockSpec(kvn.shape, whole),
                pl.BlockSpec(kvn_t.shape, whole),
                pl.BlockSpec((rank, 2 * LANES), col),
                pl.BlockSpec(krope.shape, whole),
                pl.BlockSpec((rows, LANES), col),
                pl.BlockSpec((rows, LANES), col),
                pl.BlockSpec((8, rows), lambda i, b: (i, 0)),
                pl.BlockSpec(cos.shape, whole),
                pl.BlockSpec(cos.shape, whole),
                pl.BlockSpec(cos.shape, whole),
                pl.BlockSpec((1, rows), whole),
            ],
            out_specs=[
                pl.BlockSpec((rows, 2 * LANES), col),
                pl.BlockSpec((rank, 2 * LANES), col),
                pl.BlockSpec((keys, rank), whole),
                pl.BlockSpec((keys, LANES), whole),
            ],
            scratch_shapes=[
                pltpu.VMEM((2, rows, LANES), jnp.bfloat16),
                pltpu.VMEM((2, LANES, rows), jnp.float32),
                pltpu.VMEM((8, rows), jnp.float32),
            ],
        ),
        out_shape=[
            jax.ShapeDtypeStruct((rows, HEADS * LANES), jnp.bfloat16),
            jax.ShapeDtypeStruct((rank, HEADS * LANES), jnp.float32),
            jax.ShapeDtypeStruct((keys, rank), jnp.float32),
            jax.ShapeDtypeStruct((keys, LANES), jnp.float32),
        ],
        compiler_params=pltpu.CompilerParams(vmem_limit_bytes=48 << 20),
        cost_estimate=pl.CostEstimate(flops=flops, bytes_accessed=40 << 20, transcendentals=HEADS * rows * 1536),
        name="attend_backward",
    )(bounds, q, kvn, kvn_t, kvup, krope, grad_out, out, lse, cos, sin_r, sin_l, start)


D = 2560
FF = 6400
CONTS = 4
variance_eps = 1e-05
depth_scale = 1.4 / math.sqrt(62.0)
BF16 = jnp.bfloat16
F32 = jnp.float32


def rms_forward(values, gain_vector):
    inverse = lax.rsqrt(jnp.mean(values * values, axis=-1, keepdims=True) + variance_eps)
    return (values * inverse * gain_vector, inverse)


def rms_backward(values, inverse, gain_vector, upstream):
    scaled = upstream * gain_vector
    inner_mean = jnp.mean(scaled * values, axis=-1, keepdims=True)
    grad_values = inverse * scaled - values * inverse * inverse * inverse * inner_mean
    grad_gain = jnp.sum(upstream * values * inverse, axis=0)
    return (grad_values, grad_gain)


def segment_starts(lengths, index):
    own = jnp.zeros_like(index)
    begin = jnp.int32(PROMPT)
    for c in range(CONTS):
        own = jnp.where(index >= begin, begin, own)
        begin = begin + lengths[c]
    return own


def rope_tables(position):
    frequency = jnp.exp(jnp.arange(ROPE // 2, dtype=F32) * (-2.0 * math.log(10000.0) / ROPE))
    angles = position.astype(F32)[:, None] * frequency[None, :]
    cosine, sine = jnp.cos(angles), jnp.sin(angles)
    rows = position.shape[0]
    zeros = lambda n: jnp.zeros((rows, n), F32)
    return (
        jnp.concatenate([jnp.ones((rows, NOPE), F32), cosine, cosine, zeros(32)], axis=1),
        jnp.concatenate([zeros(80), sine, zeros(32)], axis=1),
        jnp.concatenate([zeros(64), -sine, zeros(48)], axis=1),
        cosine,
        sine,
    )


def rotate(values, cosine, sine):
    first, second = values[:, : ROPE // 2], values[:, ROPE // 2 :]
    return jnp.concatenate([first * cosine - second * sine, second * cosine + first * sine], axis=1)


def swap(tensor, bit, n):
    return lax.ppermute(tensor, "fsdp", [(i, i ^ bit) for i in range(n)])


def bit_orders(n):
    bits = []
    bit = 2
    while bit < n:
        bits.append(bit)
        bit *= 2
    return [bits, bits[::-1]]


def chip_gather(tensor, n):
    half = tensor.shape[0] // 2
    gathered = []
    for part, order in enumerate(bit_orders(n)):
        blocks = {0: tensor[part * half : (part + 1) * half]}
        for bit in order:
            blocks.update({r | bit: swap(block, bit, n) for r, block in list(blocks.items())})
        gathered.append(blocks)
    return [gathered[part][r] for r in range(0, n, 2) for part in range(2)]


def chip_scatter(pieces, n):
    sums = []
    for part, order in enumerate(bit_orders(n)):
        blocks = {r: pieces[r + part] for r in range(0, n, 2)}
        for bit in order[::-1]:
            kept = {r: block for r, block in blocks.items() if not r & bit}
            for r in kept:
                arrived = swap(blocks[r | bit].astype(BF16), bit, n)
                kept[r] = kept[r].astype(F32) + arrived.astype(F32)
            blocks = kept
        sums.append(blocks[0].astype(F32))
    return jnp.concatenate(sums, axis=0)


def body(
    n,
    block_input,
    cont_lengths,
    attn_gain,
    q_down,
    q_gain,
    q_up,
    kv_down,
    kv_gain,
    kv_up,
    out_proj,
    mlp_gain,
    gate_up,
    down_proj,
    out_cotangent,
):
    rows = block_input.shape[1]
    chips = n // 2
    ff_chip = FF // chips
    group_len = rows * lax.axis_size("seq")
    device = lax.axis_index("fsdp")
    core = device % 2
    same_core = [[2 * c + k for c in range(chips)] for k in range(2)]
    pairs = [[2 * c, 2 * c + 1] for c in range(chips)]
    rank_q, rank_kv = q_up.shape[0] * n, kv_up.shape[0] * n
    first_row = lax.axis_index("seq") * rows
    index = first_row + jnp.arange(rows, dtype=jnp.int32)
    own_start = segment_starts(cont_lengths[0], index)
    position = jnp.where(own_start > 0, PROMPT + index - own_start, index)
    cos, sin_r, sin_l, cosine, sine = rope_tables(position)
    fold = SCALE * LOG2E
    start_row = own_start[None, :]
    full_rows, mask_rows = 512, 256
    full_blocks = jnp.minimum(first_row, PROMPT) // full_rows
    bounds = jnp.stack([
        full_blocks,
        jnp.where(first_row < PROMPT, full_blocks * (full_rows // mask_rows), own_start[0] // mask_rows),
        (first_row + rows) // mask_rows,
        first_row,
    ]).astype(jnp.int32)

    gains = lax.all_gather(jnp.concatenate([attn_gain, mlp_gain, q_gain, kv_gain]), "fsdp", axis=0)
    widths = [v.shape[0] for v in (attn_gain, mlp_gain, q_gain, kv_gain)]
    gain_list = []
    at = 0
    for width in widths:
        gain_list.append(gains[:, at : at + width].reshape(-1).astype(F32))
        at += width
    attn_gain_all, mlp_gain_all, q_gain_all, kv_gain_all = gain_list

    down_all = lax.all_gather(jnp.concatenate([q_down, kv_down], axis=1), "fsdp", axis=0, tiled=True)
    q_up_wide = jnp.pad(q_up.reshape(-1, HEADS, NOPE + ROPE), ((0, 0), (0, 0), (0, ROPE))).reshape(-1, HEADS * LANES)
    q_up_all = lax.all_gather(q_up_wide, "fsdp", axis=0, tiled=True)
    kv_up_all = lax.all_gather(kv_up, "fsdp", axis=0, tiled=True)
    out_proj_all = lax.all_gather(out_proj, "fsdp", axis=0, tiled=True)

    token_rows = block_input[0].astype(F32)
    normed_float, attn_inverse = rms_forward(token_rows, attn_gain_all)
    normed = normed_float.astype(BF16)
    latent = jnp.dot(normed, down_all, preferred_element_type=F32)
    q_latent, kv_latent, rope_latent = jnp.split(latent, [rank_q, rank_q + rank_kv], axis=1)
    q_lat_float, q_inverse = rms_forward(q_latent, q_gain_all)
    q_lat_normed = q_lat_float.astype(BF16)
    kv_float, kv_inverse = rms_forward(kv_latent, kv_gain_all)
    key_rope = jnp.pad(rotate(rope_latent, cosine, sine), ((0, 0), (NOPE, LANES - NOPE - ROPE)))
    kv_own = jnp.concatenate([kv_float, key_rope], axis=1).astype(BF16)
    kv_all = lax.all_gather(kv_own, "seq", axis=0, tiled=True)
    kv_normed, key_rope_all = kv_all[:, :rank_kv], kv_all[:, rank_kv:]

    attended, queries, log_total = attend_forward(
        bounds, q_lat_normed, q_up_all, kv_normed, kv_up_all, key_rope_all,
        cos * fold, sin_r * fold, sin_l * fold, start_row, full_rows, mask_rows,
    )
    attn_branch = jnp.dot(attended, out_proj_all, preferred_element_type=F32)
    middle = token_rows + depth_scale * attn_branch
    mlp_float, mlp_inverse = rms_forward(middle, mlp_gain_all)

    hidden = gate_up.reshape(-1, 2, chips, ff_chip)
    hidden = lax.all_to_all(hidden, "fsdp", 2, 0, axis_index_groups=same_core)
    hidden = lax.all_gather(hidden.reshape(chips, -1, 2, ff_chip), "fsdp", axis=1, axis_index_groups=pairs)
    gate_w = hidden[:, :, :, 0].reshape(D, ff_chip)
    up_w = hidden[:, :, :, 1].reshape(D, ff_chip)
    down_w = lax.all_gather(down_proj, "fsdp", axis=0, tiled=True, axis_index_groups=pairs)

    cotangent = out_cotangent[0].astype(F32)
    grad_mlp = jnp.concatenate(chip_gather((depth_scale * cotangent).astype(BF16), n), axis=0)
    grad_act = dot(grad_mlp, down_w, 1, 1)
    mlp_normed = jnp.concatenate(chip_gather(mlp_float.astype(BF16), n), axis=0)
    gate_part = jnp.dot(mlp_normed, gate_w, preferred_element_type=F32)
    up_part = jnp.dot(mlp_normed, up_w, preferred_element_type=F32)
    gate_sigmoid = jax.nn.sigmoid(gate_part)
    silu_gate = gate_part * gate_sigmoid
    activated = (silu_gate * up_part).astype(BF16)
    grad_gate = (grad_act * up_part * gate_sigmoid * (1.0 + gate_part * (1.0 - gate_sigmoid))).astype(BF16)
    grad_up = (grad_act * silu_gate).astype(BF16)

    def pieces(whole):
        half = rows // 2
        return [whole[i * half : (i + 1) * half] for i in range(n)]

    grad_mlp_normed = chip_scatter(pieces((dot(grad_gate, gate_w, 1, 1) + dot(grad_up, up_w, 1, 1)).astype(BF16)), n)
    mlp_branch = chip_scatter(pieces(jnp.dot(activated, down_w, preferred_element_type=F32).astype(BF16)), n)
    output = (middle + depth_scale * mlp_branch).astype(BF16).reshape(block_input.shape)

    def keep_half(split):
        mine = lax.dynamic_index_in_dim(split, core, 1, keepdims=False)
        other = lax.dynamic_index_in_dim(split, 1 - core, 1, keepdims=False).astype(BF16)
        return (mine.astype(F32) + swap(other, 1, n).astype(F32)).astype(BF16)

    down_part = keep_half(dot(activated, grad_mlp, 0, 0).astype(BF16).reshape(1, 2, ff_chip // 2, D))[0]
    hidden_part = keep_half(
        jnp.stack([dot(mlp_normed, grad_gate, 0, 0).astype(BF16), dot(mlp_normed, grad_up, 0, 0).astype(BF16)], axis=1)
        .reshape(chips, 2, D // n, 2, ff_chip)
    )
    down_grad = lax.psum(down_part, "seq").astype(F32)
    hidden_part = lax.all_to_all(hidden_part, "fsdp", 0, 2, axis_index_groups=same_core)
    gate_up_grad = lax.psum(hidden_part.reshape(D // n, 2 * FF), "seq").astype(F32)

    grad_mid_norm, mlp_gain_part = rms_backward(middle, mlp_inverse, mlp_gain_all, grad_mlp_normed)
    grad_middle = cotangent + grad_mid_norm
    grad_attn = (depth_scale * grad_middle).astype(BF16)
    out_proj_part = dot(attended, grad_attn, 0, 0)
    grad_attended = dot(grad_attn, out_proj_all, 1, 1).astype(BF16)
    grad_q_full, kv_up_part, grad_kv_all, grad_rope_all = attend_backward(
        bounds, queries, kv_normed, kv_normed.T, kv_up_all, key_rope_all, grad_attended, attended, log_total,
        cos, sin_r, sin_l, start_row, full_rows, mask_rows,
    )
    q_up_part = dot(q_lat_normed, grad_q_full, 0, 0)
    grad_q_float, q_gain_part = rms_backward(q_latent, q_inverse, q_gain_all, dot(grad_q_full, q_up_all, 1, 1))
    grad_kv = lax.psum_scatter(
        jnp.concatenate([grad_kv_all, grad_rope_all], axis=1).astype(BF16), "seq", scatter_dimension=0, tiled=True
    ).astype(F32)
    grad_kv_first, kv_gain_part = rms_backward(kv_latent, kv_inverse, kv_gain_all, grad_kv[:, :rank_kv])
    grad_rope = rotate(grad_kv[:, rank_kv + NOPE : rank_kv + NOPE + ROPE], cosine, -sine)
    grad_latent = jnp.concatenate([grad_q_float, grad_kv_first, grad_rope], axis=1).astype(BF16)
    down_all_part = dot(normed, grad_latent, 0, 0)
    grad_normed = dot(grad_latent, down_all, 1, 1)
    grad_in_norm, attn_gain_part = rms_backward(token_rows, attn_inverse, attn_gain_all, grad_normed)
    grad_input = (grad_middle + grad_in_norm).reshape(block_input.shape)

    def reduced(part):
        share = lax.psum_scatter(part.astype(BF16), "fsdp", scatter_dimension=0, tiled=True)
        return lax.psum(share, "seq").astype(F32)

    down_all_grad = reduced(down_all_part)
    q_up_grad = reduced(q_up_part).reshape(-1, HEADS, LANES)[..., : NOPE + ROPE].reshape(-1, HEADS * (NOPE + ROPE))
    kv_up_grad = reduced(kv_up_part)
    out_proj_grad = reduced(out_proj_part)
    gain_parts = [v.reshape(n, -1) for v in (attn_gain_part, mlp_gain_part, q_gain_part, kv_gain_part)]
    gain_sum = reduced(jnp.concatenate(gain_parts, axis=1)).reshape(-1)
    attn_gain_grad, mlp_gain_grad, q_gain_grad, kv_gain_grad = jnp.split(
        gain_sum, [widths[0], widths[0] + widths[1], widths[0] + widths[1] + widths[2]]
    )
    return (
        output,
        grad_input,
        attn_gain_grad,
        down_all_grad[:, :rank_q],
        q_gain_grad,
        q_up_grad,
        down_all_grad[:, rank_q:],
        kv_gain_grad,
        kv_up_grad,
        out_proj_grad,
        mlp_gain_grad,
        gate_up_grad,
        down_grad,
    )


def solution(mesh):
    tokens, matrix, vector = P("fsdp", "seq", None), P("fsdp", None), P("fsdp")
    return jax.shard_map(
        functools.partial(body, mesh.shape["fsdp"]),
        mesh=mesh,
        in_specs=(tokens, matrix, vector, matrix, vector, matrix, matrix, vector, matrix, matrix, vector, matrix, matrix, tokens),
        out_specs=(tokens, tokens, vector, matrix, vector, matrix, matrix, vector, matrix, matrix, vector, matrix, matrix),
        check_vma=False,
    )
```

time: 3190 us -> 2140 us (0.67)
  matrix products: 860 us -> 303 us
  waiting for transfers between devices: 1620 us -> 1170 us
  other arithmetic: 284 us -> 113 us
  Pallas kernels: 0 us -> 128 us
  blocking collectives: 62.1 us -> 182 us
  local copies, waits for them, and re-layouts: 290 us -> 189 us
    dot_general x49 -> x17, matrix products: 860 us -> 303 us  [the longest x12 218 us: dot(): lax.dot_general(a, b, (((ca,), (cb,)), ((), ())), preferred_element_type=...]
    reduce_scatter x6 -> x5, waiting for transfers between devices: 722 us -> 240 us  [the longest x1 178 us: body(): lax.psum_scatter(jnp.concatenate([grad_kv_all, grad_rope_all], axis=1).as...]
    all_to_all x8 -> x1, waiting for transfers between devices: 425 us -> 83.4 us  [body(): lax.all_to_all(hidden_part, 'fsdp', 0, 2, axis_index_groups=same_core)]
    ppermute x0 -> x26, waiting for transfers between devices: none -> 327 us  [swap(): return lax.ppermute(tensor, 'fsdp', [(i, i ^ bit) for i in range(n)])]
    all_to_all x0 -> x1, blocking collectives: none -> 135 us  [body(): hidden = lax.all_to_all(hidden, 'fsdp', 2, 0, axis_index_groups=same_core)]
    pallas_call x0 -> x2, Pallas kernels: none -> 128 us  [the longest x1 69.8 us: attend_backward(): pl.pallas_call(functools.partial(bwd_kernel, full_rows=full_rows, mask_ro...]
    convert_element_type x22 -> x16, other arithmetic: 168 us -> 45.2 us  [the longest x1 15.4 us: keep_half(): return (mine.astype(F32) + swap(other, 1, n).astype(F32)).astype(BF16)]
    unnamed x158 -> x126, local copies, waits for them, and re-layouts: 120 us -> 36.9 us
  transfers between devices with their start and end apart: 23 -> 40, of which waited for: 14 -> 20; matrix products, arithmetic and copies ran while one was open for 22% -> 21% of each run, Pallas kernels for 0% -> 3%
where the time goes in v1:
time: 2140 us; the launch traced here: 2130 us
  waiting for transfers between devices  1170 us (55%)
  matrix products  303 us (14%)
  local copies, waits for them, and re-layouts  189 us (9%)
  blocking collectives  182 us (9%)
  Pallas kernels  128 us (6%)
  other arithmetic  113 us (5%)
  starting transfers between devices  28.4 us (1%)
    psum x1, waiting for transfers between devices, reduced(): return lax.psum(share, 'seq').astype(F32)  489 us
    ppermute x26, waiting for transfers between devices, swap(): return lax.ppermute(tensor, 'fsdp', [(i, i ^ bit) for i in range(n)])  327 us
    dot_general x12, matrix products, dot(): lax.dot_general(a, b, (((ca,), (cb,)), ((), ())), preferred_element_type=...  218 us
    reduce_scatter x1, waiting for transfers between devices, body(): lax.psum_scatter(jnp.concatenate([grad_kv_all, grad_rope_all], axis=1).as...  178 us
    all_to_all x1, blocking collectives, body(): hidden = lax.all_to_all(hidden, 'fsdp', 2, 0, axis_index_groups=same_core)  135 us
    all_to_all x1, waiting for transfers between devices, body(): lax.all_to_all(hidden_part, 'fsdp', 0, 2, axis_index_groups=same_core)  83.4 us
    pallas_call x1, Pallas kernels, attend_backward(): pl.pallas_call(functools.partial(bwd_kernel, full_rows=full_rows, mask_ro...  69.8 us
    reduce_scatter x4, waiting for transfers between devices, reduced(): lax.psum_scatter(part.astype(BF16), 'fsdp', scatter_dimension=0, tiled=True)  61.6 us
  transfers between devices with their start and end apart: 40, of which 20 were waited for; matrix products, arithmetic and copies ran while one was open for 21% of the time, Pallas kernels for 3%

profile of v1, /device:TPU:0, one launch (start us, length us, event | category | flops | bytes accessed | tf_op | source)
XLA Modules:
  0.0 2133.9 jit_solution(1579167363528814940)
XLA Ops:
  27.7 29.4 %all-gather.11.cloned.1.call-done = bf16[2560,1056]{1,0:T(8,128)(2,1)} async-done(((bf16[320,1056]{1,0:T(8,128)(2,1)}), bf16[2560,1056]{1,0:T(8,128)(2,1)}) %all-gather.11.cloned.1.call-update) | async-done | bytes 5406736 | tf_op jit(solution)/shard_map/all_gather | solution.py:354
  98.5 134.5 %all_to_all.30 = bf16[1,320,2,4,1600]{4,1,2,0,3:T(8,128)(2,1)} all-to-all(bf16[1,320,2,4,1600]{4,1,2,0,3:T(8,128)(2,1)} %copy.126), channel_id=1, replica_groups={{0,8,16,24},{4,12,20,28},{1,9,17,25},{5,13,21,29},{2,10,18,26},{6,14,22..., dimensions={3} | all-to-all | bytes 16384000 | tf_op jit(solution)/shard_map/all_to_all | solution.py:382
  248.7 32.7 %collective-permute-done.12 = bf16[256,2560]{1,0:T(8,128)(2,1)} collective-permute-done((bf16[256,2560]{1,0:T(8,128)(2,1)S(1)}, bf16[256,2560]{1,0:T(8,128)(2,1)}, u32[]{:S(2)}, u32[]{:S(2)}) %collective-permute-start.12) | collective-permute-done | bytes 1310752 | tf_op jit(solution)/shard_map/ppermute | solution.py:266
  284.3 45.3 %collective-permute-done.15 = bf16[256,2560]{1,0:T(8,128)(2,1)} collective-permute-done((bf16[256,2560]{1,0:T(8,128)(2,1)}, bf16[256,2560]{1,0:T(8,128)(2,1)}, u32[]{:S(2)}, u32[]{:S(2)}) %collective-permute-start.15) | collective-permute-done | bytes 1310752 | tf_op jit(solution)/shard_map/ppermute | solution.py:266
  335.2 44.2 %collective-permute-done.16 = bf16[256,2560]{1,0:T(8,128)(2,1)S(1)} collective-permute-done((bf16[256,2560]{1,0:T(8,128)(2,1)}, bf16[256,2560]{1,0:T(8,128)(2,1)S(1)}, u32[]{:S(2)}, u32[]{:S(2)}) %collective-permute-start.16) | collective-permute-done | bytes 1310752 | tf_op jit(solution)/shard_map/ppermute | solution.py:266
  390.4 58.6 %attend_forward.1 = (bf16[512,2560]{1,0:T(8,128)(2,1)S(1)}, bf16[512,5120]{1,0:T(8,128)(2,1)}, f32[160,512]{1,0:T(8,128)S(1)}) custom-call(s32[4]{0:T(128)S(1)} %pad_add_fusion.bounds, bf16[512,768]{1,0:T(8,128)(2,1)S(1)} %multiply_convert_fusion.5.qlat, bf16[768,5120]{1,0:T(8,128)(2,1)} %all-gather.13.cloned.1.call-done.qup, ...), custom_call_target="tpu_custom_call" | custom-call | flops 16106127360 | bytes 31457280 | tf_op jit(solution)/shard_map/attend_forward/pallas_call | solution.py:74
  502.7 28.2 %collective-permute-done.3 = bf16[256,2560]{1,0:T(8,128)(2,1)} collective-permute-done((bf16[256,2560]{1,0:T(8,128)(2,1)}, bf16[256,2560]{1,0:T(8,128)(2,1)}, u32[]{:S(2)}, u32[]{:S(2)}) %collective-permute-start.3) | collective-permute-done | bytes 1310752 | tf_op jit(solution)/shard_map/ppermute | solution.py:266
  580.3 23.8 %fusion.55 = f32[2048,1600]{0,1:T(8,128)} fusion(bf16[2048,2560]{1,0:T(8,128)(2,1)} %constant_dynamic-update-slice_fusion, bf16[2560,1600]{1,0:T(8,128)(2,1)} %bitcast.118), kind=kOutput, calls=%fused_computation.165 | convolution fusion | flops 16777216000 | bytes 31784960 | tf_op jit(solution)/shard_map/dot_general | solution.py:393
  604.1 32.6 %multiply_convert_fusion = (bf16[2048,1600]{0,1:T(8,128)(2,1)}, bf16[2048,1600]{0,1:T(8,128)(2,1)}, bf16[2048,1600]{0,1:T(8,128)(2,1)}) fusion(f32[2048,1600]{0,1:T(8,128)} %fusion.54, f32[2048,1600]{0,1:T(8,128)} %fusion.55, bf16[2048,2560]{1,0:T(8,128)(2,1)} %constant_dynamic-update-slice_fusion.7, bf16[1600,2560]{1,0:T(8,128)(2,1)} %all-gather.21.cloned.1.call-done), kind=kOutput, calls=%fused_computation.8 | convolution fusion | flops 16826368000 | bytes 64552960 | tf_op jit(solution)/shard_map/dot_general | solution.py:21
  636.7 25.7 %fusion.56 = f32[2048,2560]{1,0:T(8,128)} fusion(bf16[2048,1600]{0,1:T(8,128)(2,1)} %get-tuple-element.143, bf16[2560,1600]{1,0:T(8,128)(2,1)} %bitcast.116), kind=kOutput, calls=%fused_computation.166 | convolution fusion | flops 16777216000 | bytes 35717120 | tf_op jit(solution)/shard_map/dot_general | solution.py:21
  662.4 27.1 %add_convert_fusion = bf16[2048,2560]{1,0:T(8,128)(2,1)} fusion(f32[2048,2560]{1,0:T(8,128)} %fusion.56, bf16[2048,1600]{0,1:T(8,128)(2,1)} %get-tuple-element.142, bf16[2560,1600]{1,0:T(8,128)(2,1)} %bitcast.119), kind=kOutput, calls=%fused_computation | convolution fusion | flops 16787701760 | bytes 46202880 | tf_op jit(solution)/shard_map/dot_general | solution.py:21
  729.2 24.3 %collective-permute-done.7 = bf16[256,2560]{1,0:T(8,128)(2,1)S(1)} collective-permute-done((bf16[256,2560]{1,0:T(8,128)(2,1)S(1)}, bf16[256,2560]{1,0:T(8,128)(2,1)S(1)}, u32[]{:S(2)}, u32[]{:S(2)}) %collective-permute-start.7) | collective-permute-done | bytes 1310752 | tf_op jit(solution)/shard_map/ppermute | solution.py:266
  755.5 26.1 %collective-permute-done.18 = bf16[256,2560]{1,0:T(8,128)(2,1)S(1)} collective-permute-done((bf16[256,2560]{1,0:T(8,128)(2,1)S(1)}, bf16[256,2560]{1,0:T(8,128)(2,1)S(1)}, u32[]{:S(2)}, u32[]{:S(2)}) %collective-permute-start.18) | collective-permute-done | bytes 1310752 | tf_op jit(solution)/shard_map/ppermute | solution.py:266
  809.8 26.8 %collective-permute-done.8 = bf16[256,2560]{1,0:T(8,128)(2,1)} collective-permute-done((bf16[256,2560]{1,0:T(8,128)(2,1)}, bf16[256,2560]{1,0:T(8,128)(2,1)}, u32[]{:S(2)}, u32[]{:S(2)}) %collective-permute-start.8) | collective-permute-done | bytes 1310752 | tf_op jit(solution)/shard_map/ppermute | solution.py:266
  842.6 22.0 %collective-permute-done.21 = bf16[256,2560]{1,0:T(8,128)(2,1)} collective-permute-done((bf16[256,2560]{1,0:T(8,128)(2,1)}, bf16[256,2560]{1,0:T(8,128)(2,1)}, u32[]{:S(2)}, u32[]{:S(2)}) %collective-permute-start.21) | collective-permute-done | bytes 1310752 | tf_op jit(solution)/shard_map/ppermute | solution.py:266
  910.5 69.8 %attend_backward.1 = (bf16[512,5120]{1,0:T(8,128)(2,1)}, f32[256,5120]{1,0:T(8,128)}, f32[2048,256]{1,0:T(8,128)}, f32[2048,128]{1,0:T(8,128)S(1)}) custom-call(s32[4]{0:T(128)S(1)} %pad_add_fusion.bounds, bf16[512,5120]{1,0:T(8,128)(2,1)} %get-tuple-element.21.q, bf16[2048,256]{1,0:T(8,128)(2,1)S(1)} %get-tuple-element.170.kvn, ...), custom_call_target="tpu_custom_call" | custom-call | flops 40265318400 | bytes 41943040 | tf_op jit(solution)/shard_map/attend_backward/pallas_call | solution.py:171
  1007.4 178.2 %reduce-scatter.6.cloned.1.call-done = bf16[512,384]{1,0:T(8,128)(2,1)} async-done(((bf16[2048,384]{1,0:T(8,128)(2,1)}), bf16[512,384]{1,0:T(8,128)(2,1)}) %reduce-scatter.6.cloned.1.call-update) | async-done | bytes 393232 | tf_op jit(solution)/shard_map/reduce_scatter | solution.py:433
  1201.9 24.1 %convolution_convert_fusion.2 = bf16[2560,1600]{0,1:T(8,128)(2,1)} fusion(bf16[2048,1600]{0,1:T(8,128)(2,1)} %get-tuple-element.143, bf16[2048,2560]{1,0:T(8,128)(2,1)} %constant_dynamic-update-slice_fusion), kind=kOutput, calls=%fused_computation.14 | convolution fusion | flops 16781312000 | bytes 25231360 | tf_op jit(solution)/shard_map/dot_general | solution.py:21
  1238.0 23.4 %convolution_convert_fusion.1 = bf16[2560,1600]{0,1:T(8,128)(2,1)} fusion(bf16[2048,1600]{0,1:T(8,128)(2,1)} %get-tuple-element.142, bf16[2048,2560]{1,0:T(8,128)(2,1)} %constant_dynamic-update-slice_fusion), kind=kOutput, calls=%fused_computation.13 | convolution fusion | flops 16781312000 | bytes 25231360 | tf_op jit(solution)/shard_map/dot_general | solution.py:21
  1340.5 21.7 %convolution_convert_fusion.3 = bf16[1600,2560]{1,0:T(8,128)(2,1)S(1)} fusion(bf16[2048,1600]{0,1:T(8,128)(2,1)} %get-tuple-element.144, bf16[2048,2560]{1,0:T(8,128)(2,1)} %constant_dynamic-update-slice_fusion.7), kind=kOutput, calls=%fused_computation.15 | convolution fusion | flops 16781312000 | bytes 25231360 | tf_op jit(solution)/shard_map/dot_general | solution.py:21
  1372.6 83.4 %all-to-all-done.1 = bf16[4,320,2,1,1600]{4,1,2,3,0:T(8,128)(2,1)} async-done(((bf16[4,320,2,1,1600]{4,1,2,3,0:T(8,128)(2,1)}), bf16[4,320,2,1,1600]{4,1,2,3,0:T(8,128)(2,1)}, u32[]{:S(2)}, u32[]{:S(2)}) %all-to-all-start.1) | async-done | bytes 8192032 | tf_op jit(solution)/shard_map/all_to_all | solution.py:419
  1492.6 61.6 %reduce-scatter.14.cloned.1.call-done = bf16[320,2560]{1,0:T(8,128)(2,1)} async-done(((bf16[2560,2560]{1,0:T(8,128)(2,1)}), bf16[320,2560]{1,0:T(8,128)(2,1)}) %reduce-scatter.14.cloned.1.call-update) | async-done | bytes 1638416 | tf_op jit(solution)/shard_map/reduce_scatter | solution.py:445
  1565.9 24.3 %all-reduce.2 = bf16[8,768]{1,0:T(8,128)(2,1)S(1)} all-reduce(bf16[8,768]{1,0:T(8,128)(2,1)S(1)} %pad_maximum_fusion.4), channel_id=5, replica_groups=mesh['fsdp'=8,'seq'=4] {'fsdp'}, use_global_device_ids=true, to_apply=%region_13.14.clone | all-reduce | flops 6144 | bytes 24576
  1611.8 488.8 %all-reduce.6.cloned.1.call-done = (bf16[320,1056]{1,0:T(8,128)(2,1)}, bf16[96,40,128]{2,1,0:T(8,128)(2,1)}, bf16[32,5120]{1,0:T(8,128)(2,1)}, bf16[320,2560]{1,...) async-done(((bf16[320,1056]{1,0:T(8,128)(2,1)}, bf16[96,40,128]{2,1,0:T(8,128)(2,1)}, bf16[32,5120]{1,0:T(8,128)(2,1)}, bf16[320,2560]{1,0:T(8,128)(2,1)}, ...) | async-done | bytes 15912976 | tf_op jit(solution)/shard_map/psum | solution.py:446
  (330 shorter events, 557.6 us)
Async XLA Ops:
  10.3 373.7 %all-gather.15.cloned.1.call-start = ((), (), s32[]{:S(2)}) async-start(), calls=%async_computation.9 | async-start | bytes 1966080 | tf_op jit(solution)/shard_map/all_gather | solution.py:370
  67.0 321.2 %all-gather.17.cloned.1.call-start = ((), (), s32[]{:S(2)}) async-start(), calls=%async_computation.10 | async-start | bytes 2949120 | tf_op jit(solution)/shard_map/all_gather | solution.py:357
  67.7 320.4 %all-gather.13.cloned.1.call-start = ((), (), s32[]{:S(2)}) async-start(), calls=%async_computation.8 | async-start | bytes 8847360 | tf_op jit(solution)/shard_map/all_gather | solution.py:356
  71.7 379.5 %all-gather.19.cloned.1.call-start = ((), (), s32[]{:S(2)}) async-start(), calls=%async_computation.11 | async-start | bytes 14745600 | tf_op jit(solution)/shard_map/all_gather | solution.py:358
  72.3 401.3 %all-gather.23.cloned.1.call-start = ((), (), s32[]{:S(2)}) async-start(), calls=%async_computation.18 | async-start | bytes 25559040 | tf_op jit(solution)/shard_map/all_gather | solution.py:383
  233.0 371.1 %all-gather.21.cloned.1.call-start = ((), (), s32[]{:S(2)}) async-start(), calls=%async_computation.12 | async-start | bytes 12288000 | tf_op jit(solution)/shard_map/all_gather | solution.py:386
  237.9 94.5 %collective-permute-start.14 = (bf16[256,2560]{1,0:T(8,128)(2,1)S(1)}, bf16[256,2560]{1,0:T(8,128)(2,1)}, u32[]{:S(2)}, u32[]{:S(2)}) collective-permute-start(bf16[256,2560]{1,0:T(8,128)(2,1)S(1)} %get-tuple-element.164), channel_id=1, source_target_pairs={{0,16},{4,20},{8,24},{12,28},{16,0},{20,4},{24,8},{28,12},{1,17},{... | collective-permute-start | bytes 3932168 | tf_op jit(solution)/shard_map/ppermute | solution.py:266
  237.9 93.1 %collective-permute-start.13 = (bf16[256,2560]{1,0:T(8,128)(2,1)}, bf16[256,2560]{1,0:T(8,128)(2,1)}, u32[]{:S(2)}, u32[]{:S(2)}) collective-permute-start(bf16[256,2560]{1,0:T(8,128)(2,1)} %get-tuple-element.163), channel_id=1, source_target_pairs={{0,8},{4,12},{8,0},{12,4},{16,24},{20,28},{24,16},{28,20},{1,9},{5... | collective-permute-start | bytes 3932168 | tf_op jit(solution)/shard_map/ppermute | solution.py:266
  239.9 89.7 %collective-permute-start.15 = (bf16[256,2560]{1,0:T(8,128)(2,1)}, bf16[256,2560]{1,0:T(8,128)(2,1)}, u32[]{:S(2)}, u32[]{:S(2)}) collective-permute-start(bf16[256,2560]{1,0:T(8,128)(2,1)} %get-tuple-element.163), channel_id=1, source_target_pairs={{0,16},{4,20},{8,24},{12,28},{16,0},{20,4},{24,8},{28,12},{1,17},{... | collective-permute-start | bytes 3932168 | tf_op jit(solution)/shard_map/ppermute | solution.py:266
  240.5 945.1 %reduce-scatter.6.cloned.1.call-start = ((), (), s32[]{:S(2)}) async-start(), calls=%async_computation.13 | async-start | bytes 1966080 | tf_op jit(solution)/shard_map/reduce_scatter | solution.py:433
  281.4 98.0 %collective-permute-start.16 = (bf16[256,2560]{1,0:T(8,128)(2,1)}, bf16[256,2560]{1,0:T(8,128)(2,1)S(1)}, u32[]{:S(2)}, u32[]{:S(2)}) collective-permute-start(bf16[256,2560]{1,0:T(8,128)(2,1)} %collective-permute-done.12), channel_id=1, source_target_pairs={{0,16},{4,20},{8,24},{12,28},{16,0},{20,4},{24,8},{28,12},{1,17},{... | collective-permute-start | bytes 3932168 | tf_op jit(solution)/shard_map/ppermute | solution.py:266
  329.6 139.0 %collective-permute-start.17 = (bf16[256,2560]{1,0:T(8,128)(2,1)}, bf16[256,2560]{1,0:T(8,128)(2,1)}, u32[]{:S(2)}, u32[]{:S(2)}) collective-permute-start(bf16[256,2560]{1,0:T(8,128)(2,1)} %collective-permute-done.15), channel_id=1, source_target_pairs={{0,8},{4,12},{8,0},{12,4},{16,24},{20,28},{24,16},{28,20},{1,9},{5... | collective-permute-start | bytes 3932168 | tf_op jit(solution)/shard_map/ppermute | solution.py:266
  471.0 63.0 %collective-permute-start.2 = (bf16[256,2560]{1,0:T(8,128)(2,1)S(1)}, bf16[256,2560]{1,0:T(8,128)(2,1)}, u32[]{:S(2)}, u32[]{:S(2)}) collective-permute-start(bf16[256,2560]{1,0:T(8,128)(2,1)S(1)} %get-tuple-element.166), channel_id=1, source_target_pairs={{0,16},{4,20},{8,24},{12,28},{16,0},{20,4},{24,8},{28,12},{1,17},{... | collective-permute-start | bytes 3932168 | tf_op jit(solution)/shard_map/ppermute | solution.py:266
  719.2 62.3 %collective-permute-start.18 = (bf16[256,2560]{1,0:T(8,128)(2,1)S(1)}, bf16[256,2560]{1,0:T(8,128)(2,1)S(1)}, u32[]{:S(2)}, u32[]{:S(2)}) collective-permute-start(bf16[256,2560]{1,0:T(8,128)(2,1)S(1)} %get-tuple-element.151), channel_id=1, source_target_pairs={{0,16},{4,20},{8,24},{12,28},{16,0},{20,4},{24,8},{28,12},{1,17},{... | collective-permute-start | bytes 3932168 | tf_op jit(solution)/shard_map/ppermute | solution.py:266
  727.8 80.7 %collective-permute-start.10 = (bf16[256,2560]{1,0:T(8,128)(2,1)}, bf16[256,2560]{1,0:T(8,128)(2,1)}, u32[]{:S(2)}, u32[]{:S(2)}) collective-permute-start(bf16[256,2560]{1,0:T(8,128)(2,1)} %get-tuple-element.158), channel_id=1, source_target_pairs={{0,8},{4,12},{8,0},{12,4},{16,24},{20,28},{24,16},{28,20},{1,9},{5... | collective-permute-start | bytes 3932168 | tf_op jit(solution)/shard_map/ppermute | solution.py:266
  782.2 82.4 %collective-permute-start.21 = (bf16[256,2560]{1,0:T(8,128)(2,1)}, bf16[256,2560]{1,0:T(8,128)(2,1)}, u32[]{:S(2)}, u32[]{:S(2)}) collective-permute-start(bf16[256,2560]{1,0:T(8,128)(2,1)} %get-tuple-element.153), channel_id=1, source_target_pairs={{0,8},{4,12},{8,0},{12,4},{16,24},{20,28},{24,16},{28,20},{1,9},{5... | collective-permute-start | bytes 3932168 | tf_op jit(solution)/shard_map/ppermute | solution.py:266
  788.1 76.6 %collective-permute-start.23 = (bf16[256,2560]{1,0:T(8,128)(2,1)}, bf16[256,2560]{1,0:T(8,128)(2,1)}, u32[]{:S(2)}, u32[]{:S(2)}) collective-permute-start(bf16[256,2560]{1,0:T(8,128)(2,1)} %get-tuple-element.150), channel_id=1, source_target_pairs={{0,16},{4,20},{8,24},{12,28},{16,0},{20,4},{24,8},{28,12},{1,17},{... | collective-permute-start | bytes 3932168 | tf_op jit(solution)/shard_map/ppermute | solution.py:266
  808.4 80.3 %collective-permute-start.9 = (bf16[256,2560]{1,0:T(8,128)(2,1)}, bf16[256,2560]{1,0:T(8,128)(2,1)S(1)}, u32[]{:S(2)}, u32[]{:S(2)}) collective-permute-start(bf16[256,2560]{1,0:T(8,128)(2,1)} %get-tuple-element.159), channel_id=1, source_target_pairs={{0,8},{4,12},{8,0},{12,4},{16,24},{20,28},{24,16},{28,20},{1,9},{5... | collective-permute-start | bytes 3932168 | tf_op jit(solution)/shard_map/ppermute | solution.py:266
  983.5 506.8 %reduce-scatter.10.cloned.1.call-start = ((), (), s32[]{:S(2)}) async-start(), calls=%async_computation.15 | async-start | bytes 8847360 | tf_op jit(solution)/shard_map/reduce_scatter | solution.py:445
  992.9 499.7 %reduce-scatter.12.cloned.1.call-start = ((), (), s32[]{:S(2)}) async-start(), calls=%async_computation.16 | async-start | bytes 2949120 | tf_op jit(solution)/shard_map/reduce_scatter | solution.py:445
  997.5 495.1 %reduce-scatter.8.cloned.1.call-start = ((), (), s32[]{:S(2)}) async-start(), calls=%async_computation.14 | async-start | bytes 6635520 | tf_op jit(solution)/shard_map/reduce_scatter | solution.py:445
  1201.8 352.4 %reduce-scatter.14.cloned.1.call-start = ((), (), s32[]{:S(2)}) async-start(), calls=%async_computation.17 | async-start | bytes 14745600 | tf_op jit(solution)/shard_map/reduce_scatter | solution.py:445
  1334.7 121.3 %all-to-all-start.1 = ((bf16[4,320,2,1,1600]{4,1,2,3,0:T(8,128)(2,1)}), bf16[4,320,2,1,1600]{4,1,2,3,0:T(8,128)(2,1)}, u32[]{:S(2)}, u32[]{:S(2)}) async-start(bf16[4,320,2,1,1600]{4,1,2,3,0:T(8,128)(2,1)} %fusion.2), calls=%async_computation.6 | async-start | bytes 17039360 | tf_op jit(solution)/shard_map/all_to_all | solution.py:419
  1340.5 760.2 %all-reduce.6.cloned.1.call-start = ((), (), s32[]{:S(2)}) async-start(), calls=%async_computation.19 | async-start | bytes 31948800 | tf_op jit(solution)/shard_map/psum | solution.py:446
  (70 other events, 3115.6 us)
Sparse Core Ops, SparseCore 0:
  10.5 46.5 all-gather.10
  67.1 37.0 all-gather.14
  106.1 50.4 all-gather.16
  158.9 89.5 all-gather.12
  250.2 127.3 all-gather.18
  379.0 31.8 all-gather.22
  412.5 20.7 all-gather.20
  983.6 201.9 reduce-scatter.5
  1189.0 68.3 reduce-scatter.9
  1261.6 43.6 reduce-scatter.11
  1309.2 134.0 reduce-scatter.7
  1447.7 106.3 reduce-scatter.13
  1558.9 541.6 all-reduce.5

commit v2 on v1

v2 whole, which is shorter than its diff:
```python
import functools, math
import jax
import jax.numpy as jnp
from jax import lax
from jax.experimental import pallas as pl
from jax.experimental.pallas import tpu as pltpu
from jax.sharding import PartitionSpec as P

HEADS = 40
NOPE = 64
ROPE = 32
PROMPT = 1024
LANES = 128
NEG = -1e30
SCALE = (NOPE + ROPE) ** -0.5
LOG2E = math.log2(math.e)
LN2 = math.log(2.0)


LIGHT = pl.CostEstimate(flops=1 << 20, bytes_accessed=1 << 16, transcendentals=0)


def dot(a, b, ca, cb):
    return lax.dot_general(a, b, (((ca,), (cb,)), ((), ())), preferred_element_type=jnp.float32)


def flat(ref):
    return ref[...].reshape(-1, ref.shape[-1])


def fwd_kernel(bounds, qlat, qup_ref, kvn, kvup_ref, krope, cos, sin_r, sin_l, start, *rest, full_rows, mask_rows):
    out, q_out, lse_out, m_scr, acc_scr = rest[-5:]
    rows = qlat.shape[0]
    lane = lax.broadcasted_iota(jnp.int32, (1, LANES), 1)
    low_half = lane < NOPE
    raw = dot(qlat[...], flat(qup_ref), 1, 0)
    kvup = flat(kvup_ref)
    for h in range(2):
        u = raw[:, h * LANES:(h + 1) * LANES]
        turned = u * cos[...] + pltpu.roll(u, 16, 1) * sin_r[...] + pltpu.roll(u, LANES - 16, 1) * sin_l[...]
        q_out[:, h * LANES:(h + 1) * LANES] = turned.astype(jnp.bfloat16)
    m_scr[...] = jnp.full_like(m_scr, NEG)
    acc_scr[...] = jnp.zeros_like(acc_scr)

    def block(first, size, masked):
        span = pl.ds(first, size)
        kv = dot(kvn[span, :], kvup, 1, 0).astype(jnp.bfloat16)
        rope_rows = krope[span, :]
        if masked:
            key_index = first + lax.broadcasted_iota(jnp.int32, (size, rows), 0)
            own = bounds[3] + lax.broadcasted_iota(jnp.int32, (size, rows), 1)
            allowed = (key_index <= own) & ((key_index >= start[...]) | (key_index < PROMPT))
        for h in range(2):
            kv_h = kv[:, h * LANES:(h + 1) * LANES]
            key = jnp.where(low_half, kv_h, rope_rows)
            val = jnp.where(low_half, jnp.ones_like(kv_h), kv_h)
            s = dot(key, q_out[:, h * LANES:(h + 1) * LANES], 1, 1)
            if masked:
                s = jnp.where(allowed, s, NEG)
            m_old = m_scr[h:h + 1, :]
            m_new = jnp.maximum(m_old, jnp.max(s, axis=0, keepdims=True))
            p = jnp.exp2(s - m_new)
            m_scr[h:h + 1, :] = m_new
            acc_scr[h] = acc_scr[h] * jnp.exp2(m_old - m_new) + dot(val, p.astype(jnp.bfloat16), 0, 0)

    lax.fori_loop(0, bounds[0], lambda i, c: (block(pl.multiple_of(i * full_rows, full_rows), full_rows, False), c)[1], 0)
    lax.fori_loop(bounds[1], bounds[2], lambda i, c: (block(pl.multiple_of(i * mask_rows, mask_rows), mask_rows, True), c)[1], 0)
    parts = []
    for h in range(2):
        total = acc_scr[h, 0:1, :]
        parts.append(acc_scr[h, NOPE:, :] / total)
        lse_out[h:h + 1, :] = m_scr[h:h + 1, :] + jnp.log2(total)
    out[...] = jnp.concatenate(parts, axis=0).T.astype(jnp.bfloat16)


def attend_forward(part, prev, deps, bounds, qlat, up, kvn, krope, cos, sin_r, sin_l, start, full_rows, mask_rows):
    rows, rank = qlat.shape
    q_rows, kv_rows = rank // up.shape[0], kvn.shape[1] // up.shape[0]
    whole = lambda *_: (0, 0)
    first_pair, pairs = part
    col = lambda i, b: (0, i + first_pair)
    return pl.pallas_call(
        functools.partial(fwd_kernel, full_rows=full_rows, mask_rows=mask_rows),
        grid_spec=pltpu.PrefetchScalarGridSpec(
            num_scalar_prefetch=1,
            grid=(pairs,),
            in_specs=[
                pl.BlockSpec((rows, rank), whole),
                pl.BlockSpec((up.shape[0], q_rows, 2 * LANES), lambda i, b: (0, 0, i + first_pair)),
                pl.BlockSpec(kvn.shape, whole),
                pl.BlockSpec((up.shape[0], kv_rows, 2 * LANES), lambda i, b: (0, q_rows // kv_rows, i + first_pair)),
                pl.BlockSpec(krope.shape, whole),
                pl.BlockSpec(cos.shape, whole),
                pl.BlockSpec(cos.shape, whole),
                pl.BlockSpec(cos.shape, whole),
                pl.BlockSpec((1, rows), whole),
            ] + [pl.BlockSpec(memory_space=pl.ANY)] * (len(prev) + len(deps)),
            out_specs=[
                pl.BlockSpec((rows, LANES), col),
                pl.BlockSpec((rows, 2 * LANES), col),
                pl.BlockSpec((8, rows), lambda i, b: (i + first_pair, 0)),
            ],
            scratch_shapes=[pltpu.VMEM((8, rows), jnp.float32), pltpu.VMEM((2, LANES, rows), jnp.float32)],
        ),
        out_shape=[
            jax.ShapeDtypeStruct((rows, HEADS * NOPE), jnp.bfloat16),
            jax.ShapeDtypeStruct((rows, HEADS * LANES), jnp.bfloat16),
            jax.ShapeDtypeStruct((HEADS // 2 * 8, rows), jnp.float32),
        ],
        compiler_params=pltpu.CompilerParams(vmem_limit_bytes=48 << 20),
        cost_estimate=LIGHT,
        input_output_aliases={10 + i: i for i in range(len(prev))},
        name="attend_forward",
    )(bounds, qlat, up, kvn, up, krope, cos, sin_r, sin_l, start, *prev, *deps)


def bwd_kernel(bounds, qlat_t, qup_ref, q, kvn, kvn_t, kvup_ref, krope, grad_out, out, lse, cos, sin_r, sin_l, start, *rest, full_rows, mask_rows, resumes):
    dqup_out, dkvup_out, dkvn, drope, dqlat, go_scr, dq_scr, delta_scr, dkvup = rest[-9:]
    kvup = flat(kvup_ref)
    rows = q.shape[0]
    lane = lax.broadcasted_iota(jnp.int32, (1, LANES), 1)
    low_half = lane < NOPE

    @pl.when(pl.program_id(0) == 0)
    def _():
        dkvn[...] = rest[-12][...] if resumes else jnp.zeros_like(dkvn)
        drope[...] = rest[-11][...] if resumes else jnp.zeros_like(drope)
        dqlat[...] = rest[-10][...] if resumes else jnp.zeros_like(dqlat)

    go = grad_out[...].astype(jnp.float32)
    prod_t = (go * out[...].astype(jnp.float32)).T
    delta_scr[0:1, :] = jnp.sum(prod_t[:NOPE], axis=0, keepdims=True)
    delta_scr[1:2, :] = jnp.sum(prod_t[NOPE:], axis=0, keepdims=True)
    zero = jnp.zeros_like(go)
    go_scr[0] = jnp.where(low_half, zero, pltpu.roll(go, NOPE, 1)).astype(jnp.bfloat16)
    go_scr[1] = jnp.where(low_half, zero, go).astype(jnp.bfloat16)
    dq_scr[...] = jnp.zeros_like(dq_scr)
    dkvup[...] = jnp.zeros_like(dkvup)

    def block(first, size, masked):
        span = pl.ds(first, size)
        kv = dot(kvn[span, :], kvup, 1, 0).astype(jnp.bfloat16)
        rope_rows = krope[span, :]
        if masked:
            key_index = first + lax.broadcasted_iota(jnp.int32, (size, rows), 0)
            own = bounds[3] + lax.broadcasted_iota(jnp.int32, (size, rows), 1)
            allowed = (key_index <= own) & ((key_index >= start[...]) | (key_index < PROMPT))
        pieces = []
        rope_sum = None
        for h in range(2):
            kv_h = kv[:, h * LANES:(h + 1) * LANES]
            q_h = q[:, h * LANES:(h + 1) * LANES]
            key = jnp.where(low_half, kv_h, rope_rows)
            p = jnp.exp2(dot(key, q_h, 1, 1) - lse[h:h + 1, :])
            if masked:
                p = jnp.where(allowed, p, 0.0)
            ds = (p * (dot(kv_h, go_scr[h], 1, 1) - delta_scr[h:h + 1, :])).astype(jnp.bfloat16)
            dk = dot(ds, q_h, 1, 0) * LN2
            dv = dot(p.astype(jnp.bfloat16), go_scr[h], 1, 0)
            dq_scr[h] += dot(key, ds, 0, 0)
            pieces.append(jnp.where(low_half, dk, dv).astype(jnp.bfloat16))
            rope_sum = dk if rope_sum is None else rope_sum + dk
        dkv = jnp.concatenate(pieces, axis=1)
        drope[span, :] += rope_sum
        dkvn[span, :] += dot(dkv, kvup, 1, 1)
        dkvup[...] += dot(kvn_t[:, span], dkv, 1, 0)

    lax.fori_loop(0, bounds[0], lambda i, c: (block(pl.multiple_of(i * full_rows, full_rows), full_rows, False), c)[1], 0)
    lax.fori_loop(bounds[1], bounds[2], lambda i, c: (block(pl.multiple_of(i * mask_rows, mask_rows), mask_rows, True), c)[1], 0)
    turned = []
    for h in range(2):
        u = dq_scr[h].T * SCALE
        turned.append(u * cos[...] - pltpu.roll(u, 16, 1) * sin_r[...] - pltpu.roll(u, LANES - 16, 1) * sin_l[...])
    dq = jnp.concatenate(turned, axis=1).astype(jnp.bfloat16)
    dqlat[...] += dot(dq, flat(qup_ref), 1, 1)
    dqup_out[...] = dot(qlat_t[...], dq, 1, 0).astype(jnp.bfloat16).reshape(dqup_out.shape)
    dkvup_out[...] = dkvup[...].astype(jnp.bfloat16).reshape(dkvup_out.shape)


def attend_backward(part, prev, deps, bounds, qlat_t, up, q, kvn, kvn_t, krope, grad_out, out, lse, cos, sin_r, sin_l, start, full_rows, mask_rows):
    rows = q.shape[0]
    keys, rank = kvn.shape
    devices = up.shape[0]
    q_rows, kv_rows = qlat_t.shape[0] // devices, rank // devices
    up_block = lambda i, b: (0, 0, i + first_pair)
    whole = lambda *_: (0, 0)
    first_pair, pairs = part
    col = lambda i, b: (0, i + first_pair)
    return pl.pallas_call(
        functools.partial(bwd_kernel, full_rows=full_rows, mask_rows=mask_rows, resumes=bool(prev)),
        grid_spec=pltpu.PrefetchScalarGridSpec(
            num_scalar_prefetch=1,
            grid=(pairs,),
            in_specs=[
                pl.BlockSpec(qlat_t.shape, whole),
                pl.BlockSpec((devices, q_rows, 2 * LANES), up_block),
                pl.BlockSpec((rows, 2 * LANES), col),
                pl.BlockSpec(kvn.shape, whole),
                pl.BlockSpec(kvn_t.shape, whole),
                pl.BlockSpec((devices, kv_rows, 2 * LANES), lambda i, b: (0, q_rows // kv_rows, i + first_pair)),
                pl.BlockSpec(krope.shape, whole),
                pl.BlockSpec((rows, LANES), col),
                pl.BlockSpec((rows, LANES), col),
                pl.BlockSpec((8, rows), lambda i, b: (i + first_pair, 0)),
                pl.BlockSpec(cos.shape, whole),
                pl.BlockSpec(cos.shape, whole),
                pl.BlockSpec(cos.shape, whole),
                pl.BlockSpec((1, rows), whole),
            ] + [pl.BlockSpec(memory_space=pl.ANY)] * (len(prev[:2]) + len(deps)) + [pl.BlockSpec(v.shape, whole) for v in prev[2:]],
            out_specs=[
                pl.BlockSpec((devices, q_rows, 2 * LANES), up_block),
                pl.BlockSpec((devices, kv_rows, 2 * LANES), up_block),
                pl.BlockSpec((keys, rank), whole),
                pl.BlockSpec((keys, LANES), whole),
                pl.BlockSpec((rows, qlat_t.shape[0]), whole),
            ],
            scratch_shapes=[
                pltpu.VMEM((2, rows, LANES), jnp.bfloat16),
                pltpu.VMEM((2, LANES, rows), jnp.float32),
                pltpu.VMEM((8, rows), jnp.float32),
                pltpu.VMEM((rank, 2 * LANES), jnp.float32),
            ],
        ),
        out_shape=[
            jax.ShapeDtypeStruct((devices, q_rows, HEADS * LANES), jnp.bfloat16),
            jax.ShapeDtypeStruct((devices, kv_rows, HEADS * LANES), jnp.bfloat16),
            jax.ShapeDtypeStruct((keys, rank), jnp.float32),
            jax.ShapeDtypeStruct((keys, LANES), jnp.float32),
            jax.ShapeDtypeStruct((rows, qlat_t.shape[0]), jnp.float32),
        ],
        compiler_params=pltpu.CompilerParams(vmem_limit_bytes=48 << 20),
        cost_estimate=LIGHT,
        input_output_aliases={15 + i: i for i in range(len(prev[:2]))},
        name="attend_backward",
    )(bounds, qlat_t, up, q, kvn, kvn_t, up, krope, grad_out, out, lse, cos, sin_r, sin_l, start, *prev[:2], *deps, *prev[2:])


def hidden_kernel(*refs, count):
    normed, grads, (gate_w, up_w, down_w) = refs[:count], refs[count : 2 * count], refs[2 * count : 2 * count + 3]
    active, grad_gate, grad_up = refs[-3:]
    height = normed[0].shape[0]
    for i in range(count):
        rows = slice(i * height, (i + 1) * height)
        x = normed[i][...]
        gate = dot(x, gate_w[...], 1, 0)
        upper = dot(x, up_w[...], 1, 0)
        grad = dot(grads[i][...], down_w[...], 1, 1)
        sigmoid = jax.nn.sigmoid(gate)
        silu = gate * sigmoid
        active[rows, :] = (silu * upper).astype(jnp.bfloat16)
        grad_gate[rows, :] = (grad * upper * sigmoid * (1.0 + gate * (1.0 - sigmoid))).astype(jnp.bfloat16)
        grad_up[rows, :] = (grad * silu).astype(jnp.bfloat16)


def hidden_units(first_row, all_rows, prev, normed, grads, gate_w, up_w, down_w):
    count = len(normed)
    height, width = normed[0].shape
    rows, hidden = count * height, gate_w.shape[1]
    tile = 2 * LANES
    whole = lambda j: (0, 0)
    at = first_row // rows
    return pl.pallas_call(
        functools.partial(hidden_kernel, count=count),
        grid=(pl.cdiv(hidden, tile),),
        in_specs=[pl.BlockSpec((height, width), whole)] * (2 * count)
        + [pl.BlockSpec((width, tile), lambda j: (0, j))] * 2
        + [pl.BlockSpec((tile, width), lambda j: (j, 0))]
        + [pl.BlockSpec(memory_space=pl.ANY)] * len(prev),
        out_specs=[pl.BlockSpec((rows, tile), lambda j: (at, j))] * 3,
        out_shape=[jax.ShapeDtypeStruct((all_rows, hidden), jnp.bfloat16)] * 3,
        input_output_aliases={2 * count + 3 + i: i for i in range(len(prev))},
        compiler_params=pltpu.CompilerParams(vmem_limit_bytes=48 << 20),
        cost_estimate=LIGHT,
        name="hidden_units",
    )(*normed, *grads, gate_w, up_w, down_w, *prev)


def back_kernel(*refs, terms, contract):
    left, right, outs = refs[:terms], refs[terms : 2 * terms], refs[2 * terms :]
    height = outs[0].shape[0]
    for i, out in enumerate(outs):
        rows = slice(i * height, (i + 1) * height)
        total = dot(left[0][rows, :], right[0][...], 1, contract)
        for a, b in zip(left[1:], right[1:]):
            total = total + dot(a[rows, :], b[...], 1, contract)
        out[...] = total.astype(jnp.bfloat16)


def to_tokens(first_row, height, count, left, right, contract):
    hidden = left[0].shape[1]
    width = right[0].shape[1 - contract]
    rows = height * count
    tile = 2 * LANES
    at = first_row // rows
    if contract:
        right_spec = pl.BlockSpec((tile, hidden), lambda j: (j, 0))
    else:
        right_spec = pl.BlockSpec((hidden, tile), lambda j: (0, j))
    return pl.pallas_call(
        functools.partial(back_kernel, terms=len(left), contract=contract),
        grid=(width // tile,),
        in_specs=[pl.BlockSpec((rows, hidden), lambda j: (at, 0))] * len(left) + [right_spec] * len(left),
        out_specs=[pl.BlockSpec((height, tile), lambda j: (0, j))] * count,
        out_shape=[jax.ShapeDtypeStruct((height, width), jnp.bfloat16)] * count,
        compiler_params=pltpu.CompilerParams(vmem_limit_bytes=48 << 20),
        cost_estimate=LIGHT,
        name="to_tokens",
    )(*left, *right)


def blank(shape):
    return pl.pallas_call(
        lambda out: None,
        out_specs=pl.BlockSpec(memory_space=pl.ANY),
        out_shape=jax.ShapeDtypeStruct(shape, jnp.bfloat16),
        cost_estimate=LIGHT,
        name="blank",
    )()


D = 2560
FF = 6400
CONTS = 4
variance_eps = 1e-05
depth_scale = 1.4 / math.sqrt(62.0)
BF16 = jnp.bfloat16
F32 = jnp.float32


def rms_forward(values, gain_vector):
    inverse = lax.rsqrt(jnp.mean(values * values, axis=-1, keepdims=True) + variance_eps)
    return (values * inverse * gain_vector, inverse)


def rms_backward(values, inverse, gain_vector, upstream):
    scaled = upstream * gain_vector
    inner_mean = jnp.mean(scaled * values, axis=-1, keepdims=True)
    grad_values = inverse * scaled - values * inverse * inverse * inverse * inner_mean
    grad_gain = jnp.sum(upstream * values * inverse, axis=0)
    return (grad_values, grad_gain)


def segment_starts(lengths, index):
    own = jnp.zeros_like(index)
    begin = jnp.int32(PROMPT)
    for c in range(CONTS):
        own = jnp.where(index >= begin, begin, own)
        begin = begin + lengths[c]
    return own


def rope_tables(position):
    frequency = jnp.exp(jnp.arange(ROPE // 2, dtype=F32) * (-2.0 * math.log(10000.0) / ROPE))
    angles = position.astype(F32)[:, None] * frequency[None, :]
    cosine, sine = jnp.cos(angles), jnp.sin(angles)
    rows = position.shape[0]
    zeros = lambda n: jnp.zeros((rows, n), F32)
    return (
        jnp.concatenate([jnp.ones((rows, NOPE), F32), cosine, cosine, zeros(32)], axis=1),
        jnp.concatenate([zeros(80), sine, zeros(32)], axis=1),
        jnp.concatenate([zeros(64), -sine, zeros(48)], axis=1),
        cosine,
        sine,
    )


def rotate(values, cosine, sine):
    first, second = values[:, : ROPE // 2], values[:, ROPE // 2 :]
    return jnp.concatenate([first * cosine - second * sine, second * cosine + first * sine], axis=1)


def swap(tensor, bit, n):
    return lax.ppermute(tensor, "fsdp", [(i, i ^ bit) for i in range(n)])


def bit_orders(n):
    bits = []
    bit = 2
    while bit < n:
        bits.append(bit)
        bit *= 2
    return [bits, bits[::-1]]


def arrivals(n):
    orders = bit_orders(n)
    steps = [[(0, part) for part in range(2)]]
    for at in range(len(orders[0])):
        steps.append([
            (r | order[at], part)
            for part, order in enumerate(orders)
            for r in range(0, n, 2)
            if not r & ~sum(order[:at])
        ])
    return steps


ATTEND_PARTS = ((0, 4), (4, 5), (9, 6), (15, HEADS // 2 - 15))


def own_blocks(tensor):
    half = tensor.shape[0] // 2
    return {(0, part): tensor[part * half : (part + 1) * half] for part in range(2)}


def gather_step(blocks, n, at):
    return {
        (r | order[at], p): swap(block, order[at], n)
        for part, order in enumerate(bit_orders(n))
        for (r, p), block in blocks.items()
        if p == part
    }


def scatter_step(blocks, n, at, hold=None):
    arrived = {}
    for part, order in enumerate(bit_orders(n)):
        bit = order[at]
        for r, p in blocks:
            if p == part and not r & bit:
                arrived[r, p] = swap(blocks[r | bit, p].astype(BF16), bit, n)
    if hold is not None:
        hold, arrived = tie(hold, arrived)
    return {key: blocks[key].astype(F32) + block.astype(F32) for key, block in arrived.items()}, hold


def chip_scatter(blocks, n):
    for at in range(len(bit_orders(n)[0]))[::-1]:
        blocks, _ = scatter_step(blocks, n, at)
    return jnp.concatenate([blocks[0, part] for part in range(2)])


def tie(*trees):
    return lax.optimization_barrier(trees)


def ring(shift, count):
    return [(i, (i + shift) % count) for i in range(count)]


def seq_gather(share, layer, layers):
    whole = jnp.zeros((layers, *share.shape), share.dtype)
    for shift in range(layers):
        block = lax.ppermute(share, "seq", ring(shift, layers)) if shift else share
        whole = lax.dynamic_update_index_in_dim(whole, block, (layer - shift) % layers, 0)
    return whole.reshape(-1, *share.shape[1:])


def seq_scatter(whole, layer, layers):
    shares = whole.reshape(layers, -1, *whole.shape[1:])
    total = pick(shares, layer).astype(F32)
    for shift in range(1, layers):
        total = total + lax.ppermute(pick(shares, (layer + shift) % layers), "seq", ring(shift, layers)).astype(F32)
    return total


def pick(tensor, at, axis=0):
    return lax.dynamic_index_in_dim(tensor, at, axis, keepdims=False)


def core_scatter(split, core, n, axis=0):
    arrived = swap(pick(split, 1 - core, axis).astype(BF16), 1, n)
    return pick(split, core, axis).astype(F32) + arrived.astype(F32)


def core_shares(part, n):
    return jnp.swapaxes(part.astype(BF16).reshape(n // 2, 2, part.shape[0] // n, part.shape[1]), 0, 1)


def chip_blocks(mine, chip, n):
    half = mine.shape[1] // 2
    blocks = {}
    for r in range(0, n, 2):
        own = pick(mine, chip ^ (r // 2))
        for p in range(2):
            blocks[r, p] = own[p * half : (p + 1) * half]
    return blocks


def fsdp_scatter(part, core, chip, n):
    return chip_scatter(chip_blocks(core_scatter(core_shares(part, n), core, n).astype(BF16), chip, n), n)


def body(
    n,
    block_input,
    cont_lengths,
    attn_gain,
    q_down,
    q_gain,
    q_up,
    kv_down,
    kv_gain,
    kv_up,
    out_proj,
    mlp_gain,
    gate_up,
    down_proj,
    out_cotangent,
):
    rows = block_input.shape[1]
    chips = n // 2
    ff_chip = FF // chips
    ff_sent = -(-ff_chip // LANES) * LANES
    ff_wide = ff_sent
    group_len = rows * lax.axis_size("seq")
    device = lax.axis_index("fsdp")
    core, chip = device % 2, device // 2
    layers = lax.axis_size("seq")
    layer = lax.axis_index("seq")
    rank_q, rank_kv = q_up.shape[0] * n, kv_up.shape[0] * n
    first_row = lax.axis_index("seq") * rows
    index = first_row + jnp.arange(rows, dtype=jnp.int32)
    own_start = segment_starts(cont_lengths[0], index)
    position = jnp.where(own_start > 0, PROMPT + index - own_start, index)
    cos, sin_r, sin_l, cosine, sine = rope_tables(position)
    fold = SCALE * LOG2E
    start_row = own_start[None, :]
    full_rows, mask_rows = 1024, 512
    full_blocks = jnp.minimum(first_row, PROMPT) // full_rows
    bounds = jnp.stack([
        full_blocks,
        jnp.where(first_row < PROMPT, full_blocks * (full_rows // mask_rows), own_start[0] // mask_rows),
        (first_row + rows + mask_rows - 1) // mask_rows,
        first_row,
    ]).astype(jnp.int32)

    gains = lax.all_gather(jnp.concatenate([attn_gain, mlp_gain, q_gain, kv_gain]), "fsdp", axis=0)
    widths = [v.shape[0] for v in (attn_gain, mlp_gain, q_gain, kv_gain)]
    gain_list = []
    at = 0
    for width in widths:
        gain_list.append(gains[:, at : at + width].reshape(-1).astype(F32))
        at += width
    attn_gain_all, mlp_gain_all, q_gain_all, kv_gain_all = gain_list

    down_all = lax.all_gather(jnp.concatenate([q_down, kv_down], axis=1), "fsdp", axis=0, tiled=True)
    q_up_wide = jnp.pad(q_up.reshape(-1, HEADS, NOPE + ROPE), ((0, 0), (0, 0), (0, ROPE))).reshape(-1, HEADS * LANES)
    q_rows = q_up.shape[0]
    up_all = lax.all_gather(jnp.concatenate([q_up_wide, kv_up], axis=0), "fsdp", axis=0)
    out_proj_all = lax.all_gather(out_proj, "fsdp", axis=0, tiled=True)

    steps = arrivals(n)
    fetch = (D // n) // layers
    half_down = swap(down_proj, 1, n)
    down_w = jnp.concatenate([
        jnp.where(core == 0, down_proj, half_down),
        jnp.where(core == 0, half_down, down_proj),
        jnp.zeros((ff_wide - ff_chip, D), BF16),
    ])
    own_fetch = lax.dynamic_slice_in_dim(gate_up, layer * fetch, fetch, 0)
    widen = lambda v: jnp.pad(v, ((0, 0), (0, ff_sent - ff_chip)))
    own_fetch = jnp.stack([
        jnp.stack([widen(own_fetch[:, at + c * ff_chip : at + (c + 1) * ff_chip]) for at in (0, FF)]) for c in range(chips)
    ])
    own_fetch = [pick(own_fetch, chip ^ (r // 2)) for r in range(0, n, 2)]
    tables = (cos * fold, sin_r * fold, sin_l * fold, cos, sin_r, sin_l)
    down_all, tables, down_w, own_fetch = tie(down_all, tables, down_w, own_fetch)

    token_rows = block_input[0].astype(F32)
    normed_float, attn_inverse = rms_forward(token_rows, attn_gain_all)
    normed = normed_float.astype(BF16)
    latent = jnp.dot(normed, down_all, preferred_element_type=F32)
    q_latent, kv_latent, rope_latent = jnp.split(latent, [rank_q, rank_q + rank_kv], axis=1)
    q_lat_float, q_inverse = rms_forward(q_latent, q_gain_all)
    q_lat_normed = q_lat_float.astype(BF16)
    kv_float, kv_inverse = rms_forward(kv_latent, kv_gain_all)
    key_rope = jnp.pad(rotate(rope_latent, cosine, sine), ((0, 0), (NOPE, LANES - NOPE - ROPE)))
    kv_own = jnp.concatenate([kv_float, key_rope], axis=1).astype(BF16)
    kv_all = seq_gather(kv_own, layer, layers)
    cotangent = out_cotangent[0].astype(F32)
    grad_low = (depth_scale * cotangent).astype(BF16)
    up_all, kv_all, own_fetch, grad_low = tie(up_all, kv_all, own_fetch, grad_low)
    kv_normed, key_rope_all = kv_all[:, :rank_kv], kv_all[:, rank_kv:]
    forward_args = (
        bounds, q_lat_normed, up_all, kv_normed, key_rope_all,
        *tables[:3], start_row, full_rows, mask_rows,
    )

    fetched_blocks = [swap(block, 2 * r, n) if r else block for r, block in enumerate(own_fetch)]
    outputs = attend_forward(ATTEND_PARTS[0], [], [], *forward_args)
    outputs, fetched_blocks, grad_low = tie(outputs, fetched_blocks, grad_low)
    fetched = blank((2, chips, fetch, ff_sent))
    for r, block in enumerate(fetched_blocks):
        fetched = lax.dynamic_update_slice(fetched, block[:, None], (0, chip ^ r, 0, 0))
    grad_blocks = own_blocks(grad_low)
    passed = [(fetched, fetched)]
    for step in range(1, layers):
        link = (
            lax.ppermute(passed[-1][0], "seq", [(i, i + 1) for i in range(layers - 1)]),
            lax.ppermute(passed[-1][1], "seq", [(i + 1, i) for i in range(layers - 1)]),
        )
        moved = gather_step(grad_blocks, n, step - 1) if step < len(steps) else {}
        if step < len(ATTEND_PARTS):
            outputs = attend_forward(ATTEND_PARTS[step], outputs, [], *forward_args)
            outputs, link, moved = tie(outputs, link, moved)
        passed.append(link)
        grad_blocks = {**grad_blocks, **moved}
    for part in ATTEND_PARTS[layers:]:
        outputs = attend_forward(part, outputs, [], *forward_args)
    attended, queries, log_total = outputs
    attn_branch = jnp.dot(attended, out_proj_all, preferred_element_type=F32)
    middle = token_rows + depth_scale * attn_branch
    mlp_float, mlp_inverse = rms_forward(middle, mlp_gain_all)
    normed_blocks = own_blocks(mlp_float.astype(BF16))
    normed_blocks = {**normed_blocks, **gather_step(normed_blocks, n, 0)}
    normed_blocks, passed, grad_blocks = tie(normed_blocks, passed, grad_blocks)
    layer_blocks = [jnp.where(layer >= shift, passed[shift][0], passed[layers - shift][1]) for shift in range(1, layers)]
    for at in range(1, len(steps) - 1):
        normed_blocks = {**normed_blocks, **gather_step(normed_blocks, n, at)}
    hidden = [blank((chips, 2, layers, fetch, ff_wide)) for _ in range(2)]
    for shift in range(layers):
        block = layer_blocks[shift - 1] if shift else fetched
        source = (layer - shift) % layers
        for owner, arrived in ((core, block), (1 - core, swap(block, 1, n))):
            hidden = [
                lax.dynamic_update_slice(whole, v[:, None, None], (0, owner, source, 0, 0)) for whole, v in zip(hidden, arrived)
            ]
    gate_w, up_w = (v.reshape(D, ff_wide) for v in hidden)
    half = rows // 2
    first_rows = [sum(len(step) for step in steps[:i]) * half for i in range(len(steps))]
    kept = []
    for step, at in zip(steps, first_rows):
        kept = hidden_units(
            at, n * half, kept, [normed_blocks[key] for key in step], [grad_blocks[key] for key in step], gate_w, up_w, down_w
        )
    active, grad_gate, grad_up = kept
    all_normed = jnp.concatenate([normed_blocks[key] for step in steps for key in step])
    all_grad = jnp.concatenate([grad_blocks[key] for step in steps for key in step])

    back = lambda i, hidden: dict(zip(steps[i], to_tokens(first_rows[i], half, len(steps[i]), hidden, [gate_w, up_w], 1)))
    down_whole = dot(active, all_grad, 0, 0).astype(BF16)
    down_whole, grad_gate, grad_up = tie(down_whole, grad_gate, grad_up)
    last_blocks = back(-1, [grad_gate, grad_up])
    last_blocks, earlier = tie(last_blocks, [grad_gate, grad_up])
    half_ff = ff_chip // 2
    half_of = lambda at: lax.dynamic_slice_in_dim(down_whole, at * half_ff, half_ff, 0)
    down_part = (half_of(core).astype(F32) + swap(half_of(1 - core), 1, n).astype(F32)).astype(BF16)
    last_blocks, down_part, earlier = tie(last_blocks, down_part, [grad_gate, grad_up])
    down_share = lax.psum_scatter(down_part, "seq", scatter_dimension=0, tiled=True)
    early_blocks = {}
    for i in range(len(steps) - 1)[::-1]:
        early_blocks.update(back(i, earlier))
    blocks, _ = scatter_step({**last_blocks, **early_blocks}, n, len(steps) - 2)
    blocks, all_normed = tie(blocks, all_normed)
    hidden_parts, hidden_shares, crossing = [], [], []
    for grads in (grad_gate, grad_up):
        whole = dot(all_normed, grads, 0, 0).astype(BF16).reshape(chips, 2, layers, fetch, ff_wide)
        crossing.append((pick(whole, core, 1), swap(pick(whole, 1 - core, 1), 1, n)))
    for at in range(len(steps) - 2)[::-1]:
        blocks, _ = scatter_step(blocks, n, at)

    def over_layers(crossed):
        part = (crossed[0].astype(F32) + crossed[1].astype(F32)).astype(BF16).transpose(1, 0, 2, 3)
        hidden_parts.append(part)
        hidden_shares.append(lax.psum_scatter(part, "seq", scatter_dimension=0, tiled=True)[0])

    blocks, crossing[0], down_share = tie(blocks, crossing[0], down_share)
    over_layers(crossing[0])
    grad_mlp_normed = jnp.concatenate([blocks[0, part] for part in range(2)]).astype(F32)
    grad_mid_norm, mlp_gain_part = rms_backward(middle, mlp_inverse, mlp_gain_all, grad_mlp_normed)
    grad_middle = cotangent + grad_mid_norm
    grad_attn = (depth_scale * grad_middle).astype(BF16)
    out_proj_part = dot(attended, grad_attn, 0, 0).astype(BF16)
    grad_attended = dot(grad_attn, out_proj_all, 1, 1).astype(BF16)
    grad_attended, crossing[1] = tie(grad_attended, crossing[1])
    over_layers(crossing[1])
    backward_args = (
        bounds, q_lat_normed.T, up_all, queries, kv_normed, kv_normed.T, key_rope_all, grad_attended, attended, log_total,
        *tables[3:], start_row, full_rows, mask_rows,
    )
    out_shares = core_shares(out_proj_part, n)
    out_arrived = swap(pick(out_shares, 1 - core), 1, n)
    thirds = ((0, 12), (12, 4), (16, HEADS // 2 - 16))
    first = attend_backward(thirds[0], [], [*hidden_parts, out_proj_part], *backward_args)
    first, out_arrived = tie(first, out_arrived)
    out_mine = (pick(out_shares, core).astype(F32) + out_arrived.astype(F32)).astype(BF16)
    down_low = lax.all_gather(down_share, "seq", axis=0, tiled=True)
    second = attend_backward(thirds[1], first, [down_share, *hidden_shares], *backward_args)
    hidden_share = jnp.stack(hidden_shares)
    hidden_blocks = []
    for r in range(0, n, 2):
        block = pick(hidden_share, chip ^ (r // 2), 1)
        hidden_blocks.append(swap(block, r, n) if r else block)
    second, hidden_blocks = tie(second, hidden_blocks)
    hidden_blocks = jnp.stack(hidden_blocks)
    hidden_blocks = [pick(hidden_blocks, chip ^ c)[..., :ff_chip] for c in range(chips)]
    placed = jnp.concatenate([block[at] for at in range(2) for block in hidden_blocks], axis=1)
    out_blocks, second = scatter_step(chip_blocks(out_mine, chip, n), n, len(steps) - 2, second)
    third = attend_backward(thirds[2], second, [placed], *backward_args)
    for at in range(len(steps) - 2)[::-1]:
        out_blocks, third = scatter_step(out_blocks, n, at, third)
    out_share = jnp.concatenate([out_blocks[0, part] for part in range(2)]).astype(BF16)
    gate_up_low = lax.all_gather(placed, "seq", axis=0, tiled=True)
    q_up_part, kv_up_part, grad_kv_all, grad_rope_all, grad_q_lat = third
    grad_q_float, q_gain_part = rms_backward(q_latent, q_inverse, q_gain_all, grad_q_lat)
    grad_kv = seq_scatter(jnp.concatenate([grad_kv_all, grad_rope_all], axis=1).astype(BF16), layer, layers)
    up_parts = jnp.concatenate([q_up_part, kv_up_part], axis=1).reshape(-1, HEADS * LANES)
    up_share = fsdp_scatter(up_parts, core, chip, n).astype(BF16)
    grad_kv, active_last = tie(grad_kv, active)
    branch = {}
    for step, at in zip(steps, first_rows):
        branch.update(zip(step, to_tokens(at, half, len(step), [active_last], [down_w], 0)))
    grad_kv, up_share, out_share, down_low, gate_up_low, branch = tie(
        grad_kv, up_share, out_share, down_low, gate_up_low, branch
    )
    up_grad, out_proj_grad = lax.psum((up_share, out_share), "seq")
    down_grad, gate_up_grad = down_low.astype(F32), gate_up_low.astype(F32)
    grad_kv_first, kv_gain_part = rms_backward(kv_latent, kv_inverse, kv_gain_all, grad_kv[:, :rank_kv])
    grad_rope = rotate(grad_kv[:, rank_kv + NOPE : rank_kv + NOPE + ROPE], cosine, -sine)
    grad_latent = jnp.concatenate([grad_q_float, grad_kv_first, grad_rope], axis=1).astype(BF16)
    down_all_part = dot(normed, grad_latent, 0, 0)
    grad_normed = dot(grad_latent, down_all, 1, 1)
    grad_in_norm, attn_gain_part = rms_backward(token_rows, attn_inverse, attn_gain_all, grad_normed)
    grad_input = (grad_middle + grad_in_norm).reshape(block_input.shape)

    gain_parts = [v.reshape(n, -1) for v in (attn_gain_part, mlp_gain_part, q_gain_part, kv_gain_part)]
    gain_rows = jnp.concatenate(gain_parts, axis=1)
    gain_rows = jnp.pad(gain_rows[:, None], ((0, 0), (0, 15), (0, latent.shape[1] - gain_rows.shape[1])))
    down_rows = D // n
    down_all_part = jnp.concatenate([down_all_part.reshape(n, down_rows, -1), gain_rows], axis=1)
    down_all_share = fsdp_scatter(down_all_part.reshape(-1, latent.shape[1]), core, chip, n).astype(BF16)
    branch, down_all_share = scatter_step(branch, n, len(steps) - 2, down_all_share)
    for at in range(len(steps) - 2)[::-1]:
        branch, _ = scatter_step(branch, n, at)
    mlp_branch = jnp.concatenate([branch[0, part] for part in range(2)])
    output = (middle + depth_scale * mlp_branch).astype(BF16).reshape(block_input.shape)
    up_grad, out_proj_grad, down_all_share = tie(up_grad, out_proj_grad, down_all_share)
    down_all_grad = lax.psum(down_all_share, "seq").astype(F32)
    up_grad, out_proj_grad = up_grad.astype(F32), out_proj_grad.astype(F32)
    gain_sum = down_all_grad[down_rows]
    down_all_grad = down_all_grad[:down_rows]
    q_up_grad = up_grad[:q_rows].reshape(-1, HEADS, LANES)[..., : NOPE + ROPE].reshape(-1, HEADS * (NOPE + ROPE))
    kv_up_grad = up_grad[q_rows:]
    ends = [sum(widths[: i + 1]) for i in range(4)]
    attn_gain_grad, mlp_gain_grad, q_gain_grad, kv_gain_grad = jnp.split(gain_sum[: ends[3]], ends[:3])
    return (
        output,
        grad_input,
        attn_gain_grad,
        down_all_grad[:, :rank_q],
        q_gain_grad,
        q_up_grad,
        down_all_grad[:, rank_q:],
        kv_gain_grad,
        kv_up_grad,
        out_proj_grad,
        mlp_gain_grad,
        gate_up_grad,
        down_grad,
    )


def solution(mesh):
    tokens, matrix, vector = P("fsdp", "seq", None), P("fsdp", None), P("fsdp")
    return jax.shard_map(
        functools.partial(body, mesh.shape["fsdp"]),
        mesh=mesh,
        in_specs=(tokens, matrix, vector, matrix, vector, matrix, matrix, vector, matrix, matrix, vector, matrix, matrix, tokens),
        out_specs=(tokens, tokens, vector, matrix, vector, matrix, matrix, vector, matrix, matrix, vector, matrix, matrix),
        check_vma=False,
    )
```

time: 2140 us -> 1470 us (0.69)
  waiting for transfers between devices: 1170 us -> 508 us
  matrix products: 303 us -> 127 us
  Pallas kernels: 128 us -> 303 us
  blocking collectives: 182 us -> 10.1 us
  starting transfers between devices: 28.4 us -> 139 us
  other arithmetic: 113 us -> 178 us
    psum x1 -> x2, waiting for transfers between devices: 489 us -> 41.5 us  [the longest x1 31 us: body(): down_all_grad = lax.psum(down_all_share, 'seq').astype(F32)]
    reduce_scatter x5 -> x3, waiting for transfers between devices: 240 us -> 37.1 us  [the longest x2 37.1 us: over_layers(): lax.psum_scatter(part, 'seq', scatter_dimension=0, tiled=True)[0]]
    pallas_call x0 -> x12, Pallas kernels: none -> 169 us  [the longest x6 92.7 us: to_tokens(): pl.pallas_call(functools.partial(back_kernel, terms=len(left), contract=c...]
    all_to_all x1 -> x0, blocking collectives: 135 us -> none  [body(): hidden = lax.all_to_all(hidden, 'fsdp', 2, 0, axis_index_groups=same_core)]
    dot_general x12 -> x7, matrix products: 218 us -> 110 us  [dot(): lax.dot_general(a, b, (((ca,), (cb,)), ((), ())), preferred_element_type=...]
    ppermute x0 -> x12, starting transfers between devices: none -> 85.1 us  [the longest x3 59.4 us: seq_scatter(): lax.ppermute(pick(shares, (layer + shift) % layers), 'seq', ring(shift, l...]
    all_to_all x1 -> x0, waiting for transfers between devices: 83.4 us -> none  [body(): lax.all_to_all(hidden_part, 'fsdp', 0, 2, axis_index_groups=same_core)]
    all_gather x5 -> x3, waiting for transfers between devices: 0.04 us -> 69.1 us  [the longest x1 48.2 us: body(): gate_up_low = lax.all_gather(placed, 'seq', axis=0, tiled=True)]
  transfers between devices with their start and end apart: 40 -> 81, of which waited for: 20 -> 33; matrix products, arithmetic and copies ran while one was open for 21% -> 23% of each run, Pallas kernels for 3% -> 18%
where the time goes in v2:
time: 1470 us; the launch traced here: 1460 us
  waiting for transfers between devices  508 us (35%)
  Pallas kernels  303 us (21%)
  other arithmetic  178 us (12%)
  local copies, waits for them, and re-layouts  173 us (12%)
  starting transfers between devices  139 us (9%)
  matrix products  127 us (9%)
  between operations  21.3 us (1%)
    ppermute x59, waiting for transfers between devices, swap(): return lax.ppermute(tensor, 'fsdp', [(i, i ^ bit) for i in range(n)])  301 us
    dot_general x7, matrix products, dot(): lax.dot_general(a, b, (((ca,), (cb,)), ((), ())), preferred_element_type=...  110 us
    pallas_call x6, Pallas kernels, to_tokens(): pl.pallas_call(functools.partial(back_kernel, terms=len(left), contract=c...  92.7 us
    unnamed x290, local copies, waits for them, and re-layouts  78.3 us
    pallas_call x3, Pallas kernels, attend_backward(): pl.pallas_call(functools.partial(bwd_kernel, full_rows=full_rows, mask_ro...  77.3 us
    pallas_call x3, Pallas kernels, hidden_units(): pl.pallas_call(functools.partial(hidden_kernel, count=count), grid=(pl.cd...  76 us
    ppermute x3, starting transfers between devices, seq_scatter(): lax.ppermute(pick(shares, (layer + shift) % layers), 'seq', ring(shift, l...  59.4 us
    pallas_call x4, Pallas kernels, attend_forward(): pl.pallas_call(functools.partial(fwd_kernel, full_rows=full_rows, mask_ro...  57.4 us
  transfers between devices with their start and end apart: 81, of which 33 were waited for; matrix products, arithmetic and copies ran while one was open for 23% of the time, Pallas kernels for 18%

profile of v2, /device:TPU:0, one launch (start us, length us, event | category | flops | bytes accessed | tf_op | source)
XLA Modules:
  0.0 1459.2 jit_solution(159914013345847404)
XLA Ops:
  102.1 20.9 %all-gather.17.cloned.1.call-done = bf16[1024,5120]{1,0:T(8,128)(2,1)} async-done(((bf16[128,5120]{1,0:T(8,128)(2,1)}), bf16[1024,5120]{1,0:T(8,128)(2,1)}) %all-gather.17.cloned.1.call-update) | async-done | bytes 10485776 | tf_op jit(solution)/shard_map/all_gather | solution.py:540
  144.4 17.9 %collective-permute-done.6 = bf16[2,80,1664]{2,1,0:T(8,128)(2,1)} collective-permute-done((bf16[2,80,1664]{2,1,0:T(8,128)(2,1)}, bf16[2,80,1664]{2,1,0:T(8,128)(2,1)}, u32[]{:S(2)}, u32[]{:S(2)}) %collective-permute-start.6) | collective-permute-done | bytes 532512 | tf_op jit(solution)/shard_map/ppermute | solution.py:373
  189.9 41.2 %collective-permute-done.9.refs_2_ = bf16[256,2560]{1,0:T(8,128)(2,1)S(1)} collective-permute-done((bf16[256,2560]{1,0:T(8,128)(2,1)S(1)}, bf16[256,2560]{1,0:T(8,128)(2,1)S(1)}, u32[]{:S(2)}, u32[]{:S(2)}) %collective-permute-start.9) | collective-permute-done | bytes 1310752 | tf_op jit(solution)/shard_map/ppermute | solution.py:373
  241.6 22.1 %collective-permute-done.13.refs_6_ = bf16[256,2560]{1,0:T(8,128)(2,1)S(1)} collective-permute-done((bf16[256,2560]{1,0:T(8,128)(2,1)S(1)}, bf16[256,2560]{1,0:T(8,128)(2,1)S(1)}, u32[]{:S(2)}, u32[]{:S(2)}) %collective-permute-start.13) | collective-permute-done | bytes 1310752 | tf_op jit(solution)/shard_map/ppermute | solution.py:373
  265.1 16.4 %attend_forward.6 = (bf16[512,2560]{1,0:T(8,128)(2,1)S(1)}, bf16[512,5120]{1,0:T(8,128)(2,1)}, f32[160,512]{1,0:T(8,128)S(1)}) custom-call(s32[4]{0:T(128)S(1)} %pad_add_fusion.bounds, bf16[512,768]{1,0:T(8,128)(2,1)S(1)} %copy-done.5, bf16[8,128,5120]{2,1,0:T(8,128)(2,1)} %bitcast.396, ...), custom_call_target="tpu_custom_call", output_to_operand_aliasing={{0}: (10, {}), {1}: (11, {}), {2}: (12, {})} | custom-call | flops 1048576 | bytes 65536 | tf_op jit(solution)/shard_map/attend_forward/pallas_call | solution.py:82
  322.6 19.3 %collective-permute-done.17 = bf16[2,4,80,1664]{3,2,1,0:T(8,128)(2,1)} collective-permute-done((bf16[2,4,80,1664]{3,2,1,0:T(8,128)(2,1)}, bf16[2,4,80,1664]{3,2,1,0:T(8,128)(2,1)}, u32[]{:S(2)}, u32[]{:S(2)}) %collective-permute-start.17) | collective-permute-done | bytes 2129952 | tf_op jit(solution)/shard_map/ppermute | solution.py:590
  418.1 19.2 %hidden_units.3 = (bf16[2048,1664]{1,0:T(8,128)(2,1)}, bf16[2048,1664]{1,0:T(8,128)(2,1)}, bf16[2048,1664]{1,0:T(8,128)(2,1)}) custom-call(bf16[256,2560]{1,0:T(8,128)(2,1)S(1)} %get-tuple-element.267.refs_0_, bf16[256,2560]{1,0:T(8,128)(2,1)S(1)} %get-tuple-element.269.refs_1_, bf16[256,2560]{1,0:T(8,128)(2,1)S(1)} %copy-done.15, ...), custom_call_target="tpu_custom_call" | custom-call | flops 1048576 | bytes 65536 | tf_op jit(solution)/shard_map/hidden_units/pallas_call | solution.py:262
  437.4 19.9 %hidden_units.4 = (bf16[2048,1664]{1,0:T(8,128)(2,1)}, bf16[2048,1664]{1,0:T(8,128)(2,1)}, bf16[2048,1664]{1,0:T(8,128)(2,1)}) custom-call(bf16[256,2560]{1,0:T(8,128)(2,1)} %collective-permute-done.19.refs_0_, bf16[256,2560]{1,0:T(8,128)(2,1)} %collective-permute-done.20.refs_1_, ...), custom_call_target="tpu_custom_call", output_to_operand_aliasing={{0}: (7, {}), {1}: (8, {}), {2}: (9, {})} | custom-call | flops 1048576 | bytes 65536 | tf_op jit(solution)/shard_map/hidden_units/pallas_call | solution.py:262
  457.3 36.9 %hidden_units.5 = (bf16[2048,1664]{1,0:T(8,128)(2,1)}, bf16[2048,1664]{1,0:T(8,128)(2,1)}, bf16[2048,1664]{1,0:T(8,128)(2,1)}) custom-call(bf16[256,2560]{1,0:T(8,128)(2,1)S(1)} %collective-permute-done.21.refs_0_, bf16[256,2560]{1,0:T(8,128)(2,1)S(1)} %collective-permute-done.22.refs_1_, ...), custom_call_target="tpu_custom_call", output_to_operand_aliasing={{0}: (11, {}), {1}: (12, {}), {2}: (13, {})} | custom-call | flops 1048576 | bytes 65536 | tf_op jit(solution)/shard_map/hidden_units/pallas_call | solution.py:262
  494.2 22.4 %convolution_convert_fusion.3 = bf16[1664,2560]{1,0:T(8,128)(2,1)S(1)} fusion(bf16[2048,1664]{1,0:T(8,128)(2,1)} %get-tuple-element.380.refs_0_, bf16[2048,2560]{1,0:T(8,128)(2,1)} %copy-done.101), kind=kOutput, calls=%fused_computation.7 | convolution fusion | flops 17452564480 | bytes 25821184 | tf_op jit(solution)/shard_map/dot_general | solution.py:24
  529.4 25.9 %to_tokens.6 = (bf16[256,2560]{1,0:T(8,128)(2,1)S(1)}, bf16[256,2560]{1,0:T(8,128)(2,1)}, bf16[256,2560]{1,0:T(8,128)(2,1)}, bf16[256,2560]{1,0:T(8,128)(2,1)S(1)}) custom-call(bf16[2048,1664]{1,0:T(8,128)(2,1)} %get-tuple-element.306.refs_0_, bf16[2048,1664]{1,0:T(8,128)(2,1)} %get-tuple-element.307.refs_1_, ...), custom_call_target="tpu_custom_call" | custom-call | flops 1048576 | bytes 65536 | tf_op jit(solution)/shard_map/to_tokens/pallas_call | solution.py:299
  588.8 16.2 %to_tokens.8 = (bf16[256,2560]{1,0:T(8,128)(2,1)S(1)}, bf16[256,2560]{1,0:T(8,128)(2,1)S(1)}) custom-call(bf16[2048,1664]{1,0:T(8,128)(2,1)} %get-tuple-element.306.refs_0_, bf16[2048,1664]{1,0:T(8,128)(2,1)} %get-tuple-element.307.refs_1_, bf16[2560,1664]{1,0:T(8,128)(2,1)} %bitcast.57.refs_4_.refs_8_.refs_2_, ...), custom_call_target="tpu_custom_call" | custom-call | flops 1048576 | bytes 65536 | tf_op jit(solution)/shard_map/to_tokens/pallas_call | solution.py:299
  633.2 23.1 %convolution_convert_fusion.2 = bf16[2560,1664]{1,0:T(8,128)(2,1)} fusion(bf16[2048,2560]{1,0:T(8,128)(2,1)} %constant_dynamic-update-slice_fusion.8, bf16[2048,1664]{1,0:T(8,128)(2,1)S(1)} %bitcast.407), kind=kOutput, calls=%fused_computation.6 | convolution fusion | flops 17452564480 | bytes 25821184 | tf_op jit(solution)/shard_map/dot_general | solution.py:24
  665.3 26.8 %collective-permute-done.34 = bf16[256,2560]{1,0:T(8,128)(2,1)S(1)} collective-permute-done((bf16[256,2560]{1,0:T(8,128)(2,1)S(1)}, bf16[256,2560]{1,0:T(8,128)(2,1)S(1)}, u32[]{:S(2)}, u32[]{:S(2)}) %collective-permute-start.34) | collective-permute-done | bytes 1310752 | tf_op jit(solution)/shard_map/ppermute | solution.py:373
  701.4 25.3 %convolution_convert_fusion.1 = bf16[2560,1664]{1,0:T(8,128)(2,1)} fusion(bf16[2048,2560]{1,0:T(8,128)(2,1)} %constant_dynamic-update-slice_fusion.8, bf16[2048,1664]{1,0:T(8,128)(2,1)} %get-tuple-element.307.refs_1_), kind=kOutput, calls=%fused_computation.5 | convolution fusion | flops 17452564480 | bytes 25821184 | tf_op jit(solution)/shard_map/dot_general | solution.py:24
  788.2 41.6 %attend_backward.3 = (bf16[8,96,5120]{2,1,0:T(8,128)(2,1)}, bf16[8,32,5120]{2,1,0:T(8,128)(2,1)}, f32[2048,256]{1,0:T(8,128)}, f32[2048,128]{1,0:T(8,128)S(1)}, f32[512,768]{1,0:T(8,128)}) custom-call(s32[4]{0:T(128)S(1)} %pad_add_fusion.bounds, bf16[768,512]{1,0:T(8,128)(2,1)S(1)} %copy-done.9, bf16[8,128,5120]{2,1,0:T(8,128)(2,1)} %bitcast.400, ...), custom_call_target="tpu_custom_call" | custom-call | flops 1048576 | bytes 65536 | tf_op jit(solution)/shard_map/attend_backward/pallas_call | solution.py:189
  833.1 37.1 %reduce-scatter.8.cloned.1.call-done = bf16[1,4,80,1664]{3,2,1,0:T(8,128)(2,1)} async-done(((bf16[4,4,80,1664]{3,2,1,0:T(8,128)(2,1)}), bf16[1,4,80,1664]{3,2,1,0:T(8,128)(2,1)}) %reduce-scatter.8.cloned.1.call-update) | async-done | bytes 1064976 | tf_op jit(solution)/shard_map/reduce_scatter | solution.py:656
  904.3 18.0 %attend_backward.4 = (bf16[8,96,5120]{2,1,0:T(8,128)(2,1)}, bf16[8,32,5120]{2,1,0:T(8,128)(2,1)}, f32[2048,256]{1,0:T(8,128)}, f32[2048,128]{1,0:T(8,128)S(1)}, f32[512,768]{1,0:T(8,128)}) custom-call(s32[4]{0:T(128)S(1)} %pad_add_fusion.bounds, bf16[768,512]{1,0:T(8,128)(2,1)S(1)} %copy-done.10, ...), custom_call_target="tpu_custom_call", output_to_operand_aliasing={{0}: (15, {}), {1}: (16, {})} | custom-call | flops 1048576 | bytes 65536 | tf_op jit(solution)/shard_map/attend_backward/pallas_call | solution.py:189
  922.3 19.1 %collective-permute-done.41 = bf16[2,80,1664]{2,1,0:T(8,128)(2,1)} collective-permute-done((bf16[2,80,1664]{2,1,0:T(8,128)(2,1)}, bf16[2,80,1664]{2,1,0:T(8,128)(2,1)}, u32[]{:S(2)}, u32[]{:S(2)}) %collective-permute-start.41) | collective-permute-done | bytes 532512 | tf_op jit(solution)/shard_map/ppermute | solution.py:373
  964.5 17.8 %attend_backward.5 = (bf16[8,96,5120]{2,1,0:T(8,128)(2,1)}, bf16[8,32,5120]{2,1,0:T(8,128)(2,1)}, f32[2048,256]{1,0:T(8,128)}, f32[2048,128]{1,0:T(8,128)S(1)}, f32[512,768]{1,0:T(8,128)}) custom-call(s32[4]{0:T(128)S(1)} %pad_add_fusion.bounds, bf16[768,512]{1,0:T(8,128)(2,1)S(1)} %copy-done.11, ...), custom_call_target="tpu_custom_call", output_to_operand_aliasing={{0}: (15, {}), {1}: (16, {})} | custom-call | flops 1048576 | bytes 65536 | tf_op jit(solution)/shard_map/attend_backward/pallas_call | solution.py:189
  997.2 58.5 %collective-permute-start.50 = (bf16[512,384]{1,0:T(8,128)(2,1)}, bf16[512,384]{1,0:T(8,128)(2,1)}, u32[]{:S(2)}, u32[]{:S(2)}) collective-permute-start(bf16[512,384]{1,0:T(8,128)(2,1)} %get-tuple-element.565), channel_id=1, source_target_pairs={{0,3},{1,0},{2,1},{3,2},{4,7},{5,4},{6,5},{7,6},{8,11},{9,8},{10,9... | collective-permute-start | bytes 1179656 | tf_op jit(solution)/shard_map/ppermute | solution.py:453
  1169.1 48.2 %all-gather.15.cloned.1.call-done = bf16[320,12800]{1,0:T(8,128)(2,1)} async-done(((bf16[80,12800]{1,0:T(8,128)(2,1)}), bf16[320,12800]{1,0:T(8,128)(2,1)}) %all-gather.15.cloned.1.call-update) | async-done | bytes 8192016 | tf_op jit(solution)/shard_map/all_gather | solution.py:694
  1296.0 59.5 %collective-permute-done.62 = bf16[168,1056]{1,0:T(8,128)(2,1)S(1)} collective-permute-done((bf16[168,1056]{1,0:T(8,128)(2,1)S(1)}, bf16[168,1056]{1,0:T(8,128)(2,1)S(1)}, u32[]{:S(2)}, u32[]{:S(2)}) %collective-permute-start.62) | collective-permute-done | bytes 354848 | tf_op jit(solution)/shard_map/ppermute | solution.py:373
  1403.4 31.0 %all-reduce.14.cloned.1.call-done = bf16[336,1056]{1,0:T(8,128)(2,1)} async-done(((bf16[336,1056]{1,0:T(8,128)(2,1)}), bf16[336,1056]{1,0:T(8,128)(2,1)}) %all-reduce.14.cloned.1.call-update) | async-done | bytes 709648 | tf_op jit(solution)/shard_map/psum | solution.py:729
  (650 shorter events, 753.9 us)
Async XLA Ops:
  10.4 112.5 %all-gather.17.cloned.1.call-start = ((), (), s32[]{:S(2)}) async-start(), calls=%async_computation.11 | async-start | bytes 11796480 | tf_op jit(solution)/shard_map/all_gather | solution.py:540
  13.6 334.4 %all-gather.11.cloned.1.call-start = ((), (), s32[]{:S(2)}) async-start(), calls=%async_computation.4 | async-start | bytes 14745600 | tf_op jit(solution)/shard_map/all_gather | solution.py:541
  14.3 680.4 %reduce-scatter.4.cloned.1.call-start = ((), (), s32[]{:S(2)}) async-start(), calls=%async_computation.5 | async-start | bytes 5120000 | tf_op jit(solution)/shard_map/reduce_scatter | solution.py:640
  165.8 66.3 %collective-permute-start.7 = (bf16[2,4,80,1664]{3,2,1,0:T(8,128)(2,1)S(1)}, bf16[2,4,80,1664]{3,2,1,0:T(8,128)(2,1)}, u32[]{:S(2)}, u32[]{:S(2)}) collective-permute-start(bf16[2,4,80,1664]{3,2,1,0:T(8,128)(2,1)S(1)} %bitcast_dynamic-update-slice_fusion), channel_id=1, source_target_pairs={{0,1},{1,2},{2,3},{4,5},{5,6},{6,7},{8,9},{9,10},{10,11},{12,13},{... | collective-permute-start | bytes 6389768 | tf_op jit(solution)/shard_map/ppermute | solution.py:590
  175.8 87.8 %collective-permute-start.13 = (bf16[256,2560]{1,0:T(8,128)(2,1)S(1)}, bf16[256,2560]{1,0:T(8,128)(2,1)S(1)}, u32[]{:S(2)}, u32[]{:S(2)}) collective-permute-start(bf16[256,2560]{1,0:T(8,128)(2,1)S(1)} %get-tuple-element.285.refs_3_), channel_id=1, source_target_pairs={{0,8},{4,12},{8,0},{12,4},{16,24},{20,28},{24,16},{28,20},{1,9},{5... | collective-permute-start | bytes 3932168 | tf_op jit(solution)/shard_map/ppermute | solution.py:373
  232.1 62.6 %collective-permute-start.11 = (bf16[2,4,80,1664]{3,2,1,0:T(8,128)(2,1)}, bf16[2,4,80,1664]{3,2,1,0:T(8,128)(2,1)}, u32[]{:S(2)}, u32[]{:S(2)}) collective-permute-start(bf16[2,4,80,1664]{3,2,1,0:T(8,128)(2,1)} %collective-permute-done.7), channel_id=1, source_target_pairs={{0,1},{1,2},{2,3},{4,5},{5,6},{6,7},{8,9},{9,10},{10,11},{12,13},{... | collective-permute-start | bytes 6389768 | tf_op jit(solution)/shard_map/ppermute | solution.py:590
  303.1 65.0 %collective-permute-start.25 = (bf16[2,4,80,1664]{3,2,1,0:T(8,128)(2,1)}, bf16[2,4,80,1664]{3,2,1,0:T(8,128)(2,1)}, u32[]{:S(2)}, u32[]{:S(2)}) collective-permute-start(bf16[2,4,80,1664]{3,2,1,0:T(8,128)(2,1)} %copy-done.73), channel_id=1, source_target_pairs={{0,4},{4,0},{8,12},{12,8},{16,20},{20,16},{24,28},{28,24},{1,5},{5... | collective-permute-start | bytes 6389768 | tf_op jit(solution)/shard_map/ppermute | solution.py:373
  392.0 65.2 %collective-permute-start.21 = (bf16[256,2560]{1,0:T(8,128)(2,1)S(1)}, bf16[256,2560]{1,0:T(8,128)(2,1)S(1)}, u32[]{:S(2)}, u32[]{:S(2)}) collective-permute-start(bf16[256,2560]{1,0:T(8,128)(2,1)S(1)} %get-tuple-element.267.refs_0_), channel_id=1, source_target_pairs={{0,16},{4,20},{8,24},{12,28},{16,0},{20,4},{24,8},{28,12},{1,17},{... | collective-permute-start | bytes 3932168 | tf_op jit(solution)/shard_map/ppermute | solution.py:373
  394.0 63.2 %collective-permute-start.22 = (bf16[256,2560]{1,0:T(8,128)(2,1)}, bf16[256,2560]{1,0:T(8,128)(2,1)S(1)}, u32[]{:S(2)}, u32[]{:S(2)}) collective-permute-start(bf16[256,2560]{1,0:T(8,128)(2,1)} %collective-permute-done.19.refs_0_), channel_id=1, source_target_pairs={{0,16},{4,20},{8,24},{12,28},{16,0},{20,4},{24,8},{28,12},{1,17},{... | collective-permute-start | bytes 3932168 | tf_op jit(solution)/shard_map/ppermute | solution.py:373
  394.1 63.2 %collective-permute-start.23 = (bf16[256,2560]{1,0:T(8,128)(2,1)S(1)}, bf16[256,2560]{1,0:T(8,128)(2,1)S(1)}, u32[]{:S(2)}, u32[]{:S(2)}) collective-permute-start(bf16[256,2560]{1,0:T(8,128)(2,1)S(1)} %get-tuple-element.269.refs_1_), channel_id=1, source_target_pairs={{0,8},{4,12},{8,0},{12,4},{16,24},{20,28},{24,16},{28,20},{1,9},{5... | collective-permute-start | bytes 3932168 | tf_op jit(solution)/shard_map/ppermute | solution.py:373
  573.3 257.5 %reduce-scatter.6.cloned.1.call-start = ((), (), s32[]{:S(2)}) async-start(), calls=%async_computation.6 | async-start | bytes 5324800 | tf_op jit(solution)/shard_map/reduce_scatter | solution.py:656
  701.4 168.8 %reduce-scatter.8.cloned.1.call-start = ((), (), s32[]{:S(2)}) async-start(), calls=%async_computation.7 | async-start | bytes 5324800 | tf_op jit(solution)/shard_map/reduce_scatter | solution.py:656
  763.5 405.5 %all-gather.13.cloned.1.call-start = ((), (), s32[]{:S(2)}) async-start(), calls=%async_computation.8 | async-start | bytes 5120000 | tf_op jit(solution)/shard_map/all_gather | solution.py:678
  903.0 314.3 %all-gather.15.cloned.1.call-start = ((), (), s32[]{:S(2)}) async-start(), calls=%async_computation.9 | async-start | bytes 10240000 | tf_op jit(solution)/shard_map/all_gather | solution.py:694
  994.0 65.0 %collective-permute-start.51 = (bf16[4,128,5120]{2,1,0:T(8,128)(2,1)}, bf16[4,128,5120]{2,1,0:T(8,128)(2,1)}, u32[]{:S(2)}, u32[]{:S(2)}) collective-permute-start(bf16[4,128,5120]{2,1,0:T(8,128)(2,1)} %dynamic-slice_bitcast_fusion.1), channel_id=1, source_target_pairs={{0,4},{4,0},{8,12},{12,8},{16,20},{20,16},{24,28},{28,24},{1,5},{5... | collective-permute-start | bytes 15728648 | tf_op jit(solution)/shard_map/ppermute | solution.py:373
  994.0 395.1 %all-reduce.16.cloned.1.call-start = ((), (), s32[]{:S(2)}) async-start(), calls=%async_computation.12 | async-start | bytes 5898240 | tf_op jit(solution)/shard_map/psum | solution.py:707
  997.2 113.5 %collective-permute-start.50 = (bf16[512,384]{1,0:T(8,128)(2,1)}, bf16[512,384]{1,0:T(8,128)(2,1)}, u32[]{:S(2)}, u32[]{:S(2)}) collective-permute-start(bf16[512,384]{1,0:T(8,128)(2,1)} %get-tuple-element.565), channel_id=1, source_target_pairs={{0,3},{1,0},{2,1},{3,2},{4,7},{5,4},{6,5},{7,6},{8,11},{9,8},{10,9... | collective-permute-start | bytes 1179656 | tf_op jit(solution)/shard_map/ppermute | solution.py:453
  1101.6 64.9 %collective-permute-start.55 = (bf16[64,5120]{1,0:T(8,128)(2,1)S(1)}, bf16[64,5120]{1,0:T(8,128)(2,1)S(1)}, u32[]{:S(2)}, u32[]{:S(2)}) collective-permute-start(bf16[64,5120]{1,0:T(8,128)(2,1)S(1)} %copy-done.93), channel_id=1, source_target_pairs={{0,8},{4,12},{8,0},{12,4},{16,24},{20,28},{24,16},{28,20},{1,9},{5... | collective-permute-start | bytes 1966088 | tf_op jit(solution)/shard_map/ppermute | solution.py:373
  1268.9 165.5 %all-reduce.14.cloned.1.call-start = ((), (), s32[]{:S(2)}) async-start(), calls=%async_computation.10 | async-start | bytes 1548288 | tf_op jit(solution)/shard_map/psum | solution.py:729
  1282.0 92.3 %collective-permute-start.65 = (bf16[256,2560]{1,0:T(8,128)(2,1)}, bf16[256,2560]{1,0:T(8,128)(2,1)}, u32[]{:S(2)}, u32[]{:S(2)}) collective-permute-start(bf16[256,2560]{1,0:T(8,128)(2,1)} %copy-done.49), channel_id=1, source_target_pairs={{0,16},{4,20},{8,24},{12,28},{16,0},{20,4},{24,8},{28,12},{1,17},{... | collective-permute-start | bytes 3932168 | tf_op jit(solution)/shard_map/ppermute | solution.py:373
  1282.6 91.6 %collective-permute-start.66 = (bf16[256,2560]{1,0:T(8,128)(2,1)}, bf16[256,2560]{1,0:T(8,128)(2,1)}, u32[]{:S(2)}, u32[]{:S(2)}) collective-permute-start(bf16[256,2560]{1,0:T(8,128)(2,1)} %copy-done.48), channel_id=1, source_target_pairs={{0,8},{4,12},{8,0},{12,4},{16,24},{20,28},{24,16},{28,20},{1,9},{5... | collective-permute-start | bytes 3932168 | tf_op jit(solution)/shard_map/ppermute | solution.py:373
  1288.4 85.9 %collective-permute-start.67 = (bf16[256,2560]{1,0:T(8,128)(2,1)}, bf16[256,2560]{1,0:T(8,128)(2,1)}, u32[]{:S(2)}, u32[]{:S(2)}) collective-permute-start(bf16[256,2560]{1,0:T(8,128)(2,1)} %copy-done.47), channel_id=1, source_target_pairs={{0,16},{4,20},{8,24},{12,28},{16,0},{20,4},{24,8},{28,12},{1,17},{... | collective-permute-start | bytes 3932168 | tf_op jit(solution)/shard_map/ppermute | solution.py:373
  1289.2 85.0 %collective-permute-start.68 = (bf16[256,2560]{1,0:T(8,128)(2,1)}, bf16[256,2560]{1,0:T(8,128)(2,1)}, u32[]{:S(2)}, u32[]{:S(2)}) collective-permute-start(bf16[256,2560]{1,0:T(8,128)(2,1)} %copy-done.46), channel_id=1, source_target_pairs={{0,8},{4,12},{8,0},{12,4},{16,24},{20,28},{24,16},{28,20},{1,9},{5... | collective-permute-start | bytes 3932168 | tf_op jit(solution)/shard_map/ppermute | solution.py:373
  1377.4 65.0 %collective-permute-start.70 = (bf16[256,2560]{1,0:T(8,128)(2,1)}, bf16[256,2560]{1,0:T(8,128)(2,1)}, u32[]{:S(2)}, u32[]{:S(2)}) collective-permute-start(bf16[256,2560]{1,0:T(8,128)(2,1)} %add_convert_fusion.3), channel_id=1, source_target_pairs={{0,16},{4,20},{8,24},{12,28},{16,0},{20,4},{24,8},{28,12},{1,17},{... | collective-permute-start | bytes 3932168 | tf_op jit(solution)/shard_map/ppermute | solution.py:373
  (187 other events, 4059.7 us)
Sparse Core Ops, SparseCore 0:
  10.5 46.6 all-gather.8
  59.6 63.2 all-gather.16
  124.8 121.8 all-gather.10
  573.4 86.1 reduce-scatter.3
  701.5 88.1 reduce-scatter.5
  791.9 78.3 reduce-scatter.7
  903.1 112.8 all-gather.12
  1017.7 199.5 all-gather.14
  1269.1 120.0 all-reduce.15
  1391.9 42.5 all-reduce.13

commit v3 on v2

--- a/solution.py
+++ b/solution.py
@@ -50,18 +50,19 @@
             key_index = first + lax.broadcasted_iota(jnp.int32, (size, rows), 0)
             own = bounds[3] + lax.broadcasted_iota(jnp.int32, (size, rows), 1)
             allowed = (key_index <= own) & ((key_index >= start[...]) | (key_index < PROMPT))
+        scores, vals = [], []
         for h in range(2):
             kv_h = kv[:, h * LANES:(h + 1) * LANES]
             key = jnp.where(low_half, kv_h, rope_rows)
-            val = jnp.where(low_half, jnp.ones_like(kv_h), kv_h)
+            vals.append(jnp.where(low_half, jnp.ones_like(kv_h), kv_h))
             s = dot(key, q_out[:, h * LANES:(h + 1) * LANES], 1, 1)
-            if masked:
-                s = jnp.where(allowed, s, NEG)
+            scores.append(jnp.where(allowed, s, NEG) if masked else s)
+        for h in range(2):
             m_old = m_scr[h:h + 1, :]
-            m_new = jnp.maximum(m_old, jnp.max(s, axis=0, keepdims=True))
-            p = jnp.exp2(s - m_new)
+            m_new = jnp.maximum(m_old, jnp.max(scores[h], axis=0, keepdims=True))
             m_scr[h:h + 1, :] = m_new
-            acc_scr[h] = acc_scr[h] * jnp.exp2(m_old - m_new) + dot(val, p.astype(jnp.bfloat16), 0, 0)
+            p = jnp.exp2(scores[h] - m_new).astype(jnp.bfloat16)
+            acc_scr[h] = acc_scr[h] * jnp.exp2(m_old - m_new) + dot(vals[h], p, 0, 0)
 
     lax.fori_loop(0, bounds[0], lambda i, c: (block(pl.multiple_of(i * full_rows, full_rows), full_rows, False), c)[1], 0)
     lax.fori_loop(bounds[1], bounds[2], lambda i, c: (block(pl.multiple_of(i * mask_rows, mask_rows), mask_rows, True), c)[1], 0)
@@ -270,7 +271,9 @@
         out_shape=[jax.ShapeDtypeStruct((all_rows, hidden), jnp.bfloat16)] * 3,
         input_output_aliases={2 * count + 3 + i: i for i in range(len(prev))},
         compiler_params=pltpu.CompilerParams(vmem_limit_bytes=48 << 20),
-        cost_estimate=LIGHT,
+        cost_estimate=pl.CostEstimate(
+            flops=6 * rows * width * hidden, bytes_accessed=6 * width * hidden + 8 * rows * width, transcendentals=0
+        ),
         name="hidden_units",
     )(*normed, *grads, gate_w, up_w, down_w, *prev)
 
@@ -395,7 +398,8 @@
     return steps
 
 
-ATTEND_PARTS = ((0, 4), (4, 5), (9, 6), (15, HEADS // 2 - 15))
+BACK_PARTS = ((0, 12), (12, 4), (16, HEADS // 2 - 16))
+ATTEND_PARTS = ((0, 4), (4, 7), (11, 7), (18, HEADS // 2 - 18))
 
 
 def own_blocks(tensor):
@@ -579,32 +583,38 @@
 
     fetched_blocks = [swap(block, 2 * r, n) if r else block for r, block in enumerate(own_fetch)]
     outputs = attend_forward(ATTEND_PARTS[0], [], [], *forward_args)
-    outputs, fetched_blocks, grad_low = tie(outputs, fetched_blocks, grad_low)
+    grad_blocks = own_blocks(grad_low)
+    moved = gather_step(grad_blocks, n, 0)
+    outputs, fetched_blocks = tie(outputs, fetched_blocks)
     fetched = blank((2, chips, fetch, ff_sent))
     for r, block in enumerate(fetched_blocks):
         fetched = lax.dynamic_update_slice(fetched, block[:, None], (0, chip ^ r, 0, 0))
-    grad_blocks = own_blocks(grad_low)
     passed = [(fetched, fetched)]
     for step in range(1, layers):
         link = (
             lax.ppermute(passed[-1][0], "seq", [(i, i + 1) for i in range(layers - 1)]),
             lax.ppermute(passed[-1][1], "seq", [(i + 1, i) for i in range(layers - 1)]),
         )
-        moved = gather_step(grad_blocks, n, step - 1) if step < len(steps) else {}
         if step < len(ATTEND_PARTS):
             outputs = attend_forward(ATTEND_PARTS[step], outputs, [], *forward_args)
-            outputs, link, moved = tie(outputs, link, moved)
+            if step < layers - 1:
+                outputs, link = tie(outputs, link)
+            if step == 1:
+                outputs, moved = tie(outputs, moved)
+                grad_blocks = {**grad_blocks, **moved}
         passed.append(link)
-        grad_blocks = {**grad_blocks, **moved}
     for part in ATTEND_PARTS[layers:]:
         outputs = attend_forward(part, outputs, [], *forward_args)
     attended, queries, log_total = outputs
+    for at in range(1, len(steps) - 1):
+        grad_blocks = {**grad_blocks, **gather_step(grad_blocks, n, at)}
     attn_branch = jnp.dot(attended, out_proj_all, preferred_element_type=F32)
+    attn_branch, grad_blocks = tie(attn_branch, grad_blocks)
     middle = token_rows + depth_scale * attn_branch
     mlp_float, mlp_inverse = rms_forward(middle, mlp_gain_all)
     normed_blocks = own_blocks(mlp_float.astype(BF16))
     normed_blocks = {**normed_blocks, **gather_step(normed_blocks, n, 0)}
-    normed_blocks, passed, grad_blocks = tie(normed_blocks, passed, grad_blocks)
+    normed_blocks, passed = tie(normed_blocks, passed)
     layer_blocks = [jnp.where(layer >= shift, passed[shift][0], passed[layers - shift][1]) for shift in range(1, layers)]
     for at in range(1, len(steps) - 1):
         normed_blocks = {**normed_blocks, **gather_step(normed_blocks, n, at)}
@@ -629,20 +639,19 @@
     all_grad = jnp.concatenate([grad_blocks[key] for step in steps for key in step])
 
     back = lambda i, hidden: dict(zip(steps[i], to_tokens(first_rows[i], half, len(steps[i]), hidden, [gate_w, up_w], 1)))
-    down_whole = dot(active, all_grad, 0, 0).astype(BF16)
-    down_whole, grad_gate, grad_up = tie(down_whole, grad_gate, grad_up)
     last_blocks = back(-1, [grad_gate, grad_up])
+    last_blocks, active_late, earlier = tie(last_blocks, active, [grad_gate, grad_up])
+    down_whole = dot(active_late, all_grad, 0, 0).astype(BF16)
     last_blocks, earlier = tie(last_blocks, [grad_gate, grad_up])
     half_ff = ff_chip // 2
     half_of = lambda at: lax.dynamic_slice_in_dim(down_whole, at * half_ff, half_ff, 0)
     down_part = (half_of(core).astype(F32) + swap(half_of(1 - core), 1, n).astype(F32)).astype(BF16)
-    last_blocks, down_part, earlier = tie(last_blocks, down_part, [grad_gate, grad_up])
-    down_share = lax.psum_scatter(down_part, "seq", scatter_dimension=0, tiled=True)
     early_blocks = {}
     for i in range(len(steps) - 1)[::-1]:
         early_blocks.update(back(i, earlier))
     blocks, _ = scatter_step({**last_blocks, **early_blocks}, n, len(steps) - 2)
-    blocks, all_normed = tie(blocks, all_normed)
+    blocks, all_normed, down_part = tie(blocks, all_normed, down_part)
+    down_share = lax.psum_scatter(down_part, "seq", scatter_dimension=0, tiled=True)
     hidden_parts, hidden_shares, crossing = [], [], []
     for grads in (grad_gate, grad_up):
         whole = dot(all_normed, grads, 0, 0).astype(BF16).reshape(chips, 2, layers, fetch, ff_wide)
@@ -671,41 +680,31 @@
     )
     out_shares = core_shares(out_proj_part, n)
     out_arrived = swap(pick(out_shares, 1 - core), 1, n)
-    thirds = ((0, 12), (12, 4), (16, HEADS // 2 - 16))
-    first = attend_backward(thirds[0], [], [*hidden_parts, out_proj_part], *backward_args)
-    first, out_arrived = tie(first, out_arrived)
+    first = attend_backward(BACK_PARTS[0], [], [*hidden_parts, out_proj_part], *backward_args)
+    down_low = lax.all_gather(down_share, "seq", axis=0, tiled=True)
+    first, hidden_shares, down_share, out_arrived = tie(first, hidden_shares, down_share, out_arrived)
     out_mine = (pick(out_shares, core).astype(F32) + out_arrived.astype(F32)).astype(BF16)
-    down_low = lax.all_gather(down_share, "seq", axis=0, tiled=True)
-    second = attend_backward(thirds[1], first, [down_share, *hidden_shares], *backward_args)
+    first, out_mine = tie(first, out_mine)
     hidden_share = jnp.stack(hidden_shares)
-    hidden_blocks = []
-    for r in range(0, n, 2):
-        block = pick(hidden_share, chip ^ (r // 2), 1)
-        hidden_blocks.append(swap(block, r, n) if r else block)
+    hidden_blocks = [pick(hidden_share, chip ^ (r // 2), 1) for r in range(0, n, 2)]
+    hidden_blocks = [swap(block, 2 * r, n) if r else block for r, block in enumerate(hidden_blocks)]
+    second = attend_backward(BACK_PARTS[1], first, [down_share], *backward_args)
     second, hidden_blocks = tie(second, hidden_blocks)
     hidden_blocks = jnp.stack(hidden_blocks)
     hidden_blocks = [pick(hidden_blocks, chip ^ c)[..., :ff_chip] for c in range(chips)]
-    placed = jnp.concatenate([block[at] for at in range(2) for block in hidden_blocks], axis=1)
-    out_blocks, second = scatter_step(chip_blocks(out_mine, chip, n), n, len(steps) - 2, second)
-    third = attend_backward(thirds[2], second, [placed], *backward_args)
+    placed = [jnp.concatenate([block[at] for block in hidden_blocks], axis=1) for at in range(2)]
+    gate_low, up_low = (lax.all_gather(v, "seq", axis=0, tiled=True) for v in placed)
+    third = attend_backward(BACK_PARTS[2], second, placed, *backward_args)
+    out_blocks, third = scatter_step(chip_blocks(out_mine, chip, n), n, len(steps) - 2, third)
     for at in range(len(steps) - 2)[::-1]:
-        out_blocks, third = scatter_step(out_blocks, n, at, third)
+        out_blocks, _ = scatter_step(out_blocks, n, at)
     out_share = jnp.concatenate([out_blocks[0, part] for part in range(2)]).astype(BF16)
-    gate_up_low = lax.all_gather(placed, "seq", axis=0, tiled=True)
     q_up_part, kv_up_part, grad_kv_all, grad_rope_all, grad_q_lat = third
     grad_q_float, q_gain_part = rms_backward(q_latent, q_inverse, q_gain_all, grad_q_lat)
     grad_kv = seq_scatter(jnp.concatenate([grad_kv_all, grad_rope_all], axis=1).astype(BF16), layer, layers)
+    grad_kv, gate_low, down_low = tie(grad_kv, gate_low, down_low)
     up_parts = jnp.concatenate([q_up_part, kv_up_part], axis=1).reshape(-1, HEADS * LANES)
     up_share = fsdp_scatter(up_parts, core, chip, n).astype(BF16)
-    grad_kv, active_last = tie(grad_kv, active)
-    branch = {}
-    for step, at in zip(steps, first_rows):
-        branch.update(zip(step, to_tokens(at, half, len(step), [active_last], [down_w], 0)))
-    grad_kv, up_share, out_share, down_low, gate_up_low, branch = tie(
-        grad_kv, up_share, out_share, down_low, gate_up_low, branch
-    )
-    up_grad, out_proj_grad = lax.psum((up_share, out_share), "seq")
-    down_grad, gate_up_grad = down_low.astype(F32), gate_up_low.astype(F32)
     grad_kv_first, kv_gain_part = rms_backward(kv_latent, kv_inverse, kv_gain_all, grad_kv[:, :rank_kv])
     grad_rope = rotate(grad_kv[:, rank_kv + NOPE : rank_kv + NOPE + ROPE], cosine, -sine)
     grad_latent = jnp.concatenate([grad_q_float, grad_kv_first, grad_rope], axis=1).astype(BF16)
@@ -720,14 +719,14 @@
     down_rows = D // n
     down_all_part = jnp.concatenate([down_all_part.reshape(n, down_rows, -1), gain_rows], axis=1)
     down_all_share = fsdp_scatter(down_all_part.reshape(-1, latent.shape[1]), core, chip, n).astype(BF16)
-    branch, down_all_share = scatter_step(branch, n, len(steps) - 2, down_all_share)
-    for at in range(len(steps) - 2)[::-1]:
-        branch, _ = scatter_step(branch, n, at)
-    mlp_branch = jnp.concatenate([branch[0, part] for part in range(2)])
-    output = (middle + depth_scale * mlp_branch).astype(BF16).reshape(block_input.shape)
-    up_grad, out_proj_grad, down_all_share = tie(up_grad, out_proj_grad, down_all_share)
-    down_all_grad = lax.psum(down_all_share, "seq").astype(F32)
-    up_grad, out_proj_grad = up_grad.astype(F32), out_proj_grad.astype(F32)
+    up_share, out_share, down_all_share, up_low, active_last = tie(up_share, out_share, down_all_share, up_low, active)
+    up_grad, out_proj_grad, down_all_grad = (v.astype(F32) for v in lax.psum((up_share, out_share, down_all_share), "seq"))
+    branch = {}
+    for step, at in zip(steps, first_rows):
+        branch.update(zip(step, to_tokens(at, half, len(step), [active_last], [down_w], 0)))
+    down_grad = down_low.astype(F32)
+    gate_up_grad = jnp.concatenate([gate_low, up_low], axis=1).astype(F32)
+    output = (middle + depth_scale * chip_scatter(branch, n)).astype(BF16).reshape(block_input.shape)
     gain_sum = down_all_grad[down_rows]
     down_all_grad = down_all_grad[:down_rows]
     q_up_grad = up_grad[:q_rows].reshape(-1, HEADS, LANES)[..., : NOPE + ROPE].reshape(-1, HEADS * (NOPE + ROPE))

time: 1470 us -> 1370 us (0.932)
  waiting for transfers between devices: 508 us -> 455 us
  local copies, waits for them, and re-layouts: 173 us -> 138 us
    ppermute x59, waiting for transfers between devices: 301 us -> 216 us  [swap(): return lax.ppermute(tensor, 'fsdp', [(i, i ^ bit) for i in range(n)])]
    all_gather x1 -> x2, waiting for transfers between devices: 48.2 us -> 0.01 us  [body(): lax.all_gather(v, 'seq', axis=0, tiled=True)]
    unnamed x290 -> x215, local copies, waits for them, and re-layouts: 78.3 us -> 50 us
    ppermute x3, waiting for transfers between devices: 19.3 us -> 46.4 us  [body(): lax.ppermute(passed[-1][0], 'seq', [(i, i + 1) for i in range(layers - 1)])]
    reduce_scatter x1, waiting for transfers between devices: 0.01 us -> 22.9 us  [body(): lax.psum_scatter(down_part, 'seq', scatter_dimension=0, tiled=True)]
    ppermute x3, waiting for transfers between devices: 11.8 us -> 30.2 us  [seq_scatter(): lax.ppermute(pick(shares, (layer + shift) % layers), 'seq', ring(shift, l...]
    psum x2 -> x1, waiting for transfers between devices: 41.5 us -> 57.4 us  [body(): lax.psum((up_share, out_share, down_all_share), 'seq')]
  transfers between devices with their start and end apart: 81 -> 81, of which waited for: 33 -> 32; matrix products, arithmetic and copies ran while one was open for 23% -> 28% of each run, Pallas kernels for 18% -> 16%
where the time goes in v3:
time: 1370 us; the launch traced here: 1360 us
  waiting for transfers between devices  455 us (33%)
  Pallas kernels  297 us (22%)
  other arithmetic  166 us (12%)
  starting transfers between devices  145 us (11%)
  local copies, waits for them, and re-layouts  138 us (10%)
  matrix products  128 us (9%)
  between operations  21 us (2%)
    ppermute x59, waiting for transfers between devices, swap(): return lax.ppermute(tensor, 'fsdp', [(i, i ^ bit) for i in range(n)])  216 us
    dot_general x7, matrix products, dot(): lax.dot_general(a, b, (((ca,), (cb,)), ((), ())), preferred_element_type=...  111 us
    pallas_call x6, Pallas kernels, to_tokens(): pl.pallas_call(functools.partial(back_kernel, terms=len(left), contract=c...  92.7 us
    pallas_call x3, Pallas kernels, attend_backward(): pl.pallas_call(functools.partial(bwd_kernel, full_rows=full_rows, mask_ro...  77.4 us
    pallas_call x3, Pallas kernels, hidden_units(): pl.pallas_call(functools.partial(hidden_kernel, count=count), grid=(pl.cd...  75.3 us
    ppermute x3, starting transfers between devices, seq_scatter(): lax.ppermute(pick(shares, (layer + shift) % layers), 'seq', ring(shift, l...  64.9 us
    psum x1, waiting for transfers between devices, body(): lax.psum((up_share, out_share, down_all_share), 'seq')  57.4 us
    ppermute x59, starting transfers between devices, swap(): return lax.ppermute(tensor, 'fsdp', [(i, i ^ bit) for i in range(n)])  56.2 us
  transfers between devices with their start and end apart: 81, of which 32 were waited for; matrix products, arithmetic and copies ran while one was open for 28% of the time, Pallas kernels for 16%

profile of v3, /device:TPU:0, one launch (start us, length us, event | category | flops | bytes accessed | tf_op | source)
XLA Modules:
  0.0 1361.3 jit_solution(3120041588603254261)
XLA Ops:
  102.1 20.8 %all-gather.20.cloned.1.call-done = bf16[1024,5120]{1,0:T(8,128)(2,1)} async-done(((bf16[128,5120]{1,0:T(8,128)(2,1)}), bf16[1024,5120]{1,0:T(8,128)(2,1)}) %all-gather.20.cloned.1.call-update) | async-done | bytes 10485776 | tf_op jit(solution)/shard_map/all_gather | solution.py:544
  144.4 18.0 %collective-permute-done.6 = bf16[2,80,1664]{2,1,0:T(8,128)(2,1)} collective-permute-done((bf16[2,80,1664]{2,1,0:T(8,128)(2,1)}, bf16[2,80,1664]{2,1,0:T(8,128)(2,1)}, u32[]{:S(2)}, u32[]{:S(2)}) %collective-permute-start.6) | collective-permute-done | bytes 532512 | tf_op jit(solution)/shard_map/ppermute | solution.py:376
  192.1 24.4 %collective-permute-done.7 = bf16[2,4,80,1664]{3,2,1,0:T(8,128)(2,1)} collective-permute-done((bf16[2,4,80,1664]{3,2,1,0:T(8,128)(2,1)}, bf16[2,4,80,1664]{3,2,1,0:T(8,128)(2,1)}, u32[]{:S(2)}, u32[]{:S(2)}) %collective-permute-start.7) | collective-permute-done | bytes 2129952 | tf_op jit(solution)/shard_map/ppermute | solution.py:595
  235.5 21.8 %collective-permute-done.9.refs_2_ = bf16[256,2560]{1,0:T(8,128)(2,1)} collective-permute-done((bf16[256,2560]{1,0:T(8,128)(2,1)}, bf16[256,2560]{1,0:T(8,128)(2,1)}, u32[]{:S(2)}, u32[]{:S(2)}) %collective-permute-start.9) | collective-permute-done | bytes 1310752 | tf_op jit(solution)/shard_map/ppermute | solution.py:376
  343.6 22.0 %collective-permute-done.19 = bf16[2,4,80,1664]{3,2,1,0:T(8,128)(2,1)S(1)} collective-permute-done((bf16[2,4,80,1664]{3,2,1,0:T(8,128)(2,1)}, bf16[2,4,80,1664]{3,2,1,0:T(8,128)(2,1)S(1)}, u32[]{:S(2)}, u32[]{:S(2)}) %collective-permute-start.19) | collective-permute-done | bytes 2129952 | tf_op jit(solution)/shard_map/ppermute | solution.py:595
  379.9 21.8 %collective-permute-done.21.refs_0_ = bf16[256,2560]{1,0:T(8,128)(2,1)S(1)} collective-permute-done((bf16[256,2560]{1,0:T(8,128)(2,1)S(1)}, bf16[256,2560]{1,0:T(8,128)(2,1)S(1)}, u32[]{:S(2)}, u32[]{:S(2)}) %collective-permute-start.21) | collective-permute-done | bytes 1310752 | tf_op jit(solution)/shard_map/ppermute | solution.py:376
  412.3 20.0 %hidden_units.3 = (bf16[2048,1664]{1,0:T(8,128)(2,1)}, bf16[2048,1664]{1,0:T(8,128)(2,1)}, bf16[2048,1664]{1,0:T(8,128)(2,1)}) custom-call(bf16[256,2560]{1,0:T(8,128)(2,1)S(1)} %get-tuple-element.240.refs_0_, bf16[256,2560]{1,0:T(8,128)(2,1)S(1)} %get-tuple-element.242.refs_1_, bf16[256,2560]{1,0:T(8,128)(2,1)} %get-tuple-element.257.refs_2_, ...), custom_call_target="tpu_custom_call" | custom-call | flops 13086228480 | bytes 36044800 | tf_op jit(solution)/shard_map/hidden_units/pallas_call | solution.py:263
  432.3 20.1 %hidden_units.4 = (bf16[2048,1664]{1,0:T(8,128)(2,1)}, bf16[2048,1664]{1,0:T(8,128)(2,1)}, bf16[2048,1664]{1,0:T(8,128)(2,1)}) custom-call(bf16[256,2560]{1,0:T(8,128)(2,1)S(1)} %collective-permute-done.17.refs_0_, bf16[256,2560]{1,0:T(8,128)(2,1)S(1)} %collective-permute-done.18.refs_1_, ...), custom_call_target="tpu_custom_call", output_to_operand_aliasing={{0}: (7, {}), {1}: (8, {}), {2}: (9, {})} | custom-call | flops 13086228480 | bytes 36044800 | tf_op jit(solution)/shard_map/hidden_units/pallas_call | solution.py:263
  452.4 35.2 %hidden_units.5 = (bf16[2048,1664]{1,0:T(8,128)(2,1)}, bf16[2048,1664]{1,0:T(8,128)(2,1)}, bf16[2048,1664]{1,0:T(8,128)(2,1)}) custom-call(bf16[256,2560]{1,0:T(8,128)(2,1)S(1)} %collective-permute-done.21.refs_0_, bf16[256,2560]{1,0:T(8,128)(2,1)S(1)} %collective-permute-done.22.refs_1_, ...), custom_call_target="tpu_custom_call", output_to_operand_aliasing={{0}: (11, {}), {1}: (12, {}), {2}: (13, {})} | custom-call | flops 26172456960 | bytes 46530560 | tf_op jit(solution)/shard_map/hidden_units/pallas_call | solution.py:263
  487.7 24.9 %to_tokens.6 = (bf16[256,2560]{1,0:T(8,128)(2,1)S(1)}, bf16[256,2560]{1,0:T(8,128)(2,1)S(1)}, bf16[256,2560]{1,0:T(8,128)(2,1)S(1)}, bf16[256,2560]{1,0:T(8,128)(2,1)S(1)}) custom-call(bf16[2048,1664]{1,0:T(8,128)(2,1)} %get-tuple-element.276.refs_0_, bf16[2048,1664]{1,0:T(8,128)(2,1)} %get-tuple-element.277.refs_1_, ...), custom_call_target="tpu_custom_call" | custom-call | flops 1048576 | bytes 65536 | tf_op jit(solution)/shard_map/to_tokens/pallas_call | solution.py:302
  513.0 22.3 %convolution_convert_fusion.3 = bf16[1664,2560]{1,0:T(8,128)(2,1)S(1)} fusion(bf16[2048,1664]{1,0:T(8,128)(2,1)} %get-tuple-element.354.refs_0_, bf16[2048,2560]{1,0:T(8,128)(2,1)} %copy-done.64), kind=kOutput, calls=%fused_computation.7 | convolution fusion | flops 17452564480 | bytes 25821184 | tf_op jit(solution)/shard_map/dot_general | solution.py:24
  579.9 18.2 %collective-permute-done.30 = bf16[256,2560]{1,0:T(8,128)(2,1)S(1)} collective-permute-done((bf16[256,2560]{1,0:T(8,128)(2,1)S(1)}, bf16[256,2560]{1,0:T(8,128)(2,1)S(1)}, u32[]{:S(2)}, u32[]{:S(2)}) %collective-permute-start.30) | collective-permute-done | bytes 1310752 | tf_op jit(solution)/shard_map/ppermute | solution.py:376
  606.5 25.1 %convolution_convert_fusion.2 = bf16[2560,1664]{1,0:T(8,128)(2,1)} fusion(bf16[2048,2560]{1,0:T(8,128)(2,1)} %constant_dynamic-update-slice_fusion, bf16[2048,1664]{1,0:T(8,128)(2,1)} %get-tuple-element.276.refs_0_), kind=kOutput, calls=%fused_computation.6 | convolution fusion | flops 17452564480 | bytes 25821184 | tf_op jit(solution)/shard_map/dot_general | solution.py:24
  641.9 25.5 %collective-permute-done.34 = bf16[256,2560]{1,0:T(8,128)(2,1)S(1)} collective-permute-done((bf16[256,2560]{1,0:T(8,128)(2,1)S(1)}, bf16[256,2560]{1,0:T(8,128)(2,1)S(1)}, u32[]{:S(2)}, u32[]{:S(2)}) %collective-permute-start.34) | collective-permute-done | bytes 1310752 | tf_op jit(solution)/shard_map/ppermute | solution.py:376
  669.6 22.9 %reduce-scatter.4.cloned.1.call-done.rest_2_ = bf16[200,2560]{1,0:T(8,128)(2,1)} async-done(((bf16[800,2560]{1,0:T(8,128)(2,1)}), bf16[200,2560]{1,0:T(8,128)(2,1)}) %reduce-scatter.4.cloned.1.call-update) | async-done | bytes 1024016 | tf_op jit(solution)/shard_map/reduce_scatter | solution.py:654
  699.1 25.6 %convolution_convert_fusion.1 = bf16[2560,1664]{1,0:T(8,128)(2,1)} fusion(bf16[2048,2560]{1,0:T(8,128)(2,1)} %constant_dynamic-update-slice_fusion, bf16[2048,1664]{1,0:T(8,128)(2,1)} %get-tuple-element.277.refs_1_), kind=kOutput, calls=%fused_computation.5 | convolution fusion | flops 17452564480 | bytes 25821184 | tf_op jit(solution)/shard_map/dot_general | solution.py:24
  786.2 41.2 %attend_backward.3 = (bf16[8,96,5120]{2,1,0:T(8,128)(2,1)}, bf16[8,32,5120]{2,1,0:T(8,128)(2,1)}, f32[2048,256]{1,0:T(8,128)}, f32[2048,128]{1,0:T(8,128)S(1)}, f32[512,768]{1,0:T(8,128)}) custom-call(s32[4]{0:T(128)S(1)} %pad_add_fusion.bounds, bf16[768,512]{1,0:T(8,128)(2,1)S(1)} %copy-done.8, bf16[8,128,5120]{2,1,0:T(8,128)(2,1)} %bitcast.403, ...), custom_call_target="tpu_custom_call" | custom-call | flops 1048576 | bytes 65536 | tf_op jit(solution)/shard_map/attend_backward/pallas_call | solution.py:190
  828.4 29.7 %reduce-scatter.8.cloned.1.call-done = bf16[1,4,80,1664]{3,2,1,0:T(8,128)(2,1)} async-done(((bf16[4,4,80,1664]{3,2,1,0:T(8,128)(2,1)}), bf16[1,4,80,1664]{3,2,1,0:T(8,128)(2,1)}) %reduce-scatter.8.cloned.1.call-update) | async-done | bytes 1064976 | tf_op jit(solution)/shard_map/reduce_scatter | solution.py:665
  875.7 17.8 %attend_backward.4 = (bf16[8,96,5120]{2,1,0:T(8,128)(2,1)}, bf16[8,32,5120]{2,1,0:T(8,128)(2,1)}, f32[2048,256]{1,0:T(8,128)}, f32[2048,128]{1,0:T(8,128)S(1)}, f32[512,768]{1,0:T(8,128)}) custom-call(s32[4]{0:T(128)S(1)} %pad_add_fusion.bounds, bf16[768,512]{1,0:T(8,128)(2,1)S(1)} %copy-done.9, ...), custom_call_target="tpu_custom_call", output_to_operand_aliasing={{0}: (15, {}), {1}: (16, {})} | custom-call | flops 1048576 | bytes 65536 | tf_op jit(solution)/shard_map/attend_backward/pallas_call | solution.py:190
  911.7 18.3 %attend_backward.5 = (bf16[8,96,5120]{2,1,0:T(8,128)(2,1)}, bf16[8,32,5120]{2,1,0:T(8,128)(2,1)}, f32[2048,256]{1,0:T(8,128)}, f32[2048,128]{1,0:T(8,128)S(1)}, f32[512,768]{1,0:T(8,128)}) custom-call(s32[4]{0:T(128)S(1)} %pad_add_fusion.bounds, bf16[768,512]{1,0:T(8,128)(2,1)S(1)} %copy-done.9, ...), custom_call_target="tpu_custom_call", output_to_operand_aliasing={{0}: (15, {}), {1}: (16, {})} | custom-call | flops 1048576 | bytes 65536 | tf_op jit(solution)/shard_map/attend_backward/pallas_call | solution.py:190
  960.4 64.3 %collective-permute-start.57 = (bf16[512,384]{1,0:T(8,128)(2,1)}, bf16[512,384]{1,0:T(8,128)(2,1)}, u32[]{:S(2)}, u32[]{:S(2)}) collective-permute-start(bf16[512,384]{1,0:T(8,128)(2,1)} %get-tuple-element.526), channel_id=1, source_target_pairs={{0,3},{1,0},{2,1},{3,2},{4,7},{5,4},{6,5},{7,6},{8,11},{9,8},{10,9... | collective-permute-start | bytes 1179656 | tf_op jit(solution)/shard_map/ppermute | solution.py:457
  1040.0 24.8 %collective-permute-done.56 = bf16[512,384]{1,0:T(8,128)(2,1)} collective-permute-done((bf16[512,384]{1,0:T(8,128)(2,1)}, bf16[512,384]{1,0:T(8,128)(2,1)}, u32[]{:S(2)}, u32[]{:S(2)}) %collective-permute-start.56) | collective-permute-done | bytes 393248 | tf_op jit(solution)/shard_map/ppermute | solution.py:457
  1139.4 19.6 %collective-permute-done.60 = bf16[168,1056]{1,0:T(8,128)(2,1)S(1)} collective-permute-done((bf16[168,1056]{1,0:T(8,128)(2,1)S(1)}, bf16[168,1056]{1,0:T(8,128)(2,1)S(1)}, u32[]{:S(2)}, u32[]{:S(2)}) %collective-permute-start.60) | collective-permute-done | bytes 354848 | tf_op jit(solution)/shard_map/ppermute | solution.py:376
  1284.7 57.4 %all-reduce.13.cloned.1.call-done = (bf16[336,1056]{1,0:T(8,128)(2,1)}, bf16[128,5120]{1,0:T(8,128)(2,1)}, bf16[320,2560]{1,0:T(8,128)(2,1)}) async-done(((bf16[336,1056]{1,0:T(8,128)(2,1)}, bf16[128,5120]{1,0:T(8,128)(2,1)}, bf16[320,2560]{1,0:T(8,128)(2,1)}), (bf16[336,1056]{1,0:T(8,128)(2,1)}, bf16[128,5120]{1,0:T(8,128)(2,1)}, bf16[320,2560]{1,0:T(8,128)(2,1)})) %all-reduce.13.cloned.1.call-update) | async-done | bytes 3658768 | tf_op jit(solution)/shard_map/psum | solution.py:723
  (576 shorter events, 698.6 us)
Async XLA Ops:
  7.2 52.1 %all-gather.10.cloned.1.call-start = ((), (), s32[]{:S(2)}) async-start(), calls=%async_computation.3 | async-start | bytes 6635520 | tf_op jit(solution)/shard_map/all_gather | solution.py:541
  10.4 112.5 %all-gather.20.cloned.1.call-start = ((), (), s32[]{:S(2)}) async-start(), calls=%async_computation.11 | async-start | bytes 11796480 | tf_op jit(solution)/shard_map/all_gather | solution.py:544
  13.6 274.7 %all-gather.12.cloned.1.call-start = ((), (), s32[]{:S(2)}) async-start(), calls=%async_computation.4 | async-start | bytes 14745600 | tf_op jit(solution)/shard_map/all_gather | solution.py:545
  14.3 678.1 %reduce-scatter.4.cloned.1.call-start = ((), (), s32[]{:S(2)}) async-start(), calls=%async_computation.5 | async-start | bytes 5120000 | tf_op jit(solution)/shard_map/reduce_scatter | solution.py:654
  175.1 103.5 %collective-permute-start.25 = (bf16[2,4,80,1664]{3,2,1,0:T(8,128)(2,1)}, bf16[2,4,80,1664]{3,2,1,0:T(8,128)(2,1)}, u32[]{:S(2)}, u32[]{:S(2)}) collective-permute-start(bf16[2,4,80,1664]{3,2,1,0:T(8,128)(2,1)} %bitcast_dynamic-update-slice_fusion), channel_id=1, source_target_pairs={{0,4},{4,0},{8,12},{12,8},{16,20},{20,16},{24,28},{28,24},{1,5},{5... | collective-permute-start | bytes 6389768 | tf_op jit(solution)/shard_map/ppermute | solution.py:376
  222.0 59.7 %collective-permute-start.11 = (bf16[2,4,80,1664]{3,2,1,0:T(8,128)(2,1)}, bf16[2,4,80,1664]{3,2,1,0:T(8,128)(2,1)}, u32[]{:S(2)}, u32[]{:S(2)}) collective-permute-start(bf16[2,4,80,1664]{3,2,1,0:T(8,128)(2,1)} %collective-permute-done.7), channel_id=1, source_target_pairs={{0,1},{1,2},{2,3},{4,5},{5,6},{6,7},{8,9},{9,10},{10,11},{12,13},{... | collective-permute-start | bytes 6389768 | tf_op jit(solution)/shard_map/ppermute | solution.py:595
  225.4 56.5 %collective-permute-start.12 = (bf16[2,4,80,1664]{3,2,1,0:T(8,128)(2,1)}, bf16[2,4,80,1664]{3,2,1,0:T(8,128)(2,1)}, u32[]{:S(2)}, u32[]{:S(2)}) collective-permute-start(bf16[2,4,80,1664]{3,2,1,0:T(8,128)(2,1)} %collective-permute-done.8), channel_id=1, source_target_pairs={{1,0},{2,1},{3,2},{5,4},{6,5},{7,6},{9,8},{10,9},{11,10},{13,12},{... | collective-permute-start | bytes 6389768 | tf_op jit(solution)/shard_map/ppermute | solution.py:596
  370.5 81.9 %collective-permute-start.22 = (bf16[256,2560]{1,0:T(8,128)(2,1)S(1)}, bf16[256,2560]{1,0:T(8,128)(2,1)S(1)}, u32[]{:S(2)}, u32[]{:S(2)}) collective-permute-start(bf16[256,2560]{1,0:T(8,128)(2,1)S(1)} %collective-permute-done.17.refs_0_), channel_id=1, source_target_pairs={{0,16},{4,20},{8,24},{12,28},{16,0},{20,4},{24,8},{28,12},{1,17},{... | collective-permute-start | bytes 3932168 | tf_op jit(solution)/shard_map/ppermute | solution.py:376
  372.2 80.3 %collective-permute-start.23 = (bf16[256,2560]{1,0:T(8,128)(2,1)S(1)}, bf16[256,2560]{1,0:T(8,128)(2,1)S(1)}, u32[]{:S(2)}, u32[]{:S(2)}) collective-permute-start(bf16[256,2560]{1,0:T(8,128)(2,1)S(1)} %get-tuple-element.242.refs_1_), channel_id=1, source_target_pairs={{0,8},{4,12},{8,0},{12,4},{16,24},{20,28},{24,16},{28,20},{1,9},{5... | collective-permute-start | bytes 3932168 | tf_op jit(solution)/shard_map/ppermute | solution.py:376
  512.6 64.0 %collective-permute-start.31 = (bf16[256,2560]{1,0:T(8,128)(2,1)S(1)}, bf16[256,2560]{1,0:T(8,128)(2,1)S(1)}, u32[]{:S(2)}, u32[]{:S(2)}) collective-permute-start(bf16[256,2560]{1,0:T(8,128)(2,1)S(1)} %get-tuple-element.283), channel_id=1, source_target_pairs={{0,16},{4,20},{8,24},{12,28},{16,0},{20,4},{24,8},{28,12},{1,17},{... | collective-permute-start | bytes 3932168 | tf_op jit(solution)/shard_map/ppermute | solution.py:376
  537.7 62.3 %collective-permute-start.33 = (bf16[800,2560]{1,0:T(8,128)(2,1)}, bf16[800,2560]{1,0:T(8,128)(2,1)}, u32[]{:S(2)}, u32[]{:S(2)}) collective-permute-start(bf16[800,2560]{1,0:T(8,128)(2,1)} %constant_dynamic-slice_fusion.4), channel_id=1, source_target_pairs={{0,4},{4,0},{8,12},{12,8},{16,20},{20,16},{24,28},{28,24},{1,5},{5... | collective-permute-start | bytes 12288008 | tf_op jit(solution)/shard_map/ppermute | solution.py:376
  544.2 53.9 %collective-permute-start.30 = (bf16[256,2560]{1,0:T(8,128)(2,1)S(1)}, bf16[256,2560]{1,0:T(8,128)(2,1)S(1)}, u32[]{:S(2)}, u32[]{:S(2)}) collective-permute-start(bf16[256,2560]{1,0:T(8,128)(2,1)S(1)} %get-tuple-element.281), channel_id=1, source_target_pairs={{0,8},{4,12},{8,0},{12,4},{16,24},{20,28},{24,16},{28,20},{1,9},{5... | collective-permute-start | bytes 3932168 | tf_op jit(solution)/shard_map/ppermute | solution.py:376
  606.4 221.9 %reduce-scatter.6.cloned.1.call-start = ((), (), s32[]{:S(2)}) async-start(), calls=%async_computation.6 | async-start | bytes 5324800 | tf_op jit(solution)/shard_map/reduce_scatter | solution.py:665
  699.1 159.0 %reduce-scatter.8.cloned.1.call-start = ((), (), s32[]{:S(2)}) async-start(), calls=%async_computation.7 | async-start | bytes 5324800 | tf_op jit(solution)/shard_map/reduce_scatter | solution.py:665
  761.1 318.7 %all-gather.16.cloned.1.call-start = ((), (), s32[]{:S(2)}) async-start(), calls=%async_computation.9 | async-start | bytes 5120000 | tf_op jit(solution)/shard_map/all_gather | solution.py:684
  779.5 300.3 %all-gather.14.cloned.1.call-start = ((), (), s32[]{:S(2)}) async-start(), calls=%async_computation.8 | async-start | bytes 5120000 | tf_op jit(solution)/shard_map/all_gather | solution.py:696
  900.3 279.8 %all-gather.18.cloned.1.call-start = ((), (), s32[]{:S(2)}) async-start(), calls=%async_computation.10 | async-start | bytes 5120000 | tf_op jit(solution)/shard_map/all_gather | solution.py:696
  953.2 113.9 %collective-permute-start.46 = (bf16[4,128,5120]{2,1,0:T(8,128)(2,1)}, bf16[4,128,5120]{2,1,0:T(8,128)(2,1)}, u32[]{:S(2)}, u32[]{:S(2)}) collective-permute-start(bf16[4,128,5120]{2,1,0:T(8,128)(2,1)} %dynamic-slice_bitcast_fusion.1), channel_id=1, source_target_pairs={{0,4},{4,0},{8,12},{12,8},{16,20},{20,16},{24,28},{28,24},{1,5},{5... | collective-permute-start | bytes 15728648 | tf_op jit(solution)/shard_map/ppermute | solution.py:376
  953.3 388.8 %all-reduce.13.cloned.1.call-start = ((), (), s32[]{:S(2)}) async-start(), calls=%async_computation.12 | async-start | bytes 7446528 | tf_op jit(solution)/shard_map/psum | solution.py:723
  956.9 156.7 %collective-permute-start.53 = (bf16[160,2560]{1,0:T(8,128)(2,1)}, bf16[160,2560]{1,0:T(8,128)(2,1)}, u32[]{:S(2)}, u32[]{:S(2)}) collective-permute-start(bf16[160,2560]{1,0:T(8,128)(2,1)} %get-tuple-element.470), channel_id=1, source_target_pairs={{0,8},{4,12},{8,0},{12,4},{16,24},{20,28},{24,16},{28,20},{1,9},{5... | collective-permute-start | bytes 2457608 | tf_op jit(solution)/shard_map/ppermute | solution.py:376
  960.4 78.1 %collective-permute-start.57 = (bf16[512,384]{1,0:T(8,128)(2,1)}, bf16[512,384]{1,0:T(8,128)(2,1)}, u32[]{:S(2)}, u32[]{:S(2)}) collective-permute-start(bf16[512,384]{1,0:T(8,128)(2,1)} %get-tuple-element.526), channel_id=1, source_target_pairs={{0,3},{1,0},{2,1},{3,2},{4,7},{5,4},{6,5},{7,6},{8,11},{9,8},{10,9... | collective-permute-start | bytes 1179656 | tf_op jit(solution)/shard_map/ppermute | solution.py:457
  1038.5 75.7 %collective-permute-start.54 = (bf16[160,2560]{1,0:T(8,128)(2,1)}, bf16[160,2560]{1,0:T(8,128)(2,1)}, u32[]{:S(2)}, u32[]{:S(2)}) collective-permute-start(bf16[160,2560]{1,0:T(8,128)(2,1)} %get-tuple-element.471), channel_id=1, source_target_pairs={{0,16},{4,20},{8,24},{12,28},{16,0},{20,4},{24,8},{28,12},{1,17},{... | collective-permute-start | bytes 2457608 | tf_op jit(solution)/shard_map/ppermute | solution.py:376
  1201.6 55.3 %collective-permute-start.68 = (bf16[256,2560]{1,0:T(8,128)(2,1)S(1)}, bf16[256,2560]{1,0:T(8,128)(2,1)}, u32[]{:S(2)}, u32[]{:S(2)}) collective-permute-start(bf16[256,2560]{1,0:T(8,128)(2,1)S(1)} %get-tuple-element.360), channel_id=1, source_target_pairs={{0,8},{4,12},{8,0},{12,4},{16,24},{20,28},{24,16},{28,20},{1,9},{5... | collective-permute-start | bytes 3932168 | tf_op jit(solution)/shard_map/ppermute | solution.py:376
  1203.0 73.9 %collective-permute-start.65 = (bf16[256,2560]{1,0:T(8,128)(2,1)S(1)}, bf16[256,2560]{1,0:T(8,128)(2,1)}, u32[]{:S(2)}, u32[]{:S(2)}) collective-permute-start(bf16[256,2560]{1,0:T(8,128)(2,1)S(1)} %get-tuple-element.356), channel_id=1, source_target_pairs={{0,16},{4,20},{8,24},{12,28},{16,0},{20,4},{24,8},{28,12},{1,17},{... | collective-permute-start | bytes 3932168 | tf_op jit(solution)/shard_map/ppermute | solution.py:376
  (150 other events, 3182.4 us)
Sparse Core Ops, SparseCore 0:
  10.5 46.6 all-gather.9
  59.6 63.2 all-gather.19
  124.8 87.3 all-gather.11
  606.6 85.8 reduce-scatter.3
  699.2 78.2 reduce-scatter.5
  779.7 78.3 reduce-scatter.7
  859.7 79.6 all-gather.15
  941.1 124.6 all-gather.13
  1067.4 77.3 all-gather.17
  1203.7 138.3 all-reduce.12

commit v4 on v3

--- a/solution.py
+++ b/solution.py
@@ -399,7 +399,7 @@
 
 
 BACK_PARTS = ((0, 12), (12, 4), (16, HEADS // 2 - 16))
-ATTEND_PARTS = ((0, 4), (4, 7), (11, 7), (18, HEADS // 2 - 18))
+ATTEND_PARTS = ((0, 4), (4, 7), (11, 5), (16, HEADS // 2 - 16))
 
 
 def own_blocks(tensor):
@@ -609,12 +609,11 @@
     for at in range(1, len(steps) - 1):
         grad_blocks = {**grad_blocks, **gather_step(grad_blocks, n, at)}
     attn_branch = jnp.dot(attended, out_proj_all, preferred_element_type=F32)
-    attn_branch, grad_blocks = tie(attn_branch, grad_blocks)
+    attn_branch, grad_blocks, passed = tie(attn_branch, grad_blocks, passed)
     middle = token_rows + depth_scale * attn_branch
     mlp_float, mlp_inverse = rms_forward(middle, mlp_gain_all)
     normed_blocks = own_blocks(mlp_float.astype(BF16))
     normed_blocks = {**normed_blocks, **gather_step(normed_blocks, n, 0)}
-    normed_blocks, passed = tie(normed_blocks, passed)
     layer_blocks = [jnp.where(layer >= shift, passed[shift][0], passed[layers - shift][1]) for shift in range(1, layers)]
     for at in range(1, len(steps) - 1):
         normed_blocks = {**normed_blocks, **gather_step(normed_blocks, n, at)}
@@ -655,6 +654,8 @@
     hidden_parts, hidden_shares, crossing = [], [], []
     for grads in (grad_gate, grad_up):
         whole = dot(all_normed, grads, 0, 0).astype(BF16).reshape(chips, 2, layers, fetch, ff_wide)
+        if crossing:
+            whole, down_share = tie(whole, down_share)
         crossing.append((pick(whole, core, 1), swap(pick(whole, 1 - core, 1), 1, n)))
     for at in range(len(steps) - 2)[::-1]:
         blocks, _ = scatter_step(blocks, n, at)
@@ -664,7 +665,7 @@
         hidden_parts.append(part)
         hidden_shares.append(lax.psum_scatter(part, "seq", scatter_dimension=0, tiled=True)[0])
 
-    blocks, crossing[0], down_share = tie(blocks, crossing[0], down_share)
+    blocks, crossing[0] = tie(blocks, crossing[0])
     over_layers(crossing[0])
     grad_mlp_normed = jnp.concatenate([blocks[0, part] for part in range(2)]).astype(F32)
     grad_mid_norm, mlp_gain_part = rms_backward(middle, mlp_inverse, mlp_gain_all, grad_mlp_normed)
@@ -699,10 +700,14 @@
     for at in range(len(steps) - 2)[::-1]:
         out_blocks, _ = scatter_step(out_blocks, n, at)
     out_share = jnp.concatenate([out_blocks[0, part] for part in range(2)]).astype(BF16)
+    third, active_last = tie(third, active)
     q_up_part, kv_up_part, grad_kv_all, grad_rope_all, grad_q_lat = third
     grad_q_float, q_gain_part = rms_backward(q_latent, q_inverse, q_gain_all, grad_q_lat)
     grad_kv = seq_scatter(jnp.concatenate([grad_kv_all, grad_rope_all], axis=1).astype(BF16), layer, layers)
-    grad_kv, gate_low, down_low = tie(grad_kv, gate_low, down_low)
+    branch = {}
+    for step, at in zip(steps, first_rows):
+        branch.update(zip(step, to_tokens(at, half, len(step), [active_last], [down_w], 0)))
+    grad_kv, gate_low, down_low, branch = tie(grad_kv, gate_low, down_low, branch)
     up_parts = jnp.concatenate([q_up_part, kv_up_part], axis=1).reshape(-1, HEADS * LANES)
     up_share = fsdp_scatter(up_parts, core, chip, n).astype(BF16)
     grad_kv_first, kv_gain_part = rms_backward(kv_latent, kv_inverse, kv_gain_all, grad_kv[:, :rank_kv])
@@ -719,11 +724,8 @@
     down_rows = D // n
     down_all_part = jnp.concatenate([down_all_part.reshape(n, down_rows, -1), gain_rows], axis=1)
     down_all_share = fsdp_scatter(down_all_part.reshape(-1, latent.shape[1]), core, chip, n).astype(BF16)
-    up_share, out_share, down_all_share, up_low, active_last = tie(up_share, out_share, down_all_share, up_low, active)
+    up_share, out_share, down_all_share, up_low, branch = tie(up_share, out_share, down_all_share, up_low, branch)
     up_grad, out_proj_grad, down_all_grad = (v.astype(F32) for v in lax.psum((up_share, out_share, down_all_share), "seq"))
-    branch = {}
-    for step, at in zip(steps, first_rows):
-        branch.update(zip(step, to_tokens(at, half, len(step), [active_last], [down_w], 0)))
     down_grad = down_low.astype(F32)
     gate_up_grad = jnp.concatenate([gate_low, up_low], axis=1).astype(F32)
     output = (middle + depth_scale * chip_scatter(branch, n)).astype(BF16).reshape(block_input.shape)

time: 1370 us -> 1340 us (0.978)
  waiting for transfers between devices: 455 us -> 422 us
    ppermute x3, waiting for transfers between devices: 30.2 us -> 0.01 us  [seq_scatter(): lax.ppermute(pick(shares, (layer + shift) % layers), 'seq', ring(shift, l...]
    reduce_scatter x2, waiting for transfers between devices: 29.7 us -> 58.5 us  [over_layers(): lax.psum_scatter(part, 'seq', scatter_dimension=0, tiled=True)[0]]
    reduce_scatter x1, waiting for transfers between devices: 22.9 us -> 0.01 us  [body(): lax.psum_scatter(down_part, 'seq', scatter_dimension=0, tiled=True)]
    ppermute x3, waiting for transfers between devices: 46.4 us -> 24.4 us  [body(): lax.ppermute(passed[-1][0], 'seq', [(i, i + 1) for i in range(layers - 1)])]
    unnamed x215 -> x227, local copies, waits for them, and re-layouts: 50 us -> 50.1 us
  transfers between devices with their start and end apart: 81 -> 81, of which waited for: 32 -> 27; matrix products, arithmetic and copies ran while one was open for 28% -> 29% of each run, Pallas kernels for 16% -> 18%
where the time goes in v4:
time: 1340 us; the launch traced here: 1330 us
  waiting for transfers between devices  422 us (31%)
  Pallas kernels  296 us (22%)
  other arithmetic  175 us (13%)
  local copies, waits for them, and re-layouts  138 us (10%)
  starting transfers between devices  138 us (10%)
  matrix products  129 us (10%)
  between operations  20.8 us (2%)
    ppermute x59, waiting for transfers between devices, swap(): return lax.ppermute(tensor, 'fsdp', [(i, i ^ bit) for i in range(n)])  225 us
    dot_general x7, matrix products, dot(): lax.dot_general(a, b, (((ca,), (cb,)), ((), ())), preferred_element_type=...  112 us
    pallas_call x6, Pallas kernels, to_tokens(): pl.pallas_call(functools.partial(back_kernel, terms=len(left), contract=c...  92.4 us
    pallas_call x3, Pallas kernels, attend_backward(): pl.pallas_call(functools.partial(bwd_kernel, full_rows=full_rows, mask_ro...  77.5 us
    pallas_call x3, Pallas kernels, hidden_units(): pl.pallas_call(functools.partial(hidden_kernel, count=count), grid=(pl.cd...  75 us
    psum x1, waiting for transfers between devices, body(): lax.psum((up_share, out_share, down_all_share), 'seq')  61.7 us
    reduce_scatter x2, waiting for transfers between devices, over_layers(): lax.psum_scatter(part, 'seq', scatter_dimension=0, tiled=True)[0]  58.5 us
    ppermute x59, starting transfers between devices, swap(): return lax.ppermute(tensor, 'fsdp', [(i, i ^ bit) for i in range(n)])  53.9 us
  transfers between devices with their start and end apart: 81, of which 27 were waited for; matrix products, arithmetic and copies ran while one was open for 29% of the time, Pallas kernels for 18%

profile of v4, /device:TPU:0, one launch (start us, length us, event | category | flops | bytes accessed | tf_op | source)
XLA Modules:
  0.0 1329.5 jit_solution(11596397826969458073)
XLA Ops:
  102.2 20.7 %all-gather.20.cloned.1.call-done = bf16[1024,5120]{1,0:T(8,128)(2,1)} async-done(((bf16[128,5120]{1,0:T(8,128)(2,1)}), bf16[1024,5120]{1,0:T(8,128)(2,1)}) %all-gather.20.cloned.1.call-update) | async-done | bytes 10485776 | tf_op jit(solution)/shard_map/all_gather | solution.py:544
  144.4 18.0 %collective-permute-done.6 = bf16[2,80,1664]{2,1,0:T(8,128)(2,1)} collective-permute-done((bf16[2,80,1664]{2,1,0:T(8,128)(2,1)}, bf16[2,80,1664]{2,1,0:T(8,128)(2,1)}, u32[]{:S(2)}, u32[]{:S(2)}) %collective-permute-start.6) | collective-permute-done | bytes 532512 | tf_op jit(solution)/shard_map/ppermute | solution.py:376
  175.2 16.9 %attend_forward.5 = (bf16[512,2560]{1,0:T(8,128)(2,1)S(1)}, bf16[512,5120]{1,0:T(8,128)(2,1)}, f32[160,512]{1,0:T(8,128)S(1)}) custom-call(s32[4]{0:T(128)S(1)} %pad_add_fusion.bounds, bf16[512,768]{1,0:T(8,128)(2,1)S(1)} %copy-done.5, bf16[8,128,5120]{2,1,0:T(8,128)(2,1)} %bitcast.395, ...), custom_call_target="tpu_custom_call", output_to_operand_aliasing={{0}: (10, {}), {1}: (11, {}), {2}: (12, {})} | custom-call | flops 1048576 | bytes 65536 | tf_op jit(solution)/shard_map/attend_forward/pallas_call | solution.py:83
  192.1 24.4 %collective-permute-done.7 = bf16[2,4,80,1664]{3,2,1,0:T(8,128)(2,1)} collective-permute-done((bf16[2,4,80,1664]{3,2,1,0:T(8,128)(2,1)}, bf16[2,4,80,1664]{3,2,1,0:T(8,128)(2,1)}, u32[]{:S(2)}, u32[]{:S(2)}) %collective-permute-start.7) | collective-permute-done | bytes 2129952 | tf_op jit(solution)/shard_map/ppermute | solution.py:595
  232.2 25.1 %collective-permute-done.9.refs_2_ = bf16[256,2560]{1,0:T(8,128)(2,1)} collective-permute-done((bf16[256,2560]{1,0:T(8,128)(2,1)}, bf16[256,2560]{1,0:T(8,128)(2,1)}, u32[]{:S(2)}, u32[]{:S(2)}) %collective-permute-start.9) | collective-permute-done | bytes 1310752 | tf_op jit(solution)/shard_map/ppermute | solution.py:376
  372.9 16.3 %collective-permute-done.23.refs_1_ = bf16[256,2560]{1,0:T(8,128)(2,1)S(1)} collective-permute-done((bf16[256,2560]{1,0:T(8,128)(2,1)S(1)}, bf16[256,2560]{1,0:T(8,128)(2,1)S(1)}, u32[]{:S(2)}, u32[]{:S(2)}) %collective-permute-start.23) | collective-permute-done | bytes 1310752 | tf_op jit(solution)/shard_map/ppermute | solution.py:376
  401.4 20.0 %hidden_units.3 = (bf16[2048,1664]{1,0:T(8,128)(2,1)}, bf16[2048,1664]{1,0:T(8,128)(2,1)}, bf16[2048,1664]{1,0:T(8,128)(2,1)}) custom-call(bf16[256,2560]{1,0:T(8,128)(2,1)S(1)} %get-tuple-element.529.refs_0_, bf16[256,2560]{1,0:T(8,128)(2,1)S(1)} %get-tuple-element.528.refs_1_, bf16[256,2560]{1,0:T(8,128)(2,1)} %get-tuple-element.271.refs_2_, ...), custom_call_target="tpu_custom_call" | custom-call | flops 13086228480 | bytes 36044800 | tf_op jit(solution)/shard_map/hidden_units/pallas_call | solution.py:263
  421.5 19.9 %hidden_units.4 = (bf16[2048,1664]{1,0:T(8,128)(2,1)}, bf16[2048,1664]{1,0:T(8,128)(2,1)}, bf16[2048,1664]{1,0:T(8,128)(2,1)}) custom-call(bf16[256,2560]{1,0:T(8,128)(2,1)S(1)} %collective-permute-done.20.refs_0_, bf16[256,2560]{1,0:T(8,128)(2,1)S(1)} %collective-permute-done.23.refs_1_, ...), custom_call_target="tpu_custom_call", output_to_operand_aliasing={{0}: (7, {}), {1}: (8, {}), {2}: (9, {})} | custom-call | flops 13086228480 | bytes 36044800 | tf_op jit(solution)/shard_map/hidden_units/pallas_call | solution.py:263
  441.4 35.1 %hidden_units.5 = (bf16[2048,1664]{1,0:T(8,128)(2,1)}, bf16[2048,1664]{1,0:T(8,128)(2,1)}, bf16[2048,1664]{1,0:T(8,128)(2,1)}) custom-call(bf16[256,2560]{1,0:T(8,128)(2,1)S(1)} %collective-permute-done.19.refs_0_, bf16[256,2560]{1,0:T(8,128)(2,1)S(1)} %collective-permute-done.21.refs_1_, ...), custom_call_target="tpu_custom_call", output_to_operand_aliasing={{0}: (11, {}), {1}: (12, {}), {2}: (13, {})} | custom-call | flops 26172456960 | bytes 46530560 | tf_op jit(solution)/shard_map/hidden_units/pallas_call | solution.py:263
  476.5 24.9 %to_tokens.6 = (bf16[256,2560]{1,0:T(8,128)(2,1)S(1)}, bf16[256,2560]{1,0:T(8,128)(2,1)S(1)}, bf16[256,2560]{1,0:T(8,128)(2,1)S(1)}, bf16[256,2560]{1,0:T(8,128)(2,1)S(1)}) custom-call(bf16[2048,1664]{1,0:T(8,128)(2,1)} %get-tuple-element.290.refs_0_, bf16[2048,1664]{1,0:T(8,128)(2,1)} %get-tuple-element.291.refs_1_, ...), custom_call_target="tpu_custom_call" | custom-call | flops 1048576 | bytes 65536 | tf_op jit(solution)/shard_map/to_tokens/pallas_call | solution.py:302
  505.5 22.4 %convolution_convert_fusion.3 = bf16[1664,2560]{1,0:T(8,128)(2,1)S(1)} fusion(bf16[2048,1664]{1,0:T(8,128)(2,1)} %get-tuple-element.373.refs_0_, bf16[2048,2560]{1,0:T(8,128)(2,1)} %copy-done.70), kind=kOutput, calls=%fused_computation.7 | convolution fusion | flops 17452564480 | bytes 25821184 | tf_op jit(solution)/shard_map/dot_general | solution.py:24
  534.0 15.8 %to_tokens.7 = (bf16[256,2560]{1,0:T(8,128)(2,1)S(1)}, bf16[256,2560]{1,0:T(8,128)(2,1)S(1)}) custom-call(bf16[2048,1664]{1,0:T(8,128)(2,1)} %get-tuple-element.290.refs_0_, bf16[2048,1664]{1,0:T(8,128)(2,1)} %get-tuple-element.291.refs_1_, bf16[2560,1664]{1,0:T(8,128)(2,1)} %bitcast.57.refs_4_.refs_8_.refs_2_, ...), custom_call_target="tpu_custom_call" | custom-call | flops 1048576 | bytes 65536 | tf_op jit(solution)/shard_map/to_tokens/pallas_call | solution.py:302
  581.6 25.2 %convolution_convert_fusion.2 = bf16[2560,1664]{1,0:T(8,128)(2,1)} fusion(bf16[2048,2560]{1,0:T(8,128)(2,1)} %constant_dynamic-update-slice_fusion, bf16[2048,1664]{1,0:T(8,128)(2,1)} %get-tuple-element.290.refs_0_), kind=kOutput, calls=%fused_computation.6 | convolution fusion | flops 17452564480 | bytes 25821184 | tf_op jit(solution)/shard_map/dot_general | solution.py:24
  614.2 28.5 %collective-permute-done.34 = bf16[256,2560]{1,0:T(8,128)(2,1)} collective-permute-done((bf16[256,2560]{1,0:T(8,128)(2,1)S(1)}, bf16[256,2560]{1,0:T(8,128)(2,1)}, u32[]{:S(2)}, u32[]{:S(2)}) %collective-permute-start.34) | collective-permute-done | bytes 1310752 | tf_op jit(solution)/shard_map/ppermute | solution.py:376
  649.6 25.3 %convolution_convert_fusion.1 = bf16[2560,1664]{1,0:T(8,128)(2,1)} fusion(bf16[2048,2560]{1,0:T(8,128)(2,1)} %constant_dynamic-update-slice_fusion, bf16[2048,1664]{1,0:T(8,128)(2,1)} %get-tuple-element.291.refs_1_), kind=kOutput, calls=%fused_computation.5 | convolution fusion | flops 17452564480 | bytes 25821184 | tf_op jit(solution)/shard_map/dot_general | solution.py:24
  734.5 41.1 %attend_backward.3 = (bf16[8,96,5120]{2,1,0:T(8,128)(2,1)}, bf16[8,32,5120]{2,1,0:T(8,128)(2,1)}, f32[2048,256]{1,0:T(8,128)}, f32[2048,128]{1,0:T(8,128)S(1)}, f32[512,768]{1,0:T(8,128)}) custom-call(s32[4]{0:T(128)S(1)} %pad_add_fusion.bounds, bf16[768,512]{1,0:T(8,128)(2,1)S(1)} %copy-done.8, bf16[8,128,5120]{2,1,0:T(8,128)(2,1)} %bitcast.401, ...), custom_call_target="tpu_custom_call" | custom-call | flops 1048576 | bytes 65536 | tf_op jit(solution)/shard_map/attend_backward/pallas_call | solution.py:190
  776.6 58.4 %reduce-scatter.8.cloned.1.call-done = bf16[1,4,80,1664]{3,2,1,0:T(8,128)(2,1)} async-done(((bf16[4,4,80,1664]{3,2,1,0:T(8,128)(2,1)}), bf16[1,4,80,1664]{3,2,1,0:T(8,128)(2,1)}) %reduce-scatter.8.cloned.1.call-update) | async-done | bytes 1064976 | tf_op jit(solution)/shard_map/reduce_scatter | solution.py:666
  852.6 18.1 %attend_backward.4 = (bf16[8,96,5120]{2,1,0:T(8,128)(2,1)}, bf16[8,32,5120]{2,1,0:T(8,128)(2,1)}, f32[2048,256]{1,0:T(8,128)}, f32[2048,128]{1,0:T(8,128)S(1)}, f32[512,768]{1,0:T(8,128)}) custom-call(s32[4]{0:T(128)S(1)} %pad_add_fusion.bounds, bf16[768,512]{1,0:T(8,128)(2,1)S(1)} %copy-done.9, ...), custom_call_target="tpu_custom_call", output_to_operand_aliasing={{0}: (15, {}), {1}: (16, {})} | custom-call | flops 1048576 | bytes 65536 | tf_op jit(solution)/shard_map/attend_backward/pallas_call | solution.py:190
  888.5 18.3 %attend_backward.5 = (bf16[8,96,5120]{2,1,0:T(8,128)(2,1)}, bf16[8,32,5120]{2,1,0:T(8,128)(2,1)}, f32[2048,256]{1,0:T(8,128)}, f32[2048,128]{1,0:T(8,128)S(1)}, f32[512,768]{1,0:T(8,128)}) custom-call(s32[4]{0:T(128)S(1)} %pad_add_fusion.bounds, bf16[768,512]{1,0:T(8,128)(2,1)S(1)} %copy-done.9, ...), custom_call_target="tpu_custom_call", output_to_operand_aliasing={{0}: (15, {}), {1}: (16, {})} | custom-call | flops 1048576 | bytes 65536 | tf_op jit(solution)/shard_map/attend_backward/pallas_call | solution.py:190
  937.8 52.3 %collective-permute-start.57 = (bf16[512,384]{1,0:T(8,128)(2,1)}, bf16[512,384]{1,0:T(8,128)(2,1)S(1)}, u32[]{:S(2)}, u32[]{:S(2)}) collective-permute-start(bf16[512,384]{1,0:T(8,128)(2,1)} %get-tuple-element.564), channel_id=1, source_target_pairs={{0,3},{1,0},{2,1},{3,2},{4,7},{5,4},{6,5},{7,6},{8,11},{9,8},{10,9... | collective-permute-start | bytes 1179656 | tf_op jit(solution)/shard_map/ppermute | solution.py:457
  1115.3 19.3 %collective-permute-done.60 = bf16[168,1056]{1,0:T(8,128)(2,1)S(1)} collective-permute-done((bf16[168,1056]{1,0:T(8,128)(2,1)S(1)}, bf16[168,1056]{1,0:T(8,128)(2,1)S(1)}, u32[]{:S(2)}, u32[]{:S(2)}) %collective-permute-start.60) | collective-permute-done | bytes 354848 | tf_op jit(solution)/shard_map/ppermute | solution.py:376
  1169.5 21.3 %collective-permute-done.69 = bf16[256,2560]{1,0:T(8,128)(2,1)} collective-permute-done((bf16[256,2560]{1,0:T(8,128)(2,1)}, bf16[256,2560]{1,0:T(8,128)(2,1)}, u32[]{:S(2)}, u32[]{:S(2)}) %collective-permute-start.69) | collective-permute-done | bytes 1310752 | tf_op jit(solution)/shard_map/ppermute | solution.py:376
  1219.0 19.9 %collective-permute-done.70 = bf16[256,2560]{1,0:T(8,128)(2,1)} collective-permute-done((bf16[256,2560]{1,0:T(8,128)(2,1)}, bf16[256,2560]{1,0:T(8,128)(2,1)}, u32[]{:S(2)}, u32[]{:S(2)}) %collective-permute-start.70) | collective-permute-done | bytes 1310752 | tf_op jit(solution)/shard_map/ppermute | solution.py:376
  1248.7 61.7 %all-reduce.13.cloned.1.call-done = (bf16[336,1056]{1,0:T(8,128)(2,1)}, bf16[128,5120]{1,0:T(8,128)(2,1)}, bf16[320,2560]{1,0:T(8,128)(2,1)}) async-done(((bf16[336,1056]{1,0:T(8,128)(2,1)}, bf16[128,5120]{1,0:T(8,128)(2,1)}, bf16[320,2560]{1,0:T(8,128)(2,1)}), (bf16[336,1056]{1,0:T(8,128)(2,1)}, bf16[128,5120]{1,0:T(8,128)(2,1)}, bf16[320,2560]{1,0:T(8,128)(2,1)})) %all-reduce.13.cloned.1.call-update) | async-done | bytes 3658768 | tf_op jit(solution)/shard_map/psum | solution.py:728
  (588 shorter events, 659.8 us)
Async XLA Ops:
  7.2 52.3 %all-gather.10.cloned.1.call-start = ((), (), s32[]{:S(2)}) async-start(), calls=%async_computation.3 | async-start | bytes 6635520 | tf_op jit(solution)/shard_map/all_gather | solution.py:541
  10.4 112.5 %all-gather.20.cloned.1.call-start = ((), (), s32[]{:S(2)}) async-start(), calls=%async_computation.11 | async-start | bytes 11796480 | tf_op jit(solution)/shard_map/all_gather | solution.py:544
  13.6 291.5 %all-gather.12.cloned.1.call-start = ((), (), s32[]{:S(2)}) async-start(), calls=%async_computation.4 | async-start | bytes 14745600 | tf_op jit(solution)/shard_map/all_gather | solution.py:545
  14.3 662.2 %reduce-scatter.4.cloned.1.call-start = ((), (), s32[]{:S(2)}) async-start(), calls=%async_computation.5 | async-start | bytes 5120000 | tf_op jit(solution)/shard_map/reduce_scatter | solution.py:653
  175.1 114.7 %collective-permute-start.25 = (bf16[2,4,80,1664]{3,2,1,0:T(8,128)(2,1)}, bf16[2,4,80,1664]{3,2,1,0:T(8,128)(2,1)}, u32[]{:S(2)}, u32[]{:S(2)}) collective-permute-start(bf16[2,4,80,1664]{3,2,1,0:T(8,128)(2,1)} %bitcast_dynamic-update-slice_fusion), channel_id=1, source_target_pairs={{0,4},{4,0},{8,12},{12,8},{16,20},{20,16},{24,28},{28,24},{1,5},{5... | collective-permute-start | bytes 6389768 | tf_op jit(solution)/shard_map/ppermute | solution.py:376
  221.9 55.3 %collective-permute-start.11 = (bf16[2,4,80,1664]{3,2,1,0:T(8,128)(2,1)}, bf16[2,4,80,1664]{3,2,1,0:T(8,128)(2,1)}, u32[]{:S(2)}, u32[]{:S(2)}) collective-permute-start(bf16[2,4,80,1664]{3,2,1,0:T(8,128)(2,1)} %collective-permute-done.7), channel_id=1, source_target_pairs={{0,1},{1,2},{2,3},{4,5},{5,6},{6,7},{8,9},{9,10},{10,11},{12,13},{... | collective-permute-start | bytes 6389768 | tf_op jit(solution)/shard_map/ppermute | solution.py:595
  262.1 53.8 %collective-permute-start.14 = (bf16[256,2560]{1,0:T(8,128)(2,1)}, bf16[256,2560]{1,0:T(8,128)(2,1)}, u32[]{:S(2)}, u32[]{:S(2)}) collective-permute-start(bf16[256,2560]{1,0:T(8,128)(2,1)} %get-tuple-element.271.refs_2_), channel_id=1, source_target_pairs={{0,16},{4,20},{8,24},{12,28},{16,0},{20,4},{24,8},{28,12},{1,17},{... | collective-permute-start | bytes 3932168 | tf_op jit(solution)/shard_map/ppermute | solution.py:376
  338.2 52.1 %collective-permute-start.19 = (bf16[256,2560]{1,0:T(8,128)(2,1)S(1)}, bf16[256,2560]{1,0:T(8,128)(2,1)S(1)}, u32[]{:S(2)}, u32[]{:S(2)}) collective-permute-start(bf16[256,2560]{1,0:T(8,128)(2,1)S(1)} %get-tuple-element.529.refs_0_), channel_id=1, source_target_pairs={{0,16},{4,20},{8,24},{12,28},{16,0},{20,4},{24,8},{28,12},{1,17},{... | collective-permute-start | bytes 3932168 | tf_op jit(solution)/shard_map/ppermute | solution.py:376
  340.6 100.8 %collective-permute-start.22 = (bf16[256,2560]{1,0:T(8,128)(2,1)S(1)}, bf16[256,2560]{1,0:T(8,128)(2,1)S(1)}, u32[]{:S(2)}, u32[]{:S(2)}) collective-permute-start(bf16[256,2560]{1,0:T(8,128)(2,1)S(1)} %get-tuple-element.528.refs_1_), channel_id=1, source_target_pairs={{0,8},{4,12},{8,0},{12,4},{16,24},{20,28},{24,16},{28,20},{1,9},{5... | collective-permute-start | bytes 3932168 | tf_op jit(solution)/shard_map/ppermute | solution.py:376
  501.4 69.2 %collective-permute-start.29 = (bf16[256,2560]{1,0:T(8,128)(2,1)S(1)}, bf16[256,2560]{1,0:T(8,128)(2,1)S(1)}, u32[]{:S(2)}, u32[]{:S(2)}) collective-permute-start(bf16[256,2560]{1,0:T(8,128)(2,1)S(1)} %get-tuple-element.293), channel_id=1, source_target_pairs={{0,16},{4,20},{8,24},{12,28},{16,0},{20,4},{24,8},{28,12},{1,17},{... | collective-permute-start | bytes 3932168 | tf_op jit(solution)/shard_map/ppermute | solution.py:376
  501.9 71.4 %collective-permute-start.30 = (bf16[256,2560]{1,0:T(8,128)(2,1)S(1)}, bf16[256,2560]{1,0:T(8,128)(2,1)S(1)}, u32[]{:S(2)}, u32[]{:S(2)}) collective-permute-start(bf16[256,2560]{1,0:T(8,128)(2,1)S(1)} %get-tuple-element.295), channel_id=1, source_target_pairs={{0,8},{4,12},{8,0},{12,4},{16,24},{20,28},{24,16},{28,20},{1,9},{5... | collective-permute-start | bytes 3932168 | tf_op jit(solution)/shard_map/ppermute | solution.py:376
  503.0 63.5 %collective-permute-start.31 = (bf16[256,2560]{1,0:T(8,128)(2,1)S(1)}, bf16[256,2560]{1,0:T(8,128)(2,1)}, u32[]{:S(2)}, u32[]{:S(2)}) collective-permute-start(bf16[256,2560]{1,0:T(8,128)(2,1)S(1)} %get-tuple-element.297), channel_id=1, source_target_pairs={{0,16},{4,20},{8,24},{12,28},{16,0},{20,4},{24,8},{28,12},{1,17},{... | collective-permute-start | bytes 3932168 | tf_op jit(solution)/shard_map/ppermute | solution.py:376
  504.4 64.7 %collective-permute-start.32 = (bf16[256,2560]{1,0:T(8,128)(2,1)S(1)}, bf16[256,2560]{1,0:T(8,128)(2,1)S(1)}, u32[]{:S(2)}, u32[]{:S(2)}) collective-permute-start(bf16[256,2560]{1,0:T(8,128)(2,1)S(1)} %get-tuple-element.299), channel_id=1, source_target_pairs={{0,8},{4,12},{8,0},{12,4},{16,24},{20,28},{24,16},{28,20},{1,9},{5... | collective-permute-start | bytes 3932168 | tf_op jit(solution)/shard_map/ppermute | solution.py:376
  581.6 195.0 %reduce-scatter.6.cloned.1.call-start = ((), (), s32[]{:S(2)}) async-start(), calls=%async_computation.6 | async-start | bytes 5324800 | tf_op jit(solution)/shard_map/reduce_scatter | solution.py:666
  649.4 185.6 %reduce-scatter.8.cloned.1.call-start = ((), (), s32[]{:S(2)}) async-start(), calls=%async_computation.7 | async-start | bytes 5324800 | tf_op jit(solution)/shard_map/reduce_scatter | solution.py:666
  709.3 342.8 %all-gather.16.cloned.1.call-start = ((), (), s32[]{:S(2)}) async-start(), calls=%async_computation.9 | async-start | bytes 5120000 | tf_op jit(solution)/shard_map/all_gather | solution.py:685
  727.9 324.2 %all-gather.14.cloned.1.call-start = ((), (), s32[]{:S(2)}) async-start(), calls=%async_computation.8 | async-start | bytes 5120000 | tf_op jit(solution)/shard_map/all_gather | solution.py:697
  877.4 281.5 %all-gather.18.cloned.1.call-start = ((), (), s32[]{:S(2)}) async-start(), calls=%async_computation.10 | async-start | bytes 5120000 | tf_op jit(solution)/shard_map/all_gather | solution.py:697
  930.4 109.2 %collective-permute-start.46 = (bf16[4,128,5120]{2,1,0:T(8,128)(2,1)}, bf16[4,128,5120]{2,1,0:T(8,128)(2,1)}, u32[]{:S(2)}, u32[]{:S(2)}) collective-permute-start(bf16[4,128,5120]{2,1,0:T(8,128)(2,1)} %dynamic-slice_bitcast_fusion.1), channel_id=1, source_target_pairs={{0,4},{4,0},{8,12},{12,8},{16,20},{20,16},{24,28},{28,24},{1,5},{5... | collective-permute-start | bytes 15728648 | tf_op jit(solution)/shard_map/ppermute | solution.py:376
  930.5 379.9 %all-reduce.13.cloned.1.call-start = ((), (), s32[]{:S(2)}) async-start(), calls=%async_computation.12 | async-start | bytes 7446528 | tf_op jit(solution)/shard_map/psum | solution.py:728
  934.2 155.0 %collective-permute-start.53 = (bf16[160,2560]{1,0:T(8,128)(2,1)}, bf16[160,2560]{1,0:T(8,128)(2,1)}, u32[]{:S(2)}, u32[]{:S(2)}) collective-permute-start(bf16[160,2560]{1,0:T(8,128)(2,1)} %get-tuple-element.508), channel_id=1, source_target_pairs={{0,8},{4,12},{8,0},{12,4},{16,24},{20,28},{24,16},{28,20},{1,9},{5... | collective-permute-start | bytes 2457608 | tf_op jit(solution)/shard_map/ppermute | solution.py:376
  937.8 98.8 %collective-permute-start.57 = (bf16[512,384]{1,0:T(8,128)(2,1)}, bf16[512,384]{1,0:T(8,128)(2,1)S(1)}, u32[]{:S(2)}, u32[]{:S(2)}) collective-permute-start(bf16[512,384]{1,0:T(8,128)(2,1)} %get-tuple-element.564), channel_id=1, source_target_pairs={{0,3},{1,0},{2,1},{3,2},{4,7},{5,4},{6,5},{7,6},{8,11},{9,8},{10,9... | collective-permute-start | bytes 1179656 | tf_op jit(solution)/shard_map/ppermute | solution.py:457
  1036.6 53.6 %collective-permute-start.54 = (bf16[160,2560]{1,0:T(8,128)(2,1)}, bf16[160,2560]{1,0:T(8,128)(2,1)}, u32[]{:S(2)}, u32[]{:S(2)}) collective-permute-start(bf16[160,2560]{1,0:T(8,128)(2,1)} %get-tuple-element.509), channel_id=1, source_target_pairs={{0,16},{4,20},{8,24},{12,28},{16,0},{20,4},{24,8},{28,12},{1,17},{... | collective-permute-start | bytes 2457608 | tf_op jit(solution)/shard_map/ppermute | solution.py:376
  1168.7 72.4 %collective-permute-start.65 = (bf16[256,2560]{1,0:T(8,128)(2,1)}, bf16[256,2560]{1,0:T(8,128)(2,1)}, u32[]{:S(2)}, u32[]{:S(2)}) collective-permute-start(bf16[256,2560]{1,0:T(8,128)(2,1)} %get-tuple-element.392), channel_id=1, source_target_pairs={{0,16},{4,20},{8,24},{12,28},{16,0},{20,4},{24,8},{28,12},{1,17},{... | collective-permute-start | bytes 3932168 | tf_op jit(solution)/shard_map/ppermute | solution.py:376
  (158 other events, 3256.6 us)
Sparse Core Ops, SparseCore 0:
  10.5 46.6 all-gather.9
  59.6 63.2 all-gather.19
  124.8 87.3 all-gather.11
  581.7 92.1 reduce-scatter.3
  676.2 78.2 reduce-scatter.5
  756.6 78.3 reduce-scatter.7
  836.7 79.6 all-gather.15
  918.0 112.1 all-gather.13
  1031.8 77.3 all-gather.17
  1169.7 140.7 all-reduce.12

commit v5 on v4

--- a/solution.py
+++ b/solution.py
@@ -655,17 +655,15 @@
     for grads in (grad_gate, grad_up):
         whole = dot(all_normed, grads, 0, 0).astype(BF16).reshape(chips, 2, layers, fetch, ff_wide)
         if crossing:
-            whole, down_share = tie(whole, down_share)
+            for at in range(len(steps) - 2)[::-1]:
+                blocks, (whole, down_share, crossing[0]) = scatter_step(blocks, n, at, (whole, down_share, crossing[0]))
         crossing.append((pick(whole, core, 1), swap(pick(whole, 1 - core, 1), 1, n)))
-    for at in range(len(steps) - 2)[::-1]:
-        blocks, _ = scatter_step(blocks, n, at)
 
     def over_layers(crossed):
         part = (crossed[0].astype(F32) + crossed[1].astype(F32)).astype(BF16).transpose(1, 0, 2, 3)
         hidden_parts.append(part)
         hidden_shares.append(lax.psum_scatter(part, "seq", scatter_dimension=0, tiled=True)[0])
 
-    blocks, crossing[0] = tie(blocks, crossing[0])
     over_layers(crossing[0])
     grad_mlp_normed = jnp.concatenate([blocks[0, part] for part in range(2)]).astype(F32)
     grad_mid_norm, mlp_gain_part = rms_backward(middle, mlp_inverse, mlp_gain_all, grad_mlp_normed)

time: 1340 us -> 1330 us (level)
  starting transfers between devices: 138 us -> 123 us
    reduce_scatter x1, waiting for transfers between devices: 0.01 us -> 29.2 us  [body(): lax.psum_scatter(down_part, 'seq', scatter_dimension=0, tiled=True)]
    ppermute x59, waiting for transfers between devices: 225 us -> 198 us  [swap(): return lax.ppermute(tensor, 'fsdp', [(i, i ^ bit) for i in range(n)])]
    ppermute x3, starting transfers between devices: 52.9 us -> 37.7 us  [seq_scatter(): lax.ppermute(pick(shares, (layer + shift) % layers), 'seq', ring(shift, l...]
    unnamed x227 -> x230, local copies, waits for them, and re-layouts: 50.1 us -> 52.3 us
  transfers between devices with their start and end apart: 81 -> 81, of which waited for: 27 -> 30; matrix products, arithmetic and copies ran while one was open for 29% -> 29% of each run, Pallas kernels for 18% -> 18%
where the time goes in v5:
time: 1330 us; the launch traced here: 1320 us
  waiting for transfers between devices  427 us (32%)
  Pallas kernels  296 us (22%)
  other arithmetic  177 us (13%)
  local copies, waits for them, and re-layouts  140 us (11%)
  matrix products  129 us (10%)
  starting transfers between devices  123 us (9%)
  between operations  20.9 us (2%)
    ppermute x59, waiting for transfers between devices, swap(): return lax.ppermute(tensor, 'fsdp', [(i, i ^ bit) for i in range(n)])  198 us
    dot_general x7, matrix products, dot(): lax.dot_general(a, b, (((ca,), (cb,)), ((), ())), preferred_element_type=...  112 us
    pallas_call x6, Pallas kernels, to_tokens(): pl.pallas_call(functools.partial(back_kernel, terms=len(left), contract=c...  92.1 us
    pallas_call x3, Pallas kernels, attend_backward(): pl.pallas_call(functools.partial(bwd_kernel, full_rows=full_rows, mask_ro...  77.3 us
    pallas_call x3, Pallas kernels, hidden_units(): pl.pallas_call(functools.partial(hidden_kernel, count=count), grid=(pl.cd...  75.2 us
    psum x1, waiting for transfers between devices, body(): lax.psum((up_share, out_share, down_all_share), 'seq')  62.5 us
    reduce_scatter x2, waiting for transfers between devices, over_layers(): lax.psum_scatter(part, 'seq', scatter_dimension=0, tiled=True)[0]  56.9 us
    ppermute x59, starting transfers between devices, swap(): return lax.ppermute(tensor, 'fsdp', [(i, i ^ bit) for i in range(n)])  54.8 us
  transfers between devices with their start and end apart: 81, of which 30 were waited for; matrix products, arithmetic and copies ran while one was open for 29% of the time, Pallas kernels for 18%

profile of v5, /device:TPU:0, one launch (start us, length us, event | category | flops | bytes accessed | tf_op | source)
XLA Modules:
  0.0 1322.7 jit_solution(634813084695240935)
XLA Ops:
  102.3 20.7 %all-gather.20.cloned.1.call-done = bf16[1024,5120]{1,0:T(8,128)(2,1)} async-done(((bf16[128,5120]{1,0:T(8,128)(2,1)}), bf16[1024,5120]{1,0:T(8,128)(2,1)}) %all-gather.20.cloned.1.call-update) | async-done | bytes 10485776 | tf_op jit(solution)/shard_map/all_gather | solution.py:544
  144.4 17.9 %collective-permute-done.6 = bf16[2,80,1664]{2,1,0:T(8,128)(2,1)} collective-permute-done((bf16[2,80,1664]{2,1,0:T(8,128)(2,1)}, bf16[2,80,1664]{2,1,0:T(8,128)(2,1)}, u32[]{:S(2)}, u32[]{:S(2)}) %collective-permute-start.6) | collective-permute-done | bytes 532512 | tf_op jit(solution)/shard_map/ppermute | solution.py:376
  175.2 16.9 %attend_forward.5 = (bf16[512,2560]{1,0:T(8,128)(2,1)S(1)}, bf16[512,5120]{1,0:T(8,128)(2,1)}, f32[160,512]{1,0:T(8,128)S(1)}) custom-call(s32[4]{0:T(128)S(1)} %pad_add_fusion.bounds, bf16[512,768]{1,0:T(8,128)(2,1)S(1)} %copy-done.5, bf16[8,128,5120]{2,1,0:T(8,128)(2,1)} %bitcast.395, ...), custom_call_target="tpu_custom_call", output_to_operand_aliasing={{0}: (10, {}), {1}: (11, {}), {2}: (12, {})} | custom-call | flops 1048576 | bytes 65536 | tf_op jit(solution)/shard_map/attend_forward/pallas_call | solution.py:83
  192.1 24.4 %collective-permute-done.7 = bf16[2,4,80,1664]{3,2,1,0:T(8,128)(2,1)} collective-permute-done((bf16[2,4,80,1664]{3,2,1,0:T(8,128)(2,1)}, bf16[2,4,80,1664]{3,2,1,0:T(8,128)(2,1)}, u32[]{:S(2)}, u32[]{:S(2)}) %collective-permute-start.7) | collective-permute-done | bytes 2129952 | tf_op jit(solution)/shard_map/ppermute | solution.py:595
  232.2 25.1 %collective-permute-done.9.refs_2_ = bf16[256,2560]{1,0:T(8,128)(2,1)} collective-permute-done((bf16[256,2560]{1,0:T(8,128)(2,1)}, bf16[256,2560]{1,0:T(8,128)(2,1)}, u32[]{:S(2)}, u32[]{:S(2)}) %collective-permute-start.9) | collective-permute-done | bytes 1310752 | tf_op jit(solution)/shard_map/ppermute | solution.py:376
  372.8 16.3 %collective-permute-done.23.refs_1_ = bf16[256,2560]{1,0:T(8,128)(2,1)S(1)} collective-permute-done((bf16[256,2560]{1,0:T(8,128)(2,1)S(1)}, bf16[256,2560]{1,0:T(8,128)(2,1)S(1)}, u32[]{:S(2)}, u32[]{:S(2)}) %collective-permute-start.23) | collective-permute-done | bytes 1310752 | tf_op jit(solution)/shard_map/ppermute | solution.py:376
  401.4 20.3 %hidden_units.3 = (bf16[2048,1664]{1,0:T(8,128)(2,1)}, bf16[2048,1664]{1,0:T(8,128)(2,1)}, bf16[2048,1664]{1,0:T(8,128)(2,1)}) custom-call(bf16[256,2560]{1,0:T(8,128)(2,1)S(1)} %get-tuple-element.529.refs_0_, bf16[256,2560]{1,0:T(8,128)(2,1)S(1)} %get-tuple-element.528.refs_1_, bf16[256,2560]{1,0:T(8,128)(2,1)} %get-tuple-element.271.refs_2_, ...), custom_call_target="tpu_custom_call" | custom-call | flops 13086228480 | bytes 36044800 | tf_op jit(solution)/shard_map/hidden_units/pallas_call | solution.py:263
  421.6 19.8 %hidden_units.4 = (bf16[2048,1664]{1,0:T(8,128)(2,1)}, bf16[2048,1664]{1,0:T(8,128)(2,1)}, bf16[2048,1664]{1,0:T(8,128)(2,1)}) custom-call(bf16[256,2560]{1,0:T(8,128)(2,1)S(1)} %collective-permute-done.20.refs_0_, bf16[256,2560]{1,0:T(8,128)(2,1)S(1)} %collective-permute-done.23.refs_1_, ...), custom_call_target="tpu_custom_call", output_to_operand_aliasing={{0}: (7, {}), {1}: (8, {}), {2}: (9, {})} | custom-call | flops 13086228480 | bytes 36044800 | tf_op jit(solution)/shard_map/hidden_units/pallas_call | solution.py:263
  441.5 35.1 %hidden_units.5 = (bf16[2048,1664]{1,0:T(8,128)(2,1)}, bf16[2048,1664]{1,0:T(8,128)(2,1)}, bf16[2048,1664]{1,0:T(8,128)(2,1)}) custom-call(bf16[256,2560]{1,0:T(8,128)(2,1)S(1)} %collective-permute-done.19.refs_0_, bf16[256,2560]{1,0:T(8,128)(2,1)S(1)} %collective-permute-done.21.refs_1_, ...), custom_call_target="tpu_custom_call", output_to_operand_aliasing={{0}: (11, {}), {1}: (12, {}), {2}: (13, {})} | custom-call | flops 26172456960 | bytes 46530560 | tf_op jit(solution)/shard_map/hidden_units/pallas_call | solution.py:263
  476.6 24.9 %to_tokens.6 = (bf16[256,2560]{1,0:T(8,128)(2,1)S(1)}, bf16[256,2560]{1,0:T(8,128)(2,1)S(1)}, bf16[256,2560]{1,0:T(8,128)(2,1)S(1)}, bf16[256,2560]{1,0:T(8,128)(2,1)S(1)}) custom-call(bf16[2048,1664]{1,0:T(8,128)(2,1)} %get-tuple-element.290.refs_0_, bf16[2048,1664]{1,0:T(8,128)(2,1)} %get-tuple-element.291.refs_1_, ...), custom_call_target="tpu_custom_call" | custom-call | flops 1048576 | bytes 65536 | tf_op jit(solution)/shard_map/to_tokens/pallas_call | solution.py:302
  505.7 22.3 %convolution_convert_fusion.3 = bf16[1664,2560]{1,0:T(8,128)(2,1)S(1)} fusion(bf16[2048,1664]{1,0:T(8,128)(2,1)} %get-tuple-element.373.refs_0_, bf16[2048,2560]{1,0:T(8,128)(2,1)} %copy-done.72), kind=kOutput, calls=%fused_computation.7 | convolution fusion | flops 17452564480 | bytes 25821184 | tf_op jit(solution)/shard_map/dot_general | solution.py:24
  534.2 15.6 %to_tokens.7 = (bf16[256,2560]{1,0:T(8,128)(2,1)S(1)}, bf16[256,2560]{1,0:T(8,128)(2,1)S(1)}) custom-call(bf16[2048,1664]{1,0:T(8,128)(2,1)} %get-tuple-element.290.refs_0_, bf16[2048,1664]{1,0:T(8,128)(2,1)} %get-tuple-element.291.refs_1_, bf16[2560,1664]{1,0:T(8,128)(2,1)} %bitcast.57.refs_4_.refs_8_.refs_2_, ...), custom_call_target="tpu_custom_call" | custom-call | flops 1048576 | bytes 65536 | tf_op jit(solution)/shard_map/to_tokens/pallas_call | solution.py:302
  581.7 25.1 %convolution_convert_fusion.1 = bf16[2560,1664]{1,0:T(8,128)(2,1)} fusion(bf16[2048,2560]{1,0:T(8,128)(2,1)} %constant_dynamic-update-slice_fusion, bf16[2048,1664]{1,0:T(8,128)(2,1)} %get-tuple-element.290.refs_0_), kind=kOutput, calls=%fused_computation.5 | convolution fusion | flops 17452564480 | bytes 25821184 | tf_op jit(solution)/shard_map/dot_general | solution.py:24
  613.8 25.4 %convolution_convert_fusion.2 = bf16[2560,1664]{1,0:T(8,128)(2,1)} fusion(bf16[2048,2560]{1,0:T(8,128)(2,1)} %constant_dynamic-update-slice_fusion, bf16[2048,1664]{1,0:T(8,128)(2,1)} %get-tuple-element.291.refs_1_), kind=kOutput, calls=%fused_computation.6 | convolution fusion | flops 17452564480 | bytes 25821184 | tf_op jit(solution)/shard_map/dot_general | solution.py:24
  644.6 29.2 %reduce-scatter.4.cloned.1.call-done.rest_2_ = bf16[200,2560]{1,0:T(8,128)(2,1)} async-done(((bf16[800,2560]{1,0:T(8,128)(2,1)}), bf16[200,2560]{1,0:T(8,128)(2,1)}) %reduce-scatter.4.cloned.1.call-update) | async-done | bytes 1024016 | tf_op jit(solution)/shard_map/reduce_scatter | solution.py:653
  740.3 41.1 %attend_backward.3 = (bf16[8,96,5120]{2,1,0:T(8,128)(2,1)}, bf16[8,32,5120]{2,1,0:T(8,128)(2,1)}, f32[2048,256]{1,0:T(8,128)}, f32[2048,128]{1,0:T(8,128)S(1)}, f32[512,768]{1,0:T(8,128)}) custom-call(s32[4]{0:T(128)S(1)} %pad_add_fusion.bounds, bf16[768,512]{1,0:T(8,128)(2,1)S(1)} %copy-done.8, bf16[8,128,5120]{2,1,0:T(8,128)(2,1)} %bitcast.401, ...), custom_call_target="tpu_custom_call" | custom-call | flops 1048576 | bytes 65536 | tf_op jit(solution)/shard_map/attend_backward/pallas_call | solution.py:190
  782.5 56.9 %reduce-scatter.8.cloned.1.call-done = bf16[1,4,80,1664]{3,2,1,0:T(8,128)(2,1)} async-done(((bf16[4,4,80,1664]{3,2,1,0:T(8,128)(2,1)}), bf16[1,4,80,1664]{3,2,1,0:T(8,128)(2,1)}) %reduce-scatter.8.cloned.1.call-update) | async-done | bytes 1064976 | tf_op jit(solution)/shard_map/reduce_scatter | solution.py:665
  857.0 17.9 %attend_backward.4 = (bf16[8,96,5120]{2,1,0:T(8,128)(2,1)}, bf16[8,32,5120]{2,1,0:T(8,128)(2,1)}, f32[2048,256]{1,0:T(8,128)}, f32[2048,128]{1,0:T(8,128)S(1)}, f32[512,768]{1,0:T(8,128)}) custom-call(s32[4]{0:T(128)S(1)} %pad_add_fusion.bounds, bf16[768,512]{1,0:T(8,128)(2,1)S(1)} %copy-done.9, ...), custom_call_target="tpu_custom_call", output_to_operand_aliasing={{0}: (15, {}), {1}: (16, {})} | custom-call | flops 1048576 | bytes 65536 | tf_op jit(solution)/shard_map/attend_backward/pallas_call | solution.py:190
  892.9 18.3 %attend_backward.5 = (bf16[8,96,5120]{2,1,0:T(8,128)(2,1)}, bf16[8,32,5120]{2,1,0:T(8,128)(2,1)}, f32[2048,256]{1,0:T(8,128)}, f32[2048,128]{1,0:T(8,128)S(1)}, f32[512,768]{1,0:T(8,128)}) custom-call(s32[4]{0:T(128)S(1)} %pad_add_fusion.bounds, bf16[768,512]{1,0:T(8,128)(2,1)S(1)} %copy-done.9, ...), custom_call_target="tpu_custom_call", output_to_operand_aliasing={{0}: (15, {}), {1}: (16, {})} | custom-call | flops 1048576 | bytes 65536 | tf_op jit(solution)/shard_map/attend_backward/pallas_call | solution.py:190
  942.0 37.1 %collective-permute-start.57 = (bf16[512,384]{1,0:T(8,128)(2,1)}, bf16[512,384]{1,0:T(8,128)(2,1)S(1)}, u32[]{:S(2)}, u32[]{:S(2)}) collective-permute-start(bf16[512,384]{1,0:T(8,128)(2,1)} %get-tuple-element.564), channel_id=1, source_target_pairs={{0,3},{1,0},{2,1},{3,2},{4,7},{5,4},{6,5},{7,6},{8,11},{9,8},{10,9... | collective-permute-start | bytes 1179656 | tf_op jit(solution)/shard_map/ppermute | solution.py:457
  1107.9 19.3 %collective-permute-done.60 = bf16[168,1056]{1,0:T(8,128)(2,1)S(1)} collective-permute-done((bf16[168,1056]{1,0:T(8,128)(2,1)S(1)}, bf16[168,1056]{1,0:T(8,128)(2,1)S(1)}, u32[]{:S(2)}, u32[]{:S(2)}) %collective-permute-start.60) | collective-permute-done | bytes 354848 | tf_op jit(solution)/shard_map/ppermute | solution.py:376
  1162.2 21.3 %collective-permute-done.69 = bf16[256,2560]{1,0:T(8,128)(2,1)} collective-permute-done((bf16[256,2560]{1,0:T(8,128)(2,1)}, bf16[256,2560]{1,0:T(8,128)(2,1)}, u32[]{:S(2)}, u32[]{:S(2)}) %collective-permute-start.69) | collective-permute-done | bytes 1310752 | tf_op jit(solution)/shard_map/ppermute | solution.py:376
  1211.6 19.9 %collective-permute-done.70 = bf16[256,2560]{1,0:T(8,128)(2,1)} collective-permute-done((bf16[256,2560]{1,0:T(8,128)(2,1)}, bf16[256,2560]{1,0:T(8,128)(2,1)}, u32[]{:S(2)}, u32[]{:S(2)}) %collective-permute-start.70) | collective-permute-done | bytes 1310752 | tf_op jit(solution)/shard_map/ppermute | solution.py:376
  1241.1 62.5 %all-reduce.13.cloned.1.call-done = (bf16[336,1056]{1,0:T(8,128)(2,1)}, bf16[128,5120]{1,0:T(8,128)(2,1)}, bf16[320,2560]{1,0:T(8,128)(2,1)}) async-done(((bf16[336,1056]{1,0:T(8,128)(2,1)}, bf16[128,5120]{1,0:T(8,128)(2,1)}, bf16[320,2560]{1,0:T(8,128)(2,1)}), (bf16[336,1056]{1,0:T(8,128)(2,1)}, bf16[128,5120]{1,0:T(8,128)(2,1)}, bf16[320,2560]{1,0:T(8,128)(2,1)})) %all-reduce.13.cloned.1.call-update) | async-done | bytes 3658768 | tf_op jit(solution)/shard_map/psum | solution.py:726
  (590 shorter events, 668.5 us)
Async XLA Ops:
  7.2 52.3 %all-gather.10.cloned.1.call-start = ((), (), s32[]{:S(2)}) async-start(), calls=%async_computation.3 | async-start | bytes 6635520 | tf_op jit(solution)/shard_map/all_gather | solution.py:541
  10.4 112.5 %all-gather.20.cloned.1.call-start = ((), (), s32[]{:S(2)}) async-start(), calls=%async_computation.11 | async-start | bytes 11796480 | tf_op jit(solution)/shard_map/all_gather | solution.py:544
  13.6 291.4 %all-gather.12.cloned.1.call-start = ((), (), s32[]{:S(2)}) async-start(), calls=%async_computation.4 | async-start | bytes 14745600 | tf_op jit(solution)/shard_map/all_gather | solution.py:545
  14.3 659.5 %reduce-scatter.4.cloned.1.call-start = ((), (), s32[]{:S(2)}) async-start(), calls=%async_computation.5 | async-start | bytes 5120000 | tf_op jit(solution)/shard_map/reduce_scatter | solution.py:653
  175.1 114.6 %collective-permute-start.25 = (bf16[2,4,80,1664]{3,2,1,0:T(8,128)(2,1)}, bf16[2,4,80,1664]{3,2,1,0:T(8,128)(2,1)}, u32[]{:S(2)}, u32[]{:S(2)}) collective-permute-start(bf16[2,4,80,1664]{3,2,1,0:T(8,128)(2,1)} %bitcast_dynamic-update-slice_fusion), channel_id=1, source_target_pairs={{0,4},{4,0},{8,12},{12,8},{16,20},{20,16},{24,28},{28,24},{1,5},{5... | collective-permute-start | bytes 6389768 | tf_op jit(solution)/shard_map/ppermute | solution.py:376
  222.0 55.2 %collective-permute-start.11 = (bf16[2,4,80,1664]{3,2,1,0:T(8,128)(2,1)}, bf16[2,4,80,1664]{3,2,1,0:T(8,128)(2,1)}, u32[]{:S(2)}, u32[]{:S(2)}) collective-permute-start(bf16[2,4,80,1664]{3,2,1,0:T(8,128)(2,1)} %collective-permute-done.7), channel_id=1, source_target_pairs={{0,1},{1,2},{2,3},{4,5},{5,6},{6,7},{8,9},{9,10},{10,11},{12,13},{... | collective-permute-start | bytes 6389768 | tf_op jit(solution)/shard_map/ppermute | solution.py:595
  262.1 53.7 %collective-permute-start.14 = (bf16[256,2560]{1,0:T(8,128)(2,1)}, bf16[256,2560]{1,0:T(8,128)(2,1)}, u32[]{:S(2)}, u32[]{:S(2)}) collective-permute-start(bf16[256,2560]{1,0:T(8,128)(2,1)} %get-tuple-element.271.refs_2_), channel_id=1, source_target_pairs={{0,16},{4,20},{8,24},{12,28},{16,0},{20,4},{24,8},{28,12},{1,17},{... | collective-permute-start | bytes 3932168 | tf_op jit(solution)/shard_map/ppermute | solution.py:376
  338.1 52.1 %collective-permute-start.19 = (bf16[256,2560]{1,0:T(8,128)(2,1)S(1)}, bf16[256,2560]{1,0:T(8,128)(2,1)S(1)}, u32[]{:S(2)}, u32[]{:S(2)}) collective-permute-start(bf16[256,2560]{1,0:T(8,128)(2,1)S(1)} %get-tuple-element.529.refs_0_), channel_id=1, source_target_pairs={{0,16},{4,20},{8,24},{12,28},{16,0},{20,4},{24,8},{28,12},{1,17},{... | collective-permute-start | bytes 3932168 | tf_op jit(solution)/shard_map/ppermute | solution.py:376
  340.5 101.0 %collective-permute-start.22 = (bf16[256,2560]{1,0:T(8,128)(2,1)S(1)}, bf16[256,2560]{1,0:T(8,128)(2,1)S(1)}, u32[]{:S(2)}, u32[]{:S(2)}) collective-permute-start(bf16[256,2560]{1,0:T(8,128)(2,1)S(1)} %get-tuple-element.528.refs_1_), channel_id=1, source_target_pairs={{0,8},{4,12},{8,0},{12,4},{16,24},{20,28},{24,16},{28,20},{1,9},{5... | collective-permute-start | bytes 3932168 | tf_op jit(solution)/shard_map/ppermute | solution.py:376
  501.5 68.9 %collective-permute-start.29 = (bf16[256,2560]{1,0:T(8,128)(2,1)S(1)}, bf16[256,2560]{1,0:T(8,128)(2,1)S(1)}, u32[]{:S(2)}, u32[]{:S(2)}) collective-permute-start(bf16[256,2560]{1,0:T(8,128)(2,1)S(1)} %get-tuple-element.293), channel_id=1, source_target_pairs={{0,16},{4,20},{8,24},{12,28},{16,0},{20,4},{24,8},{28,12},{1,17},{... | collective-permute-start | bytes 3932168 | tf_op jit(solution)/shard_map/ppermute | solution.py:376
  502.0 71.2 %collective-permute-start.30 = (bf16[256,2560]{1,0:T(8,128)(2,1)S(1)}, bf16[256,2560]{1,0:T(8,128)(2,1)S(1)}, u32[]{:S(2)}, u32[]{:S(2)}) collective-permute-start(bf16[256,2560]{1,0:T(8,128)(2,1)S(1)} %get-tuple-element.295), channel_id=1, source_target_pairs={{0,8},{4,12},{8,0},{12,4},{16,24},{20,28},{24,16},{28,20},{1,9},{5... | collective-permute-start | bytes 3932168 | tf_op jit(solution)/shard_map/ppermute | solution.py:376
  503.1 63.2 %collective-permute-start.31 = (bf16[256,2560]{1,0:T(8,128)(2,1)S(1)}, bf16[256,2560]{1,0:T(8,128)(2,1)}, u32[]{:S(2)}, u32[]{:S(2)}) collective-permute-start(bf16[256,2560]{1,0:T(8,128)(2,1)S(1)} %get-tuple-element.297), channel_id=1, source_target_pairs={{0,16},{4,20},{8,24},{12,28},{16,0},{20,4},{24,8},{28,12},{1,17},{... | collective-permute-start | bytes 3932168 | tf_op jit(solution)/shard_map/ppermute | solution.py:376
  504.5 64.5 %collective-permute-start.32 = (bf16[256,2560]{1,0:T(8,128)(2,1)S(1)}, bf16[256,2560]{1,0:T(8,128)(2,1)S(1)}, u32[]{:S(2)}, u32[]{:S(2)}) collective-permute-start(bf16[256,2560]{1,0:T(8,128)(2,1)S(1)} %get-tuple-element.299), channel_id=1, source_target_pairs={{0,8},{4,12},{8,0},{12,4},{16,24},{20,28},{24,16},{28,20},{1,9},{5... | collective-permute-start | bytes 3932168 | tf_op jit(solution)/shard_map/ppermute | solution.py:376
  581.6 200.8 %reduce-scatter.6.cloned.1.call-start = ((), (), s32[]{:S(2)}) async-start(), calls=%async_computation.6 | async-start | bytes 5324800 | tf_op jit(solution)/shard_map/reduce_scatter | solution.py:665
  680.4 159.0 %reduce-scatter.8.cloned.1.call-start = ((), (), s32[]{:S(2)}) async-start(), calls=%async_computation.7 | async-start | bytes 5324800 | tf_op jit(solution)/shard_map/reduce_scatter | solution.py:665
  715.0 329.8 %all-gather.16.cloned.1.call-start = ((), (), s32[]{:S(2)}) async-start(), calls=%async_computation.9 | async-start | bytes 5120000 | tf_op jit(solution)/shard_map/all_gather | solution.py:683
  733.5 311.3 %all-gather.14.cloned.1.call-start = ((), (), s32[]{:S(2)}) async-start(), calls=%async_computation.8 | async-start | bytes 5120000 | tf_op jit(solution)/shard_map/all_gather | solution.py:695
  881.6 269.9 %all-gather.18.cloned.1.call-start = ((), (), s32[]{:S(2)}) async-start(), calls=%async_computation.10 | async-start | bytes 5120000 | tf_op jit(solution)/shard_map/all_gather | solution.py:695
  934.6 97.6 %collective-permute-start.46 = (bf16[4,128,5120]{2,1,0:T(8,128)(2,1)}, bf16[4,128,5120]{2,1,0:T(8,128)(2,1)}, u32[]{:S(2)}, u32[]{:S(2)}) collective-permute-start(bf16[4,128,5120]{2,1,0:T(8,128)(2,1)} %dynamic-slice_bitcast_fusion.1), channel_id=1, source_target_pairs={{0,4},{4,0},{8,12},{12,8},{16,20},{20,16},{24,28},{28,24},{1,5},{5... | collective-permute-start | bytes 15728648 | tf_op jit(solution)/shard_map/ppermute | solution.py:376
  934.8 368.8 %all-reduce.13.cloned.1.call-start = ((), (), s32[]{:S(2)}) async-start(), calls=%async_computation.12 | async-start | bytes 7446528 | tf_op jit(solution)/shard_map/psum | solution.py:726
  938.4 143.4 %collective-permute-start.53 = (bf16[160,2560]{1,0:T(8,128)(2,1)}, bf16[160,2560]{1,0:T(8,128)(2,1)}, u32[]{:S(2)}, u32[]{:S(2)}) collective-permute-start(bf16[160,2560]{1,0:T(8,128)(2,1)} %get-tuple-element.508), channel_id=1, source_target_pairs={{0,8},{4,12},{8,0},{12,4},{16,24},{20,28},{24,16},{28,20},{1,9},{5... | collective-permute-start | bytes 2457608 | tf_op jit(solution)/shard_map/ppermute | solution.py:376
  942.0 83.6 %collective-permute-start.57 = (bf16[512,384]{1,0:T(8,128)(2,1)}, bf16[512,384]{1,0:T(8,128)(2,1)S(1)}, u32[]{:S(2)}, u32[]{:S(2)}) collective-permute-start(bf16[512,384]{1,0:T(8,128)(2,1)} %get-tuple-element.564), channel_id=1, source_target_pairs={{0,3},{1,0},{2,1},{3,2},{4,7},{5,4},{6,5},{7,6},{8,11},{9,8},{10,9... | collective-permute-start | bytes 1179656 | tf_op jit(solution)/shard_map/ppermute | solution.py:457
  1025.6 57.1 %collective-permute-start.54 = (bf16[160,2560]{1,0:T(8,128)(2,1)}, bf16[160,2560]{1,0:T(8,128)(2,1)}, u32[]{:S(2)}, u32[]{:S(2)}) collective-permute-start(bf16[160,2560]{1,0:T(8,128)(2,1)} %get-tuple-element.509), channel_id=1, source_target_pairs={{0,16},{4,20},{8,24},{12,28},{16,0},{20,4},{24,8},{28,12},{1,17},{... | collective-permute-start | bytes 2457608 | tf_op jit(solution)/shard_map/ppermute | solution.py:376
  1161.6 72.1 %collective-permute-start.65 = (bf16[256,2560]{1,0:T(8,128)(2,1)}, bf16[256,2560]{1,0:T(8,128)(2,1)}, u32[]{:S(2)}, u32[]{:S(2)}) collective-permute-start(bf16[256,2560]{1,0:T(8,128)(2,1)} %get-tuple-element.392), channel_id=1, source_target_pairs={{0,16},{4,20},{8,24},{12,28},{16,0},{20,4},{24,8},{28,12},{1,17},{... | collective-permute-start | bytes 3932168 | tf_op jit(solution)/shard_map/ppermute | solution.py:376
  (160 other events, 3208.3 us)
Sparse Core Ops, SparseCore 0:
  10.5 46.6 all-gather.9
  59.6 63.2 all-gather.19
  124.8 87.3 all-gather.11
  581.8 92.0 reduce-scatter.3
  680.5 78.2 reduce-scatter.5
  761.0 78.3 reduce-scatter.7
  841.0 79.6 all-gather.15
  922.4 111.1 all-gather.13
  1035.2 77.2 all-gather.17
  1162.3 141.2 all-reduce.12

commit v6 on v5

--- a/solution.py
+++ b/solution.py
@@ -600,7 +600,7 @@
             if step < layers - 1:
                 outputs, link = tie(outputs, link)
             if step == 1:
-                outputs, moved = tie(outputs, moved)
+                outputs, moved, turned = tie(outputs, moved, (q_lat_normed.T, kv_normed.T))
                 grad_blocks = {**grad_blocks, **moved}
         passed.append(link)
     for part in ATTEND_PARTS[layers:]:
@@ -674,7 +674,7 @@
     grad_attended, crossing[1] = tie(grad_attended, crossing[1])
     over_layers(crossing[1])
     backward_args = (
-        bounds, q_lat_normed.T, up_all, queries, kv_normed, kv_normed.T, key_rope_all, grad_attended, attended, log_total,
+        bounds, turned[0], up_all, queries, kv_normed, turned[1], key_rope_all, grad_attended, attended, log_total,
         *tables[3:], start_row, full_rows, mask_rows,
     )
     out_shares = core_shares(out_proj_part, n)
@@ -722,9 +722,10 @@
     down_rows = D // n
     down_all_part = jnp.concatenate([down_all_part.reshape(n, down_rows, -1), gain_rows], axis=1)
     down_all_share = fsdp_scatter(down_all_part.reshape(-1, latent.shape[1]), core, chip, n).astype(BF16)
-    up_share, out_share, down_all_share, up_low, branch = tie(up_share, out_share, down_all_share, up_low, branch)
+    up_share, out_share, down_all_share, up_low, branch, down_grad = tie(
+        up_share, out_share, down_all_share, up_low, branch, down_low.astype(F32)
+    )
     up_grad, out_proj_grad, down_all_grad = (v.astype(F32) for v in lax.psum((up_share, out_share, down_all_share), "seq"))
-    down_grad = down_low.astype(F32)
     gate_up_grad = jnp.concatenate([gate_low, up_low], axis=1).astype(F32)
     output = (middle + depth_scale * chip_scatter(branch, n)).astype(BF16).reshape(block_input.shape)
     gain_sum = down_all_grad[down_rows]

time: 1330 us -> 1330 us (level)
    unnamed x230 -> x236, local copies, waits for them, and re-layouts: 52.3 us -> 54 us
  transfers between devices with their start and end apart: 81 -> 81, of which waited for: 30 -> 31; matrix products, arithmetic and copies ran while one was open for 29% -> 29% of each run, Pallas kernels for 18% -> 18%
where the time goes in v6:
time: 1330 us; the launch traced here: 1320 us
  waiting for transfers between devices  431 us (32%)
  Pallas kernels  295 us (22%)
  other arithmetic  175 us (13%)
  local copies, waits for them, and re-layouts  142 us (11%)
  matrix products  129 us (10%)
  starting transfers between devices  121 us (9%)
  between operations  20.9 us (2%)
    ppermute x59, waiting for transfers between devices, swap(): return lax.ppermute(tensor, 'fsdp', [(i, i ^ bit) for i in range(n)])  208 us
    dot_general x7, matrix products, dot(): lax.dot_general(a, b, (((ca,), (cb,)), ((), ())), preferred_element_type=...  112 us
    pallas_call x6, Pallas kernels, to_tokens(): pl.pallas_call(functools.partial(back_kernel, terms=len(left), contract=c...  91.4 us
    pallas_call x3, Pallas kernels, attend_backward(): pl.pallas_call(functools.partial(bwd_kernel, full_rows=full_rows, mask_ro...  77.3 us
    pallas_call x3, Pallas kernels, hidden_units(): pl.pallas_call(functools.partial(hidden_kernel, count=count), grid=(pl.cd...  75.3 us
    reduce_scatter x2, waiting for transfers between devices, over_layers(): lax.psum_scatter(part, 'seq', scatter_dimension=0, tiled=True)[0]  59.5 us
    psum x1, waiting for transfers between devices, body(): lax.psum((up_share, out_share, down_all_share), 'seq')  55.6 us
    ppermute x59, starting transfers between devices, swap(): return lax.ppermute(tensor, 'fsdp', [(i, i ^ bit) for i in range(n)])  55.3 us
  transfers between devices with their start and end apart: 81, of which 31 were waited for; matrix products, arithmetic and copies ran while one was open for 29% of the time, Pallas kernels for 18%

profile of v6, /device:TPU:0, one launch (start us, length us, event | category | flops | bytes accessed | tf_op | source)
XLA Modules:
  0.0 1323.5 jit_solution(9666657034100560379)
XLA Ops:
  85.4 15.6 %collective-permute-done.2 = bf16[512,384]{1,0:T(8,128)(2,1)S(1)} collective-permute-done((bf16[512,384]{1,0:T(8,128)(2,1)S(1)}, bf16[512,384]{1,0:T(8,128)(2,1)S(1)}, u32[]{:S(2)}, u32[]{:S(2)}) %collective-permute-start.2) | collective-permute-done | bytes 393248 | tf_op jit(solution)/shard_map/ppermute | solution.py:448
  102.6 20.3 %all-gather.20.cloned.1.call-done = bf16[1024,5120]{1,0:T(8,128)(2,1)} async-done(((bf16[128,5120]{1,0:T(8,128)(2,1)}), bf16[1024,5120]{1,0:T(8,128)(2,1)}) %all-gather.20.cloned.1.call-update) | async-done | bytes 10485776 | tf_op jit(solution)/shard_map/all_gather | solution.py:544
  144.4 18.0 %collective-permute-done.6 = bf16[2,80,1664]{2,1,0:T(8,128)(2,1)} collective-permute-done((bf16[2,80,1664]{2,1,0:T(8,128)(2,1)}, bf16[2,80,1664]{2,1,0:T(8,128)(2,1)}, u32[]{:S(2)}, u32[]{:S(2)}) %collective-permute-start.6) | collective-permute-done | bytes 532512 | tf_op jit(solution)/shard_map/ppermute | solution.py:376
  177.9 16.9 %attend_forward.5 = (bf16[512,2560]{1,0:T(8,128)(2,1)S(1)}, bf16[512,5120]{1,0:T(8,128)(2,1)}, f32[160,512]{1,0:T(8,128)S(1)}) custom-call(s32[4]{0:T(128)S(1)} %pad_add_fusion.bounds, bf16[512,768]{1,0:T(8,128)(2,1)S(1)} %copy-done.5, bf16[8,128,5120]{2,1,0:T(8,128)(2,1)} %bitcast.395, ...), custom_call_target="tpu_custom_call", output_to_operand_aliasing={{0}: (10, {}), {1}: (11, {}), {2}: (12, {})} | custom-call | flops 1048576 | bytes 65536 | tf_op jit(solution)/shard_map/attend_forward/pallas_call | solution.py:83
  194.8 21.4 %collective-permute-done.7 = bf16[2,4,80,1664]{3,2,1,0:T(8,128)(2,1)} collective-permute-done((bf16[2,4,80,1664]{3,2,1,0:T(8,128)(2,1)}, bf16[2,4,80,1664]{3,2,1,0:T(8,128)(2,1)}, u32[]{:S(2)}, u32[]{:S(2)}) %collective-permute-start.7) | collective-permute-done | bytes 2129952 | tf_op jit(solution)/shard_map/ppermute | solution.py:595
  374.2 22.0 %collective-permute-done.23.refs_1_ = bf16[256,2560]{1,0:T(8,128)(2,1)S(1)} collective-permute-done((bf16[256,2560]{1,0:T(8,128)(2,1)S(1)}, bf16[256,2560]{1,0:T(8,128)(2,1)S(1)}, u32[]{:S(2)}, u32[]{:S(2)}) %collective-permute-start.23) | collective-permute-done | bytes 1310752 | tf_op jit(solution)/shard_map/ppermute | solution.py:376
  409.8 20.3 %hidden_units.3 = (bf16[2048,1664]{1,0:T(8,128)(2,1)}, bf16[2048,1664]{1,0:T(8,128)(2,1)}, bf16[2048,1664]{1,0:T(8,128)(2,1)}) custom-call(bf16[256,2560]{1,0:T(8,128)(2,1)S(1)} %get-tuple-element.535.refs_0_, bf16[256,2560]{1,0:T(8,128)(2,1)S(1)} %get-tuple-element.534.refs_1_, bf16[256,2560]{1,0:T(8,128)(2,1)} %get-tuple-element.276.refs_2_, ...), custom_call_target="tpu_custom_call" | custom-call | flops 13086228480 | bytes 36044800 | tf_op jit(solution)/shard_map/hidden_units/pallas_call | solution.py:263
  430.1 19.9 %hidden_units.4 = (bf16[2048,1664]{1,0:T(8,128)(2,1)}, bf16[2048,1664]{1,0:T(8,128)(2,1)}, bf16[2048,1664]{1,0:T(8,128)(2,1)}) custom-call(bf16[256,2560]{1,0:T(8,128)(2,1)S(1)} %collective-permute-done.20.refs_0_, bf16[256,2560]{1,0:T(8,128)(2,1)S(1)} %collective-permute-done.23.refs_1_, ...), custom_call_target="tpu_custom_call", output_to_operand_aliasing={{0}: (7, {}), {1}: (8, {}), {2}: (9, {})} | custom-call | flops 13086228480 | bytes 36044800 | tf_op jit(solution)/shard_map/hidden_units/pallas_call | solution.py:263
  450.0 35.1 %hidden_units.5 = (bf16[2048,1664]{1,0:T(8,128)(2,1)}, bf16[2048,1664]{1,0:T(8,128)(2,1)}, bf16[2048,1664]{1,0:T(8,128)(2,1)}) custom-call(bf16[256,2560]{1,0:T(8,128)(2,1)S(1)} %collective-permute-done.19.refs_0_, bf16[256,2560]{1,0:T(8,128)(2,1)S(1)} %collective-permute-done.21.refs_1_, ...), custom_call_target="tpu_custom_call", output_to_operand_aliasing={{0}: (11, {}), {1}: (12, {}), {2}: (13, {})} | custom-call | flops 26172456960 | bytes 46530560 | tf_op jit(solution)/shard_map/hidden_units/pallas_call | solution.py:263
  485.1 24.9 %to_tokens.6 = (bf16[256,2560]{1,0:T(8,128)(2,1)S(1)}, bf16[256,2560]{1,0:T(8,128)(2,1)S(1)}, bf16[256,2560]{1,0:T(8,128)(2,1)S(1)}, bf16[256,2560]{1,0:T(8,128)(2,1)S(1)}) custom-call(bf16[2048,1664]{1,0:T(8,128)(2,1)} %get-tuple-element.295.refs_0_, bf16[2048,1664]{1,0:T(8,128)(2,1)} %get-tuple-element.296.refs_1_, ...), custom_call_target="tpu_custom_call" | custom-call | flops 1048576 | bytes 65536 | tf_op jit(solution)/shard_map/to_tokens/pallas_call | solution.py:302
  514.2 22.3 %convolution_convert_fusion.3 = bf16[1664,2560]{1,0:T(8,128)(2,1)S(1)} fusion(bf16[2048,1664]{1,0:T(8,128)(2,1)} %get-tuple-element.378.refs_0_, bf16[2048,2560]{1,0:T(8,128)(2,1)} %copy-done.75), kind=kOutput, calls=%fused_computation.7 | convolution fusion | flops 17452564480 | bytes 25821184 | tf_op jit(solution)/shard_map/dot_general | solution.py:24
  542.8 15.6 %to_tokens.7 = (bf16[256,2560]{1,0:T(8,128)(2,1)S(1)}, bf16[256,2560]{1,0:T(8,128)(2,1)S(1)}) custom-call(bf16[2048,1664]{1,0:T(8,128)(2,1)} %get-tuple-element.295.refs_0_, bf16[2048,1664]{1,0:T(8,128)(2,1)} %get-tuple-element.296.refs_1_, bf16[2560,1664]{1,0:T(8,128)(2,1)} %bitcast.57.refs_4_.refs_8_.refs_2_, ...), custom_call_target="tpu_custom_call" | custom-call | flops 1048576 | bytes 65536 | tf_op jit(solution)/shard_map/to_tokens/pallas_call | solution.py:302
  558.3 15.4 %to_tokens.8 = (bf16[256,2560]{1,0:T(8,128)(2,1)S(1)}, bf16[256,2560]{1,0:T(8,128)(2,1)S(1)}) custom-call(bf16[2048,1664]{1,0:T(8,128)(2,1)} %get-tuple-element.295.refs_0_, bf16[2048,1664]{1,0:T(8,128)(2,1)} %get-tuple-element.296.refs_1_, bf16[2560,1664]{1,0:T(8,128)(2,1)} %bitcast.57.refs_4_.refs_8_.refs_2_, ...), custom_call_target="tpu_custom_call" | custom-call | flops 1048576 | bytes 65536 | tf_op jit(solution)/shard_map/to_tokens/pallas_call | solution.py:302
  590.2 25.1 %convolution_convert_fusion.1 = bf16[2560,1664]{1,0:T(8,128)(2,1)} fusion(bf16[2048,2560]{1,0:T(8,128)(2,1)} %constant_dynamic-update-slice_fusion, bf16[2048,1664]{1,0:T(8,128)(2,1)} %get-tuple-element.295.refs_0_), kind=kOutput, calls=%fused_computation.5 | convolution fusion | flops 17452564480 | bytes 25821184 | tf_op jit(solution)/shard_map/dot_general | solution.py:24
  621.8 25.5 %convolution_convert_fusion.2 = bf16[2560,1664]{1,0:T(8,128)(2,1)} fusion(bf16[2048,2560]{1,0:T(8,128)(2,1)} %constant_dynamic-update-slice_fusion, bf16[2048,1664]{1,0:T(8,128)(2,1)} %get-tuple-element.296.refs_1_), kind=kOutput, calls=%fused_computation.6 | convolution fusion | flops 17452564480 | bytes 25821184 | tf_op jit(solution)/shard_map/dot_general | solution.py:24
  653.1 28.1 %reduce-scatter.4.cloned.1.call-done.rest_2_ = bf16[200,2560]{1,0:T(8,128)(2,1)} async-done(((bf16[800,2560]{1,0:T(8,128)(2,1)}), bf16[200,2560]{1,0:T(8,128)(2,1)}) %reduce-scatter.4.cloned.1.call-update) | async-done | bytes 1024016 | tf_op jit(solution)/shard_map/reduce_scatter | solution.py:653
  745.2 41.1 %attend_backward.3 = (bf16[8,96,5120]{2,1,0:T(8,128)(2,1)}, bf16[8,32,5120]{2,1,0:T(8,128)(2,1)}, f32[2048,256]{1,0:T(8,128)}, f32[2048,128]{1,0:T(8,128)S(1)}, f32[512,768]{1,0:T(8,128)}) custom-call(s32[4]{0:T(128)S(1)} %pad_add_fusion.bounds, bf16[768,512]{1,0:T(8,128)(2,1)S(1)} %copy-done.8, bf16[8,128,5120]{2,1,0:T(8,128)(2,1)} %bitcast.401, ...), custom_call_target="tpu_custom_call" | custom-call | flops 1048576 | bytes 65536 | tf_op jit(solution)/shard_map/attend_backward/pallas_call | solution.py:190
  787.2 59.5 %reduce-scatter.8.cloned.1.call-done = bf16[1,4,80,1664]{3,2,1,0:T(8,128)(2,1)} async-done(((bf16[4,4,80,1664]{3,2,1,0:T(8,128)(2,1)}), bf16[1,4,80,1664]{3,2,1,0:T(8,128)(2,1)}) %reduce-scatter.8.cloned.1.call-update) | async-done | bytes 1064976 | tf_op jit(solution)/shard_map/reduce_scatter | solution.py:665
  864.4 17.9 %attend_backward.4 = (bf16[8,96,5120]{2,1,0:T(8,128)(2,1)}, bf16[8,32,5120]{2,1,0:T(8,128)(2,1)}, f32[2048,256]{1,0:T(8,128)}, f32[2048,128]{1,0:T(8,128)S(1)}, f32[512,768]{1,0:T(8,128)}) custom-call(s32[4]{0:T(128)S(1)} %pad_add_fusion.bounds, bf16[768,512]{1,0:T(8,128)(2,1)S(1)} %copy-done.9, ...), custom_call_target="tpu_custom_call", output_to_operand_aliasing={{0}: (15, {}), {1}: (16, {})} | custom-call | flops 1048576 | bytes 65536 | tf_op jit(solution)/shard_map/attend_backward/pallas_call | solution.py:190
  900.3 18.3 %attend_backward.5 = (bf16[8,96,5120]{2,1,0:T(8,128)(2,1)}, bf16[8,32,5120]{2,1,0:T(8,128)(2,1)}, f32[2048,256]{1,0:T(8,128)}, f32[2048,128]{1,0:T(8,128)S(1)}, f32[512,768]{1,0:T(8,128)}) custom-call(s32[4]{0:T(128)S(1)} %pad_add_fusion.bounds, bf16[768,512]{1,0:T(8,128)(2,1)S(1)} %copy-done.9, ...), custom_call_target="tpu_custom_call", output_to_operand_aliasing={{0}: (15, {}), {1}: (16, {})} | custom-call | flops 1048576 | bytes 65536 | tf_op jit(solution)/shard_map/attend_backward/pallas_call | solution.py:190
  949.4 35.0 %collective-permute-start.57 = (bf16[512,384]{1,0:T(8,128)(2,1)}, bf16[512,384]{1,0:T(8,128)(2,1)S(1)}, u32[]{:S(2)}, u32[]{:S(2)}) collective-permute-start(bf16[512,384]{1,0:T(8,128)(2,1)} %get-tuple-element.570), channel_id=1, source_target_pairs={{0,3},{1,0},{2,1},{3,2},{4,7},{5,4},{6,5},{7,6},{8,11},{9,8},{10,9... | collective-permute-start | bytes 1179656 | tf_op jit(solution)/shard_map/ppermute | solution.py:457
  1163.0 27.9 %collective-permute-done.69 = bf16[256,2560]{1,0:T(8,128)(2,1)} collective-permute-done((bf16[256,2560]{1,0:T(8,128)(2,1)}, bf16[256,2560]{1,0:T(8,128)(2,1)}, u32[]{:S(2)}, u32[]{:S(2)}) %collective-permute-start.69) | collective-permute-done | bytes 1310752 | tf_op jit(solution)/shard_map/ppermute | solution.py:376
  1219.0 19.9 %collective-permute-done.70 = bf16[256,2560]{1,0:T(8,128)(2,1)} collective-permute-done((bf16[256,2560]{1,0:T(8,128)(2,1)}, bf16[256,2560]{1,0:T(8,128)(2,1)}, u32[]{:S(2)}, u32[]{:S(2)}) %collective-permute-start.70) | collective-permute-done | bytes 1310752 | tf_op jit(solution)/shard_map/ppermute | solution.py:376
  1248.8 55.6 %all-reduce.13.cloned.1.call-done = (bf16[336,1056]{1,0:T(8,128)(2,1)}, bf16[128,5120]{1,0:T(8,128)(2,1)}, bf16[320,2560]{1,0:T(8,128)(2,1)}) async-done(((bf16[336,1056]{1,0:T(8,128)(2,1)}, bf16[128,5120]{1,0:T(8,128)(2,1)}, bf16[320,2560]{1,0:T(8,128)(2,1)}), (bf16[336,1056]{1,0:T(8,128)(2,1)}, bf16[128,5120]{1,0:T(8,128)(2,1)}, bf16[320,2560]{1,0:T(8,128)(2,1)})) %all-reduce.13.cloned.1.call-update) | async-done | bytes 3658768 | tf_op jit(solution)/shard_map/psum | solution.py:728
  (596 shorter events, 681.0 us)
Async XLA Ops:
  10.4 112.5 %all-gather.20.cloned.1.call-start = ((), (), s32[]{:S(2)}) async-start(), calls=%async_computation.11 | async-start | bytes 11796480 | tf_op jit(solution)/shard_map/all_gather | solution.py:544
  13.6 289.1 %all-gather.12.cloned.1.call-start = ((), (), s32[]{:S(2)}) async-start(), calls=%async_computation.4 | async-start | bytes 14745600 | tf_op jit(solution)/shard_map/all_gather | solution.py:545
  14.3 666.9 %reduce-scatter.4.cloned.1.call-start = ((), (), s32[]{:S(2)}) async-start(), calls=%async_computation.5 | async-start | bytes 5120000 | tf_op jit(solution)/shard_map/reduce_scatter | solution.py:653
  176.5 59.0 %collective-permute-start.9 = (bf16[256,2560]{1,0:T(8,128)(2,1)}, bf16[256,2560]{1,0:T(8,128)(2,1)}, u32[]{:S(2)}, u32[]{:S(2)}) collective-permute-start(bf16[256,2560]{1,0:T(8,128)(2,1)} %get-tuple-element.276.refs_2_), channel_id=1, source_target_pairs={{0,8},{4,12},{8,0},{12,4},{16,24},{20,28},{24,16},{28,20},{1,9},{5... | collective-permute-start | bytes 3932168 | tf_op jit(solution)/shard_map/ppermute | solution.py:376
  226.4 58.9 %collective-permute-start.25 = (bf16[2,4,80,1664]{3,2,1,0:T(8,128)(2,1)}, bf16[2,4,80,1664]{3,2,1,0:T(8,128)(2,1)}, u32[]{:S(2)}, u32[]{:S(2)}) collective-permute-start(bf16[2,4,80,1664]{3,2,1,0:T(8,128)(2,1)} %bitcast_dynamic-update-slice_fusion), channel_id=1, source_target_pairs={{0,4},{4,0},{8,12},{12,8},{16,20},{20,16},{24,28},{28,24},{1,5},{5... | collective-permute-start | bytes 6389768 | tf_op jit(solution)/shard_map/ppermute | solution.py:376
  235.5 65.0 %collective-permute-start.13 = (bf16[256,2560]{1,0:T(8,128)(2,1)}, bf16[256,2560]{1,0:T(8,128)(2,1)}, u32[]{:S(2)}, u32[]{:S(2)}) collective-permute-start(bf16[256,2560]{1,0:T(8,128)(2,1)} %get-tuple-element.277.refs_3_), channel_id=1, source_target_pairs={{0,8},{4,12},{8,0},{12,4},{16,24},{20,28},{24,16},{28,20},{1,9},{5... | collective-permute-start | bytes 3932168 | tf_op jit(solution)/shard_map/ppermute | solution.py:376
  272.8 58.1 %collective-permute-start.17 = (bf16[2,4,80,1664]{3,2,1,0:T(8,128)(2,1)}, bf16[2,4,80,1664]{3,2,1,0:T(8,128)(2,1)}, u32[]{:S(2)}, u32[]{:S(2)}) collective-permute-start(bf16[2,4,80,1664]{3,2,1,0:T(8,128)(2,1)} %collective-permute-done.11), channel_id=1, source_target_pairs={{0,1},{1,2},{2,3},{4,5},{5,6},{6,7},{8,9},{9,10},{10,11},{12,13},{... | collective-permute-start | bytes 6389768 | tf_op jit(solution)/shard_map/ppermute | solution.py:595
  343.3 106.7 %collective-permute-start.22 = (bf16[256,2560]{1,0:T(8,128)(2,1)S(1)}, bf16[256,2560]{1,0:T(8,128)(2,1)S(1)}, u32[]{:S(2)}, u32[]{:S(2)}) collective-permute-start(bf16[256,2560]{1,0:T(8,128)(2,1)S(1)} %get-tuple-element.534.refs_1_), channel_id=1, source_target_pairs={{0,8},{4,12},{8,0},{12,4},{16,24},{20,28},{24,16},{28,20},{1,9},{5... | collective-permute-start | bytes 3932168 | tf_op jit(solution)/shard_map/ppermute | solution.py:376
  510.0 69.0 %collective-permute-start.29 = (bf16[256,2560]{1,0:T(8,128)(2,1)S(1)}, bf16[256,2560]{1,0:T(8,128)(2,1)S(1)}, u32[]{:S(2)}, u32[]{:S(2)}) collective-permute-start(bf16[256,2560]{1,0:T(8,128)(2,1)S(1)} %get-tuple-element.298), channel_id=1, source_target_pairs={{0,16},{4,20},{8,24},{12,28},{16,0},{20,4},{24,8},{28,12},{1,17},{... | collective-permute-start | bytes 3932168 | tf_op jit(solution)/shard_map/ppermute | solution.py:376
  510.7 71.0 %collective-permute-start.30 = (bf16[256,2560]{1,0:T(8,128)(2,1)S(1)}, bf16[256,2560]{1,0:T(8,128)(2,1)S(1)}, u32[]{:S(2)}, u32[]{:S(2)}) collective-permute-start(bf16[256,2560]{1,0:T(8,128)(2,1)S(1)} %get-tuple-element.300), channel_id=1, source_target_pairs={{0,8},{4,12},{8,0},{12,4},{16,24},{20,28},{24,16},{28,20},{1,9},{5... | collective-permute-start | bytes 3932168 | tf_op jit(solution)/shard_map/ppermute | solution.py:376
  510.7 64.1 %collective-permute-start.31 = (bf16[256,2560]{1,0:T(8,128)(2,1)S(1)}, bf16[256,2560]{1,0:T(8,128)(2,1)}, u32[]{:S(2)}, u32[]{:S(2)}) collective-permute-start(bf16[256,2560]{1,0:T(8,128)(2,1)S(1)} %get-tuple-element.302), channel_id=1, source_target_pairs={{0,16},{4,20},{8,24},{12,28},{16,0},{20,4},{24,8},{28,12},{1,17},{... | collective-permute-start | bytes 3932168 | tf_op jit(solution)/shard_map/ppermute | solution.py:376
  512.1 65.4 %collective-permute-start.32 = (bf16[256,2560]{1,0:T(8,128)(2,1)S(1)}, bf16[256,2560]{1,0:T(8,128)(2,1)S(1)}, u32[]{:S(2)}, u32[]{:S(2)}) collective-permute-start(bf16[256,2560]{1,0:T(8,128)(2,1)S(1)} %get-tuple-element.304), channel_id=1, source_target_pairs={{0,8},{4,12},{8,0},{12,4},{16,24},{20,28},{24,16},{28,20},{1,9},{5... | collective-permute-start | bytes 3932168 | tf_op jit(solution)/shard_map/ppermute | solution.py:376
  590.2 197.1 %reduce-scatter.6.cloned.1.call-start = ((), (), s32[]{:S(2)}) async-start(), calls=%async_computation.6 | async-start | bytes 5324800 | tf_op jit(solution)/shard_map/reduce_scatter | solution.py:665
  687.8 159.0 %reduce-scatter.8.cloned.1.call-start = ((), (), s32[]{:S(2)}) async-start(), calls=%async_computation.7 | async-start | bytes 5324800 | tf_op jit(solution)/shard_map/reduce_scatter | solution.py:665
  722.3 330.0 %all-gather.16.cloned.1.call-start = ((), (), s32[]{:S(2)}) async-start(), calls=%async_computation.9 | async-start | bytes 5120000 | tf_op jit(solution)/shard_map/all_gather | solution.py:683
  740.8 311.5 %all-gather.14.cloned.1.call-start = ((), (), s32[]{:S(2)}) async-start(), calls=%async_computation.8 | async-start | bytes 5120000 | tf_op jit(solution)/shard_map/all_gather | solution.py:695
  888.9 270.0 %all-gather.18.cloned.1.call-start = ((), (), s32[]{:S(2)}) async-start(), calls=%async_computation.10 | async-start | bytes 5120000 | tf_op jit(solution)/shard_map/all_gather | solution.py:695
  942.0 97.7 %collective-permute-start.46 = (bf16[4,128,5120]{2,1,0:T(8,128)(2,1)}, bf16[4,128,5120]{2,1,0:T(8,128)(2,1)}, u32[]{:S(2)}, u32[]{:S(2)}) collective-permute-start(bf16[4,128,5120]{2,1,0:T(8,128)(2,1)} %dynamic-slice_bitcast_fusion.1), channel_id=1, source_target_pairs={{0,4},{4,0},{8,12},{12,8},{16,20},{20,16},{24,28},{28,24},{1,5},{5... | collective-permute-start | bytes 15728648 | tf_op jit(solution)/shard_map/ppermute | solution.py:376
  942.2 362.2 %all-reduce.13.cloned.1.call-start = ((), (), s32[]{:S(2)}) async-start(), calls=%async_computation.12 | async-start | bytes 7446528 | tf_op jit(solution)/shard_map/psum | solution.py:728
  945.8 143.4 %collective-permute-start.53 = (bf16[160,2560]{1,0:T(8,128)(2,1)}, bf16[160,2560]{1,0:T(8,128)(2,1)}, u32[]{:S(2)}, u32[]{:S(2)}) collective-permute-start(bf16[160,2560]{1,0:T(8,128)(2,1)} %get-tuple-element.514), channel_id=1, source_target_pairs={{0,8},{4,12},{8,0},{12,4},{16,24},{20,28},{24,16},{28,20},{1,9},{5... | collective-permute-start | bytes 2457608 | tf_op jit(solution)/shard_map/ppermute | solution.py:376
  949.4 80.8 %collective-permute-start.57 = (bf16[512,384]{1,0:T(8,128)(2,1)}, bf16[512,384]{1,0:T(8,128)(2,1)S(1)}, u32[]{:S(2)}, u32[]{:S(2)}) collective-permute-start(bf16[512,384]{1,0:T(8,128)(2,1)} %get-tuple-element.570), channel_id=1, source_target_pairs={{0,3},{1,0},{2,1},{3,2},{4,7},{5,4},{6,5},{7,6},{8,11},{9,8},{10,9... | collective-permute-start | bytes 1179656 | tf_op jit(solution)/shard_map/ppermute | solution.py:457
  1030.2 60.0 %collective-permute-start.54 = (bf16[160,2560]{1,0:T(8,128)(2,1)}, bf16[160,2560]{1,0:T(8,128)(2,1)}, u32[]{:S(2)}, u32[]{:S(2)}) collective-permute-start(bf16[160,2560]{1,0:T(8,128)(2,1)} %get-tuple-element.515), channel_id=1, source_target_pairs={{0,16},{4,20},{8,24},{12,28},{16,0},{20,4},{24,8},{28,12},{1,17},{... | collective-permute-start | bytes 2457608 | tf_op jit(solution)/shard_map/ppermute | solution.py:376
  1161.0 58.1 %collective-permute-start.68 = (bf16[256,2560]{1,0:T(8,128)(2,1)}, bf16[256,2560]{1,0:T(8,128)(2,1)}, u32[]{:S(2)}, u32[]{:S(2)}) collective-permute-start(bf16[256,2560]{1,0:T(8,128)(2,1)} %copy-done.31), channel_id=1, source_target_pairs={{0,8},{4,12},{8,0},{12,4},{16,24},{20,28},{24,16},{28,20},{1,9},{5... | collective-permute-start | bytes 3932168 | tf_op jit(solution)/shard_map/ppermute | solution.py:376
  1162.5 78.9 %collective-permute-start.65 = (bf16[256,2560]{1,0:T(8,128)(2,1)}, bf16[256,2560]{1,0:T(8,128)(2,1)}, u32[]{:S(2)}, u32[]{:S(2)}) collective-permute-start(bf16[256,2560]{1,0:T(8,128)(2,1)} %copy-done.30), channel_id=1, source_target_pairs={{0,16},{4,20},{8,24},{12,28},{16,0},{20,4},{24,8},{28,12},{1,17},{... | collective-permute-start | bytes 3932168 | tf_op jit(solution)/shard_map/ppermute | solution.py:376
  (163 other events, 3679.2 us)
Sparse Core Ops, SparseCore 0:
  10.5 46.6 all-gather.9
  59.6 63.2 all-gather.19
  124.8 116.2 all-gather.11
  590.3 90.8 reduce-scatter.3
  687.9 78.2 reduce-scatter.5
  768.3 78.3 reduce-scatter.7
  848.4 79.6 all-gather.15
  929.7 111.1 all-gather.13
  1042.5 77.3 all-gather.17
  1163.1 141.2 all-reduce.12
